TPU v7x, 32 devices: a whole 2x2x4 slice. The times are simulated.
32 devices in a mesh: tp: 2 (over x), cp: 16 (over z, y, core).
Axes of the slice: x: 2, y: 2, z: 4, core: 2. Of those that a mesh axis runs over, the one named last changes fastest.
Arguments:
- residual: bfloat16 [4096, 1024], P('cp'), may hold values from -6 to 6
- cotangent: bfloat16 [4096, 1024], P('cp'), may hold values from -6 to 6
- span_order: int32 [32], replicated, may hold values from 0 to 31, as said below
- positions: int32 [4096], P('cp'), may hold values from 0 to 4096, as said below
- attn_gain: float32 [1024], replicated, may hold values from 0.5 to 1.5
- query_weight: bfloat16 [1024, 2048], P(None, 'tp'), may hold values from -0.1875 to 0.1875
- key_weight: bfloat16 [1024, 1024], P(None, 'tp'), may hold values from -0.1875 to 0.1875
- value_weight: bfloat16 [1024, 1024], P(None, 'tp'), may hold values from -0.1875 to 0.1875
- query_gain: float32 [128], replicated, may hold values from 0.25 to 1.75
- key_gain: float32 [128], replicated, may hold values from 0.25 to 1.75
- out_weight: bfloat16 [2048, 1024], P('tp'), may hold values from -0.5 to 0.5
- mlp_gain: float32 [1024], replicated, may hold values from 0.5 to 1.5
- gate_weight: bfloat16 [1024, 3072], P(None, 'tp'), may hold values from -0.1875 to 0.1875
- up_weight: bfloat16 [1024, 3072], P(None, 'tp'), may hold values from -0.1875 to 0.1875
- down_weight: bfloat16 [3072, 1024], P('tp'), may hold values from -0.109375 to 0.109375
Outputs:
- layer_out: bfloat16 [4096, 1024], P('cp')
- residual_grad: float32 [4096, 1024], P('cp')
- attn_gain_grad: float32 [1024], replicated
- query_weight_grad: float32 [1024, 2048], P(None, 'tp')
- key_weight_grad: float32 [1024, 1024], P(None, 'tp')
- value_weight_grad: float32 [1024, 1024], P(None, 'tp')
- query_gain_grad: float32 [128], replicated
- key_gain_grad: float32 [128], replicated
- out_weight_grad: float32 [2048, 1024], P('tp')
- mlp_gain_grad: float32 [1024], replicated
- gate_weight_grad: float32 [1024, 3072], P(None, 'tp')
- up_weight_grad: float32 [1024, 3072], P(None, 'tp')
- down_weight_grad: float32 [3072, 1024], P('tp')
Inputs may be any that keep to these rules, and one draw needn't show every extreme that they name: `span_order`: each of 0 to 31 stands once; entries 2 i and 2 i + 1 add up to 31. `positions`: the row at sequence place p has position p or p + 1; place 0 has position 0 and place 4096 - 1 has position 4096.
All inputs are finite; a program needn't handle non-finite values.
Results may differ from a plain program's by a relative error of at most 0.03.
Values may be sent and summed in bfloat16 or wider, within the bound.
No kernel may reach another device: no remote copies, remote signals or barrier semaphores. Data moves between devices by JAX's collectives and lax.ppermute only.
A program may use at most 320 MiB of HBM per device.

v0:
```python
import math

import jax
import jax.numpy as jnp
from jax import lax
from jax.sharding import PartitionSpec as P

EPS = 1e-06
ROPE_BASE = 1000000.0
NEG = -1e30
KEY_BLOCK = 2048


def norm_rows(values):
    scale_rows = lax.rsqrt(jnp.mean(values * values, axis=-1, keepdims=True) + EPS)
    return (values * scale_rows, scale_rows)


def norm_back(grad_normed, normed, scale_rows):
    return scale_rows * (
        grad_normed - normed * jnp.mean(grad_normed * normed, axis=-1, keepdims=True)
    )


def rope_tables(positions, width):
    half = width // 2
    freq = ROPE_BASE ** (-(jnp.arange(half, dtype=jnp.float32) * 2.0) / width)
    angle = positions.astype(jnp.float32)[:, None] * freq[None, :]
    return (jnp.cos(angle), jnp.sin(angle))


def rotate(values, cosine, sine):
    half = values.shape[-1] // 2
    first = values[..., :half]
    second = values[..., half:]
    return jnp.concatenate(
        [first * cosine - second * sine, second * cosine + first * sine], axis=-1
    )


def rotate_back(grad, cosine, sine):
    half = grad.shape[-1] // 2
    first = grad[..., :half]
    second = grad[..., half:]
    return jnp.concatenate(
        [first * cosine + second * sine, second * cosine - first * sine], axis=-1
    )


def across(left, right):
    return lax.dot_general(
        left, right, (((0,), (0,)), ((), ())), preferred_element_type=jnp.float32
    )


def against(left, right):
    return lax.dot_general(
        left, right, (((1,), (1,)), ((), ())), preferred_element_type=jnp.float32
    )


def body(
    residual,
    cotangent,
    span_order,
    positions,
    attn_gain,
    query_weight,
    key_weight,
    value_weight,
    query_gain,
    key_gain,
    out_weight,
    mlp_gain,
    gate_weight,
    up_weight,
    down_weight,
):
    rows = residual.shape[0]
    head_dim = query_gain.shape[0]
    heads_here = query_weight.shape[1] // head_dim
    groups_here = key_weight.shape[1] // head_dim
    pair = heads_here // groups_here
    span = rows // 2
    places = (span_order[:, None] * span + jnp.arange(span, dtype=jnp.int32)[None, :]).reshape(-1)
    total = places.shape[0]
    places_here = lax.dynamic_slice_in_dim(places, lax.axis_index("cp") * rows, rows)
    factor = 1.0 / math.sqrt(head_dim)
    residual_wide = residual.astype(jnp.float32)
    normed_one, scale_one = norm_rows(residual_wide)
    normed_low = (normed_one * attn_gain).astype(jnp.bfloat16)
    queries = jnp.dot(normed_low, query_weight, preferred_element_type=jnp.float32).reshape(
        rows, heads_here, head_dim
    )
    keys_raw = jnp.dot(normed_low, key_weight, preferred_element_type=jnp.float32).reshape(
        rows, groups_here, head_dim
    )
    values_low = jnp.dot(normed_low, value_weight, preferred_element_type=jnp.float32).astype(
        jnp.bfloat16
    )
    values_low = values_low.reshape(rows, groups_here, head_dim)
    cosine, sine = rope_tables(positions, head_dim)
    cosine = cosine[:, None, :]
    sine = sine[:, None, :]
    query_unit, query_scale = norm_rows(queries)
    query_low = rotate(query_unit * query_gain, cosine, sine).astype(jnp.bfloat16)
    key_unit, key_scale = norm_rows(keys_raw)
    key_low = rotate(key_unit * key_gain, cosine, sine).astype(jnp.bfloat16)
    query_pairs = query_low.reshape(rows, groups_here, pair, head_dim)
    keys_all, values_all = (
        lax.all_gather(key_low, "cp", axis=0, tiled=True),
        lax.all_gather(values_low, "cp", axis=0, tiled=True),
    )
    block = math.gcd(total, KEY_BLOCK)
    block_count = total // block
    key_blocks = keys_all.reshape(block_count, block, groups_here, head_dim)
    value_blocks = values_all.reshape(block_count, block, groups_here, head_dim)
    place_blocks = places.reshape(block_count, block)

    def scores_of(key_block, key_places):
        scores = (
            jnp.einsum("rgeh,kgh->gerk", query_pairs, key_block, preferred_element_type=jnp.float32)
            * factor
        )
        allowed = key_places[None, :] <= places_here[:, None]
        return (jnp.where(allowed, scores, NEG), allowed)

    def forward_step(carry, item):
        top, mass, accum = carry
        key_block, value_block, key_places = item
        scores, allowed = scores_of(key_block, key_places)
        new_top = jnp.maximum(top, jnp.max(scores, axis=-1))
        probs = jnp.where(allowed, jnp.exp(scores - new_top[..., None]), 0.0)
        fade = jnp.exp(top - new_top)
        mass = mass * fade + jnp.sum(probs, axis=-1)
        accum = accum * fade[..., None] + jnp.einsum(
            "gerk,kgh->gerh",
            probs.astype(jnp.bfloat16),
            value_block,
            preferred_element_type=jnp.float32,
        )
        return ((new_top, mass, accum), None)

    start_top = jnp.full((groups_here, pair, rows), NEG, jnp.float32)
    start_mass = jnp.zeros((groups_here, pair, rows), jnp.float32)
    start_accum = jnp.zeros((groups_here, pair, rows, head_dim), jnp.float32)
    (top, mass, accum), _ = lax.scan(
        forward_step, (start_top, start_mass, start_accum), (key_blocks, value_blocks, place_blocks)
    )
    logsum = top + jnp.log(mass)
    attended = accum / mass[..., None]
    attended_low = (
        attended.transpose(2, 0, 1, 3).reshape(rows, heads_here * head_dim).astype(jnp.bfloat16)
    )
    mixed = residual_wide + lax.psum(
        jnp.dot(attended_low, out_weight, preferred_element_type=jnp.float32).astype(jnp.bfloat16),
        "tp",
    ).astype(jnp.float32)
    normed_two, scale_two = norm_rows(mixed)
    normed_two_low = (normed_two * mlp_gain).astype(jnp.bfloat16)
    gate = jnp.dot(normed_two_low, gate_weight, preferred_element_type=jnp.float32)
    upward = jnp.dot(normed_two_low, up_weight, preferred_element_type=jnp.float32)
    sigmoid_gate = jax.nn.sigmoid(gate)
    activated = gate * sigmoid_gate
    hidden_low = (activated * upward).astype(jnp.bfloat16)
    layer_out = mixed + lax.psum(
        jnp.dot(hidden_low, down_weight, preferred_element_type=jnp.float32).astype(jnp.bfloat16),
        "tp",
    ).astype(jnp.float32)
    down_weight_grad = across(hidden_low, cotangent)
    hidden_grad = against(cotangent, down_weight)
    gate_grad_low = (
        hidden_grad * upward * sigmoid_gate * (1.0 + gate * (1.0 - sigmoid_gate))
    ).astype(jnp.bfloat16)
    up_grad_low = (hidden_grad * activated).astype(jnp.bfloat16)
    gate_weight_grad = across(normed_two_low, gate_grad_low)
    up_weight_grad = across(normed_two_low, up_grad_low)
    normed_two_grad = lax.psum(
        (against(gate_grad_low, gate_weight) + against(up_grad_low, up_weight)).astype(
            jnp.bfloat16
        ),
        "tp",
    ).astype(jnp.float32)
    mlp_gain_term = jnp.sum(normed_two_grad * normed_two, axis=0)
    mixed_grad = cotangent.astype(jnp.float32) + norm_back(
        normed_two_grad * mlp_gain, normed_two, scale_two
    )
    mixed_grad_low = mixed_grad.astype(jnp.bfloat16)
    out_weight_grad = across(attended_low, mixed_grad_low)
    attended_grad = against(mixed_grad_low, out_weight).astype(jnp.bfloat16)
    grad_pairs = attended_grad.reshape(rows, groups_here, pair, head_dim)
    delta = jnp.sum(grad_pairs.astype(jnp.float32).transpose(1, 2, 0, 3) * attended, axis=-1)

    def score_grads(key_block, value_block, key_places):
        scores, allowed = scores_of(key_block, key_places)
        probs = jnp.where(allowed, jnp.exp(scores - logsum[..., None]), 0.0)
        prob_grad = jnp.einsum(
            "rgeh,kgh->gerk", grad_pairs, value_block, preferred_element_type=jnp.float32
        )
        return (probs, (probs * (prob_grad - delta[..., None]) * factor).astype(jnp.bfloat16))

    start_query = jnp.zeros((groups_here, pair, rows, head_dim), jnp.float32)

    def back_step(query_accum, item):
        key_block, value_block, key_places = item
        probs, score_grad = score_grads(key_block, value_block, key_places)
        query_accum = query_accum + jnp.einsum(
            "gerk,kgh->gerh", score_grad, key_block, preferred_element_type=jnp.float32
        )
        key_part = jnp.einsum(
            "gerk,rgeh->kgh", score_grad, query_pairs, preferred_element_type=jnp.float32
        )
        value_part = jnp.einsum(
            "gerk,rgeh->kgh",
            probs.astype(jnp.bfloat16),
            grad_pairs,
            preferred_element_type=jnp.float32,
        )
        return (query_accum, (key_part, value_part))

    query_accum, (key_parts, value_parts) = lax.scan(
        back_step, start_query, (key_blocks, value_blocks, place_blocks)
    )
    key_grad, value_grad = (
        lax.psum_scatter(
            key_parts.reshape(total, groups_here, head_dim), "cp", scatter_dimension=0, tiled=True
        ),
        lax.psum_scatter(
            value_parts.reshape(total, groups_here, head_dim), "cp", scatter_dimension=0, tiled=True
        ),
    )
    query_grad_rows = query_accum.transpose(2, 0, 1, 3).reshape(rows, heads_here, head_dim)
    query_turned = rotate_back(query_grad_rows, cosine, sine)
    query_gain_term = jnp.sum(query_turned * query_unit, axis=(0, 1))
    query_grad_low = norm_back(query_turned * query_gain, query_unit, query_scale).astype(
        jnp.bfloat16
    )
    query_grad_low = query_grad_low.reshape(rows, heads_here * head_dim)
    key_turned = rotate_back(key_grad, cosine, sine)
    key_gain_term = jnp.sum(key_turned * key_unit, axis=(0, 1))
    key_grad_low = norm_back(key_turned * key_gain, key_unit, key_scale).astype(jnp.bfloat16)
    key_grad_low = key_grad_low.reshape(rows, groups_here * head_dim)
    value_grad_low = value_grad.astype(jnp.bfloat16).reshape(rows, groups_here * head_dim)
    query_weight_grad = across(normed_low, query_grad_low)
    key_weight_grad = across(normed_low, key_grad_low)
    value_weight_grad = across(normed_low, value_grad_low)
    normed_grad_part = (
        against(query_grad_low, query_weight)
        + against(key_grad_low, key_weight)
        + against(value_grad_low, value_weight)
    )
    normed_grad, query_gain_total, key_gain_total = (
        lax.psum(normed_grad_part.astype(jnp.bfloat16), "tp").astype(jnp.float32),
        lax.psum(query_gain_term.astype(jnp.bfloat16), "tp").astype(jnp.float32),
        lax.psum(key_gain_term.astype(jnp.bfloat16), "tp").astype(jnp.float32),
    )
    attn_gain_term = jnp.sum(normed_grad * normed_one, axis=0)
    residual_grad = mixed_grad + norm_back(normed_grad * attn_gain, normed_one, scale_one)
    (
        attn_gain_grad,
        query_weight_sum,
        key_weight_sum,
        value_weight_sum,
        query_gain_grad,
        key_gain_grad,
        out_weight_sum,
        mlp_gain_grad,
        gate_weight_sum,
        up_weight_sum,
        down_weight_sum,
    ) = lax.psum(
        (
            attn_gain_term,
            query_weight_grad,
            key_weight_grad,
            value_weight_grad,
            query_gain_total,
            key_gain_total,
            out_weight_grad,
            mlp_gain_term,
            gate_weight_grad,
            up_weight_grad,
            down_weight_grad,
        ),
        "cp",
    )
    return (
        layer_out.astype(jnp.bfloat16),
        residual_grad,
        attn_gain_grad,
        query_weight_sum,
        key_weight_sum,
        value_weight_sum,
        query_gain_grad,
        key_gain_grad,
        out_weight_sum,
        mlp_gain_grad,
        gate_weight_sum,
        up_weight_sum,
        down_weight_sum,
    )


def solution(mesh):
    return jax.shard_map(
        body,
        mesh=mesh,
        in_specs=(
            P("cp", None),
            P("cp", None),
            P(),
            P("cp"),
            P(),
            P(None, "tp"),
            P(None, "tp"),
            P(None, "tp"),
            P(),
            P(),
            P("tp", None),
            P(),
            P(None, "tp"),
            P(None, "tp"),
            P("tp", None),
        ),
        out_specs=(
            P("cp", None),
            P("cp", None),
            P(),
            P(None, "tp"),
            P(None, "tp"),
            P(None, "tp"),
            P(),
            P(),
            P("tp", None),
            P(),
            P(None, "tp"),
            P(None, "tp"),
            P("tp", None),
        ),
        check_vma=False,
    )
```

profile of v0, /device:TPU:0, one launch (start us, length us, event | category | flops | bytes accessed | tf_op | source)
XLA Modules:
  0.0 1207.9 jit_solution(10385542593278907562)
XLA Ops:
  30.8 40.5 %all-gather.3.cloned.1.call-done = bf16[4096,4,128]{2,0,1:T(8,128)(2,1)} async-done(((bf16[256,4,128]{2,0,1:T(8,128)(2,1)}), bf16[4096,4,128]{2,0,1:T(8,128)(2,1)}) %all-gather.3.cloned.1.call-update) | async-done | bytes 4194320 | tf_op jit(solution)/shard_map/all_gather | solution.py:111
  71.3 4.5 copy.151
  75.8 47.4 %all-gather.5.cloned.1.call-done = bf16[4096,4,128]{2,0,1:T(8,128)(2,1)} async-done(((bf16[256,4,128]{2,0,1:T(8,128)(2,1)}), bf16[4096,4,128]{2,0,1:T(8,128)(2,1)}) %all-gather.5.cloned.1.call-update) | async-done | bytes 4194320 | tf_op jit(solution)/shard_map/all_gather | solution.py:112
  123.2 4.5 copy.152
  127.7 59.2 %while.30 = (s32[]{:T(128)}, f32[4,2,256]{2,1,0:T(2,128)S(1)}, f32[4,2,256]{2,1,0:T(2,128)S(1)}, f32[4,2,256,128]{3,2,1,0:T(8,128)}, s32[2,2048]{1,0:T(2,128)S(1...) while((s32[]{:T(128)}, f32[4,2,256]{2,1,0:T(2,128)S(1)}, ...), condition=%wide.region_6.7_spmd.clone, body=%wide.region_3.6_spmd.clone.sunk | while | flops 2203330560 | bytes 130704608 | solution.py:147
  128.2 10.2 fusion.177
  138.4 8.9 fusion.179
  149.3 8.0 fusion.181
  157.7 10.2 fusion.177
  168.0 8.9 fusion.179
  178.8 8.1 fusion.181
  195.3 26.7 %all-reduce.9.cloned.1.call-done = bf16[256,1024]{1,0:T(8,128)(2,1)} async-done(((bf16[256,1024]{1,0:T(8,128)(2,1)}), bf16[256,1024]{1,0:T(8,128)(2,1)}) %all-reduce.9.cloned.1.call-update) | async-done | bytes 524304 | tf_op jit(solution)/shard_map/psum | solution.py:155
  234.6 28.7 %all-reduce.11.cloned.1.call-done = bf16[256,1024]{1,0:T(8,128)(2,1)} async-done(((bf16[256,1024]{1,0:T(8,128)(2,1)}), bf16[256,1024]{1,0:T(8,128)(2,1)}) %all-reduce.11.cloned.1.call-update) | async-done | bytes 524304 | tf_op jit(solution)/shard_map/psum | solution.py:178
  277.4 92.0 %while.31 = (s32[]{:T(128)}, f32[4,2,256,128]{3,2,1,0:T(8,128)}, f32[2,2048,4,128]{3,1,0,2:T(8,128)}, f32[2,2048,4,128]{3,1,0,2:T(8,128)}, s32[2,2048]{1,0:T(2,1...) while((s32[]{:T(128)}, f32[4,2,256,128]{3,2,1,0:T(8,128)}, ...), condition=%wide.region_14.15_spmd.clone, body=%wide.region_13.14_spmd.clone.sunk | while | flops 5424283648 | bytes 156812672 | solution.py:221
  277.6 9.9 fusion.192
  288.1 11.6 fusion.193
  299.7 7.6 fusion.194
  307.3 4.3 bitcast_dynamic-update-slice_fusion.4
  311.6 11.6 bitcast_dynamic-update-slice_fusion.5
  323.2 9.9 fusion.192
  333.7 11.6 fusion.193
  345.3 7.8 fusion.194
  353.1 4.4 bitcast_dynamic-update-slice_fusion.4
  357.5 11.7 bitcast_dynamic-update-slice_fusion.5
  392.1 82.1 %reduce-scatter.3.cloned.1.call-done = f32[256,4,128]{2,0,1:T(8,128)} async-done(((f32[4096,4,128]{2,0,1:T(8,128)}), f32[256,4,128]{2,0,1:T(8,128)}) %reduce-scatter.3.cloned.1.call-update) | async-done | bytes 524304 | tf_op jit(solution)/shard_map/reduce_scatter | solution.py:225
  478.6 104.0 %reduce-scatter.5.cloned.1.call-done = f32[256,4,128]{2,0,1:T(8,128)} async-done(((f32[4096,4,128]{2,0,1:T(8,128)}), f32[256,4,128]{2,0,1:T(8,128)}) %reduce-scatter.5.cloned.1.call-update) | async-done | bytes 524304 | tf_op jit(solution)/shard_map/reduce_scatter | solution.py:228
  589.9 4.2 fusion.93
  601.1 5.0 all-reduce.2
  606.1 23.7 %all-reduce.15.cloned.1.call-done = (bf16[256,1024]{1,0:T(8,128)(2,1)}, bf16[256,1024]{1,0:T(8,128)(2,1)}) async-done(((bf16[256,1024]{1,0:T(8,128)(2,1)}, bf16[256,1024]{1,0:T(8,128)(2,1)}), (bf16[256,1024]{1,0:T(8,128)(2,1)}, bf16[256,1024]{1,0:T(8,128)(2,1)})) %all-reduce.15.cloned.1.call-update) | async-done | bytes 1048592 | tf_op jit(solution)/shard_map/psum | solution.py:166
  631.4 64.2 %all-reduce = (f32[1024]{0:T(1024)}, f32[128]{0:T(128)}, f32[128]{0:T(128)}, f32[1024]{0:T(1024)}) all-reduce(f32[1024]{0:T(1024)S(1)} %get-tuple-element.341, bf16[128]{0:T(256)(128)(2,1)S(1)} %get-tuple-element.396, bf16[128]{0:T(256)(128)(2,1)S(1)} %get-tuple-element.397, ...), channel_id=1, replica_groups=mesh['tp'=2,'cp'=16] {'cp'}, use_global_device_ids=true, to_apply=%region_22.23 | all-reduce | flops 2304 | bytes 17920 | tf_op jit(solution)/shard_map/psum | solution.py:271
  699.5 479.4 %all-reduce.13.cloned.1.call-done = (f32[1024,1024]{1,0:T(8,128)}, f32[1024,512]{1,0:T(8,128)}, f32[1024,512]{1,0:T(8,128)}, f32[1024,1024]{1,0:T(8,128)}, f32[1...) async-done(((f32[1024,1024]{1,0:T(8,128)}, f32[1024,512]{1,0:T(8,128)}, f32[1024,512]{1,0:T(8,128)}, f32[1024,1024]{1,0:T(8,128)}, ...) | async-done | bytes 31457296 | tf_op jit(solution)/shard_map/psum | solution.py:271
  1178.9 5.1 copy.265
  (297 shorter events, 127.6 us)
Async XLA Ops:
  7.2 221.9 %copy-start = (bf16[1536,1024]{1,0:T(8,128)(2,1)S(1)}, bf16[1536,1024]{1,0:T(8,128)(2,1)}, u32[]{:S(2)}) copy-start(bf16[1536,1024]{1,0:T(8,128)(2,1)} %param.33) | copy-start | bytes 9437188
  7.2 64.1 %all-gather.3.cloned.1.call-start = ((), (), s32[]{:S(2)}) async-start(), calls=%async_computation.2 | async-start | bytes 4456448 | tf_op jit(solution)/shard_map/all_gather | solution.py:111
  8.7 9.3 copy-start.49
  8.7 12.4 %copy-start.51 = (f32[256]{0:T(256)}, f32[256]{0:T(256)S(1)}, u32[]{:S(2)}) copy-start(f32[256]{0:T(256)S(1)} %add_rsqrt_fusion.3) | copy-start | bytes 3076
  16.7 9.3 copy-start.28
  16.7 9.3 copy-start.30
  17.9 105.3 %all-gather.5.cloned.1.call-start = ((), (), s32[]{:S(2)}) async-start(), calls=%async_computation.3 | async-start | bytes 4456448 | tf_op jit(solution)/shard_map/all_gather | solution.py:112
  20.6 201.4 %all-reduce.9.cloned.1.call-start = ((), (), s32[]{:S(2)}) async-start(), calls=%async_computation.4 | async-start | bytes 1048576 | tf_op jit(solution)/shard_map/psum | solution.py:155
  128.2 10.2 copy-start.5
  138.4 10.8 copy-start.2
  138.4 10.9 copy-start.6
  157.7 10.2 copy-start.5
  168.0 10.8 copy-start.2
  168.0 10.9 copy-start.6
  186.9 36.7 %copy-start.55 = (f32[1024]{0:T(1024)S(1)}, f32[1024]{0:T(1024)}, u32[]{:S(2)}) copy-start(f32[1024]{0:T(1024)} %param.30) | copy-start | bytes 12292
  194.7 68.6 %all-reduce.11.cloned.1.call-start = ((), (), s32[]{:S(2)}) async-start(), calls=%async_computation.5 | async-start | bytes 1048576 | tf_op jit(solution)/shard_map/psum | solution.py:178
  223.6 42.2 %copy-start.57 = (f32[256]{0:T(256)}, f32[256]{0:T(256)S(1)}, u32[]{:S(2)}) copy-start(f32[256]{0:T(256)S(1)} %add_rsqrt_fusion.2) | copy-start | bytes 3076
  234.6 239.6 %reduce-scatter.3.cloned.1.call-start = ((), (), s32[]{:S(2)}) async-start(), calls=%async_computation.6 | async-start | bytes 8912896 | tf_op jit(solution)/shard_map/reduce_scatter | solution.py:225
  265.8 10.0 copy-start.60
  277.6 10.5 copy-start.26
  277.6 10.5 copy-start.47
  288.0 11.7 copy-start.12
  323.2 10.4 copy-start.26
  323.2 10.4 copy-start.47
  333.6 11.7 copy-start.12
  345.3 7.8 copy-start.1
  345.3 7.8 copy-start.4
  369.5 213.1 %reduce-scatter.5.cloned.1.call-start = ((), (), s32[]{:S(2)}) async-start(), calls=%async_computation.7 | async-start | bytes 8912896 | tf_op jit(solution)/shard_map/reduce_scatter | solution.py:228
  370.0 259.7 %all-reduce.15.cloned.1.call-start = ((), (), s32[]{:S(2)}) async-start(), calls=%async_computation.9 | async-start | bytes 2097152 | tf_op jit(solution)/shard_map/psum | solution.py:166
  589.5 589.3 %all-reduce.13.cloned.1.call-start = ((), (), s32[]{:S(2)}) async-start(), calls=%async_computation.8 | async-start | bytes 62914560 | tf_op jit(solution)/shard_map/psum | solution.py:271
  601.0 30.4 %copy-start.59 = (f32[1024]{0:T(1024)S(1)}, f32[1024]{0:T(1024)}, u32[]{:S(2)}) copy-start(f32[1024]{0:T(1024)} %get-tuple-element.339) | copy-start | bytes 12292
  1178.9 11.1 slice-start.4
  (60 other events, 218.8 us)
Sparse Core Ops, SparseCore 0:
  18.0 53.3 all-gather.2
  74.1 49.0 all-gather.4
  194.9 27.0 all-reduce.8
  234.7 28.5 all-reduce.10
  369.6 104.5 reduce-scatter.2
  478.1 104.3 reduce-scatter.4
  589.6 40.0 all-reduce.14
  637.7 541.1 all-reduce.12
where the time goes:
time: 1210 us
  waiting for transfers between devices  833 us (69%)
  matrix products  179 us (15%)
  blocking collectives  69.2 us (6%)
  local copies, waits for them, and re-layouts  57.1 us (5%)
  other arithmetic  52.1 us (4%)
  between operations  15.3 us (1%)
    psum x1, waiting for transfers between devices, body(): lax.psum((attn_gain_term, query_weight_grad, key_weight_grad, value_weigh...  479 us
    reduce_scatter x1, waiting for transfers between devices, body(): lax.psum_scatter(value_parts.reshape(total, groups_here, head_dim), 'cp',...  104 us
    reduce_scatter x1, waiting for transfers between devices, body(): lax.psum_scatter(key_parts.reshape(total, groups_here, head_dim), 'cp', s...  82.1 us
    psum x1, blocking collectives, body(): lax.psum((attn_gain_term, query_weight_grad, key_weight_grad, value_weigh...  64.2 us
    all_gather x1, waiting for transfers between devices, body(): lax.all_gather(values_low, 'cp', axis=0, tiled=True)  47.4 us
    all_gather x1, waiting for transfers between devices, body(): lax.all_gather(key_low, 'cp', axis=0, tiled=True)  40.5 us
    dot_general x4, matrix products, scores_of(): jnp.einsum('rgeh,kgh->gerk', query_pairs, key_block, preferred_element_ty...  40.3 us
    unnamed x141, local copies, waits for them, and re-layouts  37.3 us
  transfers between devices with their start and end apart: 8, of which 8 were waited for; matrix products, arithmetic and copies ran while one was open for 5% of the time, Pallas kernels for 0%

commit v1 on v0

v1 whole, which is shorter than its diff:
```python
import functools
import math

import jax
import jax.numpy as jnp
from jax import lax
from jax.experimental import pallas as pl
from jax.experimental.pallas import tpu as pltpu
from jax.sharding import PartitionSpec as P

EPS = 1e-06
ROPE_BASE = 1000000.0
HEAD = 128
LOG2E = 1.4426950408889634
VMEM_LIMIT = 40 * 1024 * 1024
BF = jnp.bfloat16
F32 = jnp.float32


def nn(a, b):
    return lax.dot_general(a, b, (((1,), (0,)), ((), ())), preferred_element_type=F32)


def nt(a, b):
    return lax.dot_general(a, b, (((1,), (1,)), ((), ())), preferred_element_type=F32)


def tn(a, b):
    return lax.dot_general(a, b, (((0,), (0,)), ((), ())), preferred_element_type=F32)


def norm_rows(values):
    scale_rows = lax.rsqrt(jnp.mean(values * values, axis=-1, keepdims=True) + EPS)
    return (values * scale_rows, scale_rows)


def norm_back(grad_normed, normed, scale_rows):
    return scale_rows * (
        grad_normed - normed * jnp.mean(grad_normed * normed, axis=-1, keepdims=True)
    )


def ring_order(chips):
    if chips % 8:
        return list(range(chips))
    rows, cols = 4, chips // 4
    if cols % 2 or cols < 4:
        path = list(range(cols))
    else:
        path = list(range(cols // 2)) + list(range(cols - 1, cols // 2 - 1, -1))
    walk = []
    for row in range(rows):
        across = range(1, cols) if row % 2 == 0 else range(cols - 1, 0, -1)
        walk += [(row, col) for col in across]
    walk = [(0, 0)] + walk + [(row, 0) for row in range(rows - 1, 0, -1)]
    return [row * cols + path[col] for row, col in walk]


class Ring:
    def __init__(self, devices):
        self.chips = devices // 2
        order = ring_order(self.chips)
        self.order = order
        size = self.chips
        self.up = [
            (2 * order[i] + core, 2 * order[(i + 1) % size] + core)
            for i in range(size)
            for core in range(2)
        ]
        self.down = [(b, a) for a, b in self.up]
        self.swap = [(i, i ^ 1) for i in range(devices)]
        place = [0] * size
        for i, chip in enumerate(order):
            place[chip] = i
        index = lax.axis_index("cp")
        self.core = index % 2
        self.here = jnp.asarray(place, jnp.int32)[index // 2]
        self.half = size // 2

    def send_up(self, x):
        return lax.ppermute(x, "cp", self.up)

    def send_down(self, x):
        return lax.ppermute(x, "cp", self.down)

    def sibling(self, x):
        return lax.ppermute(x, "cp", self.swap)

    def gather_steps(self, own):
        upward = downward = own
        for step in range(1, self.half):
            upward = self.send_up(upward)
            downward = self.send_down(downward)
            yield [(-step, upward), (step, downward)]
        cut = own.shape[0] // 2
        yield [
            (
                self.half,
                jnp.concatenate(
                    [self.send_up(upward[:cut]), self.send_down(downward[cut:])], axis=0
                ),
            )
        ]

    def scatter(self, local):
        far = local(self.half).astype(BF)
        cut = far.shape[0] // 2
        upward = self.send_up(far[:cut])
        downward = self.send_down(far[cut:])
        for step in range(self.half - 1, 0, -1):
            mine_up, mine_down = local(step), local(-step)
            if step == self.half - 1:
                upward = jnp.concatenate(
                    [(mine_up[:cut].astype(F32) + upward.astype(F32)).astype(BF), mine_up[cut:].astype(BF)],
                    axis=0,
                )
                downward = jnp.concatenate(
                    [mine_down[:cut].astype(BF), (mine_down[cut:].astype(F32) + downward.astype(F32)).astype(BF)],
                    axis=0,
                )
            else:
                upward = (mine_up.astype(F32) + upward.astype(F32)).astype(BF)
                downward = (mine_down.astype(F32) + downward.astype(F32)).astype(BF)
            upward = self.send_up(upward)
            downward = self.send_down(downward)
        return local(0).astype(F32) + upward.astype(F32) + downward.astype(F32)


def assemble_kernel(count, table_ref, *refs):
    parts, out = refs[:count], refs[count]
    step = pl.program_id(0)
    for i in range(count):

        @pl.when(step == i)
        def _(i=i):
            out[...] = parts[i][...].astype(F32)


def all_reduce(ring, partial):
    rows, columns = partial.shape
    half = rows // 2
    shard = half // ring.chips
    mine = lax.dynamic_slice_in_dim(partial, ring.core * half, half)
    other = ring.sibling(lax.dynamic_slice_in_dim(partial, (1 - ring.core) * half, half))

    def local(offset):
        start = ((ring.here + offset + ring.chips) % ring.chips) * shard
        return (
            lax.dynamic_slice_in_dim(mine, start, shard).astype(F32)
            + lax.dynamic_slice_in_dim(other, start, shard).astype(F32)
        ).astype(BF)

    total = ring.scatter(local).astype(BF)
    parts, places = [total], [ring.here]
    for step in ring.gather_steps(total):
        for offset, part in step:
            parts.append(part)
            places.append((ring.here + offset + ring.chips) % ring.chips)
    others = [ring.sibling(part) for part in parts]
    table = jnp.stack(
        [ring.core * ring.chips + place for place in places]
        + [(1 - ring.core) * ring.chips + place for place in places]
    ).astype(jnp.int32)
    parts = parts + others
    count = len(parts)
    return pl.pallas_call(
        functools.partial(assemble_kernel, count),
        out_shape=jax.ShapeDtypeStruct((rows, columns), F32),
        grid_spec=pltpu.PrefetchScalarGridSpec(
            num_scalar_prefetch=1,
            grid=(count,),
            in_specs=[pl.BlockSpec((shard, columns), lambda i, t: (0, 0))] * count,
            out_specs=pl.BlockSpec((shard, columns), lambda i, t: (t[i], 0)),
        ),
        compiler_params=pltpu.CompilerParams(vmem_limit_bytes=VMEM_LIMIT),
    )(table, *parts)


def total_small(devices, x):
    x = x + lax.ppermute(x, "tp", [(0, 1), (1, 0)])
    bit = 1
    while bit < devices:
        x = x + lax.ppermute(x, "cp", [(i, i ^ bit) for i in range(devices)])
        bit *= 2
    return x


def pair_sum(x):
    x = x.astype(BF)
    return x.astype(F32) + lax.ppermute(x, "tp", [(0, 1), (1, 0)]).astype(F32)


def turn(values, cosine, sine):
    return values * cosine + pltpu.roll(values, values.shape[-1] // 2, 1) * sine


def turn_back(values, cosine, sine):
    return values * cosine - pltpu.roll(values, values.shape[-1] // 2, 1) * sine


def key_value_kernel(
    residual, gain, key_weight, value_weight, key_gain, cosine, sine, normed_out, raw_out, packed_out
):
    unit, _ = norm_rows(residual[...].astype(F32))
    normed = (unit * gain[...]).astype(BF)
    normed_out[...] = normed
    width = key_gain.shape[1]
    raw = nn(normed, key_weight[...])
    raw_out[...] = raw
    values = nn(normed, value_weight[...]).astype(BF)
    for group in range(raw.shape[1] // width):
        here = slice(group * width, (group + 1) * width)
        key_unit, _ = norm_rows(raw[:, here])
        packed_out[:, 2 * group * width : (2 * group + 1) * width] = turn(
            key_unit * key_gain[...], cosine[...], sine[...]
        ).astype(BF)
        packed_out[:, (2 * group + 1) * width : (2 * group + 2) * width] = values[:, here]


def query_kernel(normed, weight, gain, cosine, sine, raw_out, low_out):
    width = gain.shape[1]
    raw = nn(normed[...], weight[...])
    raw_out[...] = raw
    for head in range(raw.shape[1] // width):
        here = slice(head * width, (head + 1) * width)
        unit, _ = norm_rows(raw[:, here])
        low_out[:, here] = turn(unit * gain[...], cosine[...], sine[...]).astype(BF)


def heads_back_kernel(grad, raw, gain, cosine, sine, low_out, gain_out):
    width = gain.shape[1]
    total = jnp.zeros((8, width), F32)
    for head in range(raw.shape[1] // width):
        here = slice(head * width, (head + 1) * width)
        unit, scale_rows = norm_rows(raw[:, here])
        turned = turn_back(grad[:, here].astype(F32), cosine[...], sine[...])
        term = turned * unit
        total = total + jnp.sum(term.reshape(-1, 8, width), axis=0)
        low_out[:, here] = norm_back(turned * gain[...], unit, scale_rows).astype(BF)
    gain_out[...] = total


def whole_call(kernel, outs, *args):
    return pl.pallas_call(
        kernel,
        out_shape=[jax.ShapeDtypeStruct(shape, dtype) for shape, dtype in outs],
        compiler_params=pltpu.CompilerParams(vmem_limit_bytes=VMEM_LIMIT),
    )(*args)


def stacked(ref, start, span, width):
    rows = pl.ds(start, span)
    return jnp.concatenate([ref[rows, :width], ref[rows, width:]], axis=0)


def causal(span, transposed):
    shape = (span, 2 * span) if transposed else (2 * span, span)
    key = lax.broadcasted_iota(jnp.int32, shape, 0 if transposed else 1)
    row = lax.broadcasted_iota(jnp.int32, shape, 1 if transposed else 0)
    return key <= row % span


def forward_kernel(count, own, last, span, width, pick_ref, query, *refs):
    blocks, refs = refs[:count], refs[count:]
    scale = LOG2E / math.sqrt(width)
    if own:
        accum = refs[0]
    else:
        before, accum = refs[0], refs[1]
    outs = refs[1 if own else 2 :]
    if last:
        accum = outs[-1]
    ones = jnp.ones((span, width), BF)

    def weighted(rows, keys, values, allowed=None):
        scores = nt(rows, keys)
        probs = jnp.exp2(scores * scale)
        if allowed is not None:
            probs = jnp.where(allowed, probs, 0.0)
        return nn(probs.astype(BF), values)

    def extended(block, start):
        return jnp.concatenate([block[pl.ds(start, span), width:], ones], axis=1)

    keys = jnp.concatenate([block[:span, :width] for block in blocks], axis=0)
    values = jnp.concatenate([extended(block, 0) for block in blocks], axis=0)
    high = weighted(stacked(query, span, span, width), keys, values)
    if own:
        allowed = causal(span, False)
        for side in range(2):
            block = blocks[0]
            start = side * span
            part = weighted(
                stacked(query, start, span, width),
                block[start : start + span, :width],
                extended(block, start),
                allowed,
            )
            accum[0, side] = part + high if side else part
    else:
        accum[0, 0] = before[0, 0]
        accum[0, 1] = before[0, 1] + high
    for i in range(1 if own else 0, count):
        side = pick_ref[i]
        start = pl.multiple_of(side * span, span)
        block = blocks[i]
        accum[0, side] += weighted(
            stacked(query, start, span, width),
            block[pl.ds(start, span), :width],
            extended(block, start),
        )
    if last:
        wide, low, logs = outs[0], outs[1], outs[2]
        for side in range(2):
            rows = slice(side * span, (side + 1) * span)
            both = accum[0, side]
            mass = both[:, width:]
            out = both[:, :width] / mass
            for head in range(2):
                part = out[head * span : (head + 1) * span]
                columns = slice(head * width, (head + 1) * width)
                wide[rows, columns] = part
                low[rows, columns] = part.astype(BF)
            logs[0, side] = jnp.log2(mass).T[:8]


def attention_forward(query, blocks, picks, before, own, last):
    rows, columns = query.shape
    span = rows // 2
    width = HEAD
    groups = columns // (2 * width)
    count = len(blocks)
    tile = pl.BlockSpec((rows, 2 * width), lambda g: (0, g))
    accum_spec = pl.BlockSpec((1, 2, 2 * span, 2 * width), lambda g: (g, 0, 0, 0))
    accum_shape = jax.ShapeDtypeStruct((groups, 2, 2 * span, 2 * width), F32)
    args = [picks, query, *blocks]
    specs = [pl.BlockSpec(memory_space=pltpu.SMEM)] + [tile] * (1 + count)
    if not own:
        args.append(before)
        specs.append(accum_spec)
    scratch = []
    if last:
        outs = [
            jax.ShapeDtypeStruct((rows, columns), F32),
            jax.ShapeDtypeStruct((rows, columns), BF),
            jax.ShapeDtypeStruct((groups, 2, 8, 2 * span), F32),
        ]
        out_specs = [tile, tile, pl.BlockSpec((1, 2, 8, 2 * span), lambda g: (g, 0, 0, 0))]
        scratch = [pltpu.VMEM((1, 2, 2 * span, 2 * width), F32)]
    else:
        outs, out_specs = [accum_shape], [accum_spec]

    def kernel(*refs):
        if last and own:
            refs = (*refs[: 2 + count], None, *refs[2 + count :])
        elif last:
            refs = (*refs[: 3 + count], None, *refs[3 + count :])
        forward_kernel(count, own, last, span, width, *refs)

    return pl.pallas_call(
        kernel,
        out_shape=outs,
        grid=(groups,),
        in_specs=specs,
        out_specs=out_specs,
        scratch_shapes=scratch,
        compiler_params=pltpu.CompilerParams(vmem_limit_bytes=VMEM_LIMIT),
        cost_estimate=pl.CostEstimate(
            flops=groups * (2 * count + own) * 2 * span * span * width * 4,
            bytes_accessed=rows * columns * 2 * (count + 1) + 8 * groups * 4 * span * 2 * width * 2,
            transcendentals=groups * (2 * count + own) * 2 * span * span,
        ),
    )(*args)


def delta_kernel(grad, out, delta):
    width = grad.shape[1] // 2
    span = grad.shape[0] // 2
    for side in range(2):
        rows = slice(side * span, (side + 1) * span)
        product = grad[rows, :].astype(F32) * out[rows, :]
        stack = jnp.concatenate([product[:, :width], product[:, width:]], axis=0)
        total = jnp.sum(stack.T, axis=0, keepdims=True)
        delta[0, side] = jnp.broadcast_to(total, (8, 2 * span))


def attention_delta(grad, out):
    rows, columns = grad.shape
    width, span = HEAD, rows // 2
    groups = columns // (2 * width)
    tile = pl.BlockSpec((rows, 2 * width), lambda g: (0, g))
    return pl.pallas_call(
        delta_kernel,
        out_shape=jax.ShapeDtypeStruct((groups, 2, 8, 2 * span), F32),
        grid=(groups,),
        in_specs=[tile, tile],
        out_specs=pl.BlockSpec((1, 2, 8, 2 * span), lambda g: (g, 0, 0, 0)),
        compiler_params=pltpu.CompilerParams(vmem_limit_bytes=VMEM_LIMIT),
    )(grad, out)


def backward_kernel(count, own, first, last, span, width, pick_ref, query, grad, logs, delta, *refs):
    blocks, refs = refs[:count], refs[count:]
    if not first:
        before, refs = refs[0], refs[1:]
    outs, refs = refs[:count], refs[count:]
    if last:
        query_out, accum = refs
    else:
        accum = refs[0]
    scale = LOG2E / math.sqrt(width)
    factor = 1.0 / math.sqrt(width)

    def products(side, start, keys, values, allowed=None):
        rows = stacked(query, start, span, width)
        grads = stacked(grad, start, span, width)
        probs = jnp.exp2(nt(keys, rows) * scale - logs[0, side, :1])
        if allowed is not None:
            probs = jnp.where(allowed, probs, 0.0)
        prob_grad = nt(values, grads)
        score_grad = (probs * (prob_grad - delta[0, side, :1])).astype(BF)
        return (
            nn(score_grad, rows),
            nn(probs.astype(BF), grads),
            tn(keys, score_grad),
        )

    keys = jnp.concatenate([block[:span, :width] for block in blocks], axis=0)
    values = jnp.concatenate([block[:span, width:] for block in blocks], axis=0)
    low_keys, low_values, high_query = products(1, span, keys, values)
    if first:
        accum[0, 0] = jnp.zeros_like(high_query)
        accum[0, 1] = high_query
    else:
        accum[0, 0] = before[0, 0]
        accum[0, 1] = before[0, 1] + high_query
    for i in range(count):
        here = slice(i * span, (i + 1) * span)
        key_low, value_low = low_keys[here], low_values[here]
        block = blocks[i]
        if own and i == 0:
            allowed = causal(span, True)
            key_part, value_part, query_part = products(
                0, 0, block[:span, :width], block[:span, width:], allowed
            )
            accum[0, 0] += query_part
            key_low, value_low = key_low + key_part, value_low + value_part
            key_high, value_high, query_part = products(
                1, span, block[span:, :width], block[span:, width:], allowed
            )
            accum[0, 1] += query_part
        else:
            side = pick_ref[i]
            start = pl.multiple_of(side * span, span)
            key_part, value_part, query_part = products(
                side, start, block[pl.ds(start, span), :width], block[pl.ds(start, span), width:]
            )
            accum[0, side] += query_part
            low = side == 0
            key_low = key_low + jnp.where(low, key_part, 0.0)
            value_low = value_low + jnp.where(low, value_part, 0.0)
            key_high = jnp.where(low, 0.0, key_part)
            value_high = jnp.where(low, 0.0, value_part)
        outs[i][:span, :width] = (key_low * factor).astype(BF)
        outs[i][:span, width:] = value_low.astype(BF)
        outs[i][span:, :width] = (key_high * factor).astype(BF)
        outs[i][span:, width:] = value_high.astype(BF)
    if last:
        for side in range(2):
            part = accum[0, side].T * factor
            rows = slice(side * span, (side + 1) * span)
            query_out[rows, :width] = part[:span]
            query_out[rows, width:] = part[span:]


def attention_backward(query, grad, logs, delta, blocks, picks, before, own, last):
    rows, columns = query.shape
    span, width = rows // 2, HEAD
    groups = columns // (2 * width)
    count = len(blocks)
    first = before is None
    tile = pl.BlockSpec((rows, 2 * width), lambda g: (0, g))
    stat = pl.BlockSpec((1, 2, 8, 2 * span), lambda g: (g, 0, 0, 0))
    accum_block = (1, 2, width, 2 * span)
    accum_spec = pl.BlockSpec(accum_block, lambda g: (g, 0, 0, 0))
    args = [picks, query, grad, logs, delta, *blocks]
    specs = [pl.BlockSpec(memory_space=pltpu.SMEM), tile, tile, stat, stat] + [tile] * count
    if not first:
        args.append(before)
        specs.append(accum_spec)
    outs = [jax.ShapeDtypeStruct((rows, columns), BF)] * count
    out_specs = [tile] * count
    scratch = []
    if last:
        outs.append(jax.ShapeDtypeStruct((rows, columns), F32))
        out_specs.append(tile)
        scratch = [pltpu.VMEM(accum_block, F32)]
    else:
        outs.append(jax.ShapeDtypeStruct((groups, 2, width, 2 * span), F32))
        out_specs.append(accum_spec)
    return pl.pallas_call(
        functools.partial(backward_kernel, count, own, first, last, span, width),
        out_shape=outs,
        grid=(groups,),
        in_specs=specs,
        out_specs=out_specs,
        scratch_shapes=scratch,
        compiler_params=pltpu.CompilerParams(vmem_limit_bytes=VMEM_LIMIT),
        cost_estimate=pl.CostEstimate(
            flops=groups * (2 * count + own) * 2 * span * span * width * 10,
            bytes_accessed=rows * columns * 2 * (2 * count + 4),
            transcendentals=groups * (2 * count + own) * 2 * span * span,
        ),
    )(*args)


def body(
    devices,
    residual,
    cotangent,
    span_order,
    positions,
    attn_gain,
    query_weight,
    key_weight,
    value_weight,
    query_gain,
    key_gain,
    out_weight,
    mlp_gain,
    gate_weight,
    up_weight,
    down_weight,
):
    ring = Ring(devices)
    rows, model = residual.shape
    head_dim = query_gain.shape[0]
    span = rows // 2
    index = lax.axis_index("cp")
    pairs = span_order.reshape(-1, 2)
    ordered = lax.dynamic_slice_in_dim(pairs, index, 1)[0]
    in_order = ordered[0] < ordered[1]

    def canonical(x):
        return jnp.where(in_order, x, jnp.roll(x, span, axis=0))

    residual = canonical(residual)
    cotangent = canonical(cotangent)
    positions = canonical(positions)

    lows = jnp.min(pairs, axis=1).reshape(-1, 2)[jnp.asarray(ring.order)]
    lows = lax.dynamic_slice_in_dim(jnp.concatenate([lows, lows]), ring.here, ring.chips)
    lows = jnp.where(ring.core == 0, lows, lows[:, ::-1])
    picks = jnp.where(lows < jnp.min(ordered), 0, 1).astype(jnp.int32)

    half = head_dim // 2
    freq = ROPE_BASE ** (-(jnp.arange(half, dtype=F32) * 2.0) / head_dim)
    angle = positions.astype(F32)[:, None] * freq[None, :]
    cosine, sine = jnp.cos(angle), jnp.sin(angle)
    cosine = jnp.concatenate([cosine, cosine], axis=1)
    sine = jnp.concatenate([-sine, sine], axis=1)

    attn_gain_row = attn_gain.reshape(1, -1)
    mlp_gain_row = mlp_gain.reshape(1, -1)
    query_gain_row = query_gain.reshape(1, -1)
    key_gain_row = key_gain.reshape(1, -1)
    key_columns = key_weight.shape[1]
    query_columns = query_weight.shape[1]

    normed_low, keys_raw, packed = whole_call(
        key_value_kernel,
        [((rows, model), BF), ((rows, key_columns), F32), ((rows, 2 * key_columns), BF)],
        residual, attn_gain_row, key_weight, value_weight, key_gain_row, cosine, sine,
    )
    queries_raw, query_low = whole_call(
        query_kernel,
        [((rows, query_columns), F32), ((rows, query_columns), BF)],
        normed_low, query_weight, query_gain_row, cosine, sine,
    )

    def picks_of(offsets):
        both = [picks[offset % ring.chips] for offset in offsets]
        return jnp.concatenate([jnp.stack([b[0] for b in both]), jnp.stack([b[1] for b in both])])

    calls = [([0], [packed, ring.sibling(packed)])]
    state = attention_forward(query_low, calls[0][1], picks_of([0]), None, True, False)
    steps = list(ring.gather_steps(packed))
    for i, step in enumerate(steps):
        offsets = [offset for offset, _ in step]
        blocks = [block for _, block in step]
        blocks = blocks + [ring.sibling(block) for block in blocks]
        calls.append((offsets, blocks))
        state = attention_forward(
            query_low, blocks, picks_of(offsets), state[0], False, i == len(steps) - 1
        )
    attended, attended_low, logs = state

    residual_wide = residual.astype(F32)
    mixed = residual_wide + pair_sum(nn(attended_low, out_weight))
    normed_two, scale_two = norm_rows(mixed)
    normed_two_low = (normed_two * mlp_gain).astype(BF)
    gate = nn(normed_two_low, gate_weight)
    upward = nn(normed_two_low, up_weight)
    sigmoid_gate = jax.nn.sigmoid(gate)
    activated = gate * sigmoid_gate
    hidden_low = (activated * upward).astype(BF)
    hidden_grad = nt(cotangent, down_weight)
    gate_grad_low = (
        hidden_grad * upward * sigmoid_gate * (1.0 + gate * (1.0 - sigmoid_gate))
    ).astype(BF)
    up_grad_low = (hidden_grad * activated).astype(BF)
    normed_two_part = (nt(gate_grad_low, gate_weight) + nt(up_grad_low, up_weight)).astype(BF)
    normed_two_grad = pair_sum(normed_two_part)
    layer_out = mixed + pair_sum(nn(hidden_low, down_weight))
    both_grad_low = jnp.concatenate([gate_grad_low, up_grad_low], axis=1)
    both_sum = all_reduce(ring, tn(normed_two_low, both_grad_low).astype(BF))
    down_weight_sum = all_reduce(ring, tn(hidden_low, cotangent).astype(BF))

    mlp_gain_term = jnp.sum(normed_two_part.astype(F32) * normed_two, axis=0)
    mixed_grad = cotangent.astype(F32) + norm_back(
        normed_two_grad * mlp_gain, normed_two, scale_two
    )
    mixed_grad_low = mixed_grad.astype(BF)
    attended_grad = nt(mixed_grad_low, out_weight).astype(BF)
    delta = attention_delta(attended_grad, attended)

    query_state = [None]
    query_grads = []

    def local(offset):
        key = abs(offset)
        if key not in done:
            place = [i for i, call in enumerate(calls) if abs(call[0][0]) == key][0]
            offsets, blocks = calls[place]
            last = place == 0
            results = attention_backward(
                query_low, attended_grad, logs, delta, blocks, picks_of(offsets), query_state[0],
                place == 0, last,
            )
            if last:
                query_grads.append(results[-1])
            else:
                query_state[0] = results[-1]
            count = len(offsets)
            done[key] = {}
            for at, own, other in zip(offsets, results[:count], results[count : 2 * count]):
                done[key][at] = own.astype(F32) + ring.sibling(other).astype(F32)
        return done[key][offset]

    done = {}
    packed_grad = ring.scatter(local)
    (query_grad_rows,) = query_grads

    query_grad_low, query_gain_term = whole_call(
        heads_back_kernel,
        [((rows, query_columns), BF), ((8, head_dim), F32)],
        query_grad_rows, queries_raw, query_gain_row, cosine, sine,
    )
    split = packed_grad.reshape(rows, -1, 2, head_dim)
    key_grad = split[:, :, 0].reshape(rows, key_columns)
    value_grad_low = split[:, :, 1].reshape(rows, key_columns).astype(BF)
    key_grad_low, key_gain_term = whole_call(
        heads_back_kernel,
        [((rows, key_columns), BF), ((8, head_dim), F32)],
        key_grad, keys_raw, key_gain_row, cosine, sine,
    )

    normed_part = (
        nt(query_grad_low, query_weight)
        + nt(key_grad_low, key_weight)
        + nt(value_grad_low, value_weight)
    ).astype(BF)
    normed_grad = pair_sum(normed_part)
    out_weight_sum = all_reduce(ring, tn(attended_low, mixed_grad_low).astype(BF))
    projections = jnp.concatenate([query_grad_low, key_grad_low, value_grad_low], axis=1)
    projection_sum = all_reduce(ring, tn(normed_low, projections).astype(BF))

    normed_one, scale_one = norm_rows(residual_wide)
    attn_gain_term = jnp.sum(normed_part.astype(F32) * normed_one, axis=0)
    residual_grad = mixed_grad + norm_back(normed_grad * attn_gain, normed_one, scale_one)

    small = jnp.concatenate(
        [
            attn_gain_term,
            mlp_gain_term,
            jnp.sum(query_gain_term, axis=0),
            jnp.sum(key_gain_term, axis=0),
        ]
    ).reshape(-1, 128)
    small = total_small(devices, small).reshape(-1)
    attn_gain_grad, mlp_gain_grad = small[:model], small[model : 2 * model]
    query_gain_grad = small[2 * model : 2 * model + head_dim]
    key_gain_grad = small[2 * model + head_dim :]
    units = gate_weight.shape[1]
    return (
        canonical(layer_out).astype(BF),
        canonical(residual_grad),
        attn_gain_grad,
        projection_sum[:, :query_columns],
        projection_sum[:, query_columns : query_columns + key_columns],
        projection_sum[:, query_columns + key_columns :],
        query_gain_grad,
        key_gain_grad,
        out_weight_sum,
        mlp_gain_grad,
        both_sum[:, :units],
        both_sum[:, units:],
        down_weight_sum,
    )


def solution(mesh):
    return jax.shard_map(
        functools.partial(body, mesh.shape["cp"]),
        mesh=mesh,
        in_specs=(
            P("cp", None),
            P("cp", None),
            P(),
            P("cp"),
            P(),
            P(None, "tp"),
            P(None, "tp"),
            P(None, "tp"),
            P(),
            P(),
            P("tp", None),
            P(),
            P(None, "tp"),
            P(None, "tp"),
            P("tp", None),
        ),
        out_specs=(
            P("cp", None),
            P("cp", None),
            P(),
            P(None, "tp"),
            P(None, "tp"),
            P(None, "tp"),
            P(),
            P(),
            P("tp", None),
            P(),
            P(None, "tp"),
            P(None, "tp"),
            P("tp", None),
        ),
        check_vma=False,
    )
```

time: 1210 us -> 584 us (0.48)
  waiting for transfers between devices: 833 us -> 269 us
  matrix products: 179 us -> 16.3 us
  starting transfers between devices: 1.4 us -> 103 us
  Pallas kernels: 0 us -> 85.2 us
  blocking collectives: 69.2 us -> 0 us
    psum x4 -> x0, waiting for transfers between devices: 558 us -> none  [the longest x1 479 us: body(): lax.psum((attn_gain_term, query_weight_grad, key_weight_grad, value_weigh...]
    ppermute x0 -> x141, waiting for transfers between devices: none -> 269 us  [the longest x40 141 us: send_up(): return lax.ppermute(x, 'cp', self.up)]
    reduce_scatter x2 -> x0, waiting for transfers between devices: 186 us -> none  [the longest x1 104 us: body(): lax.psum_scatter(value_parts.reshape(total, groups_here, head_dim), 'cp',...]
    dot_general x35 -> x15, matrix products: 179 us -> 16.3 us  [the longest x7 6.28 us: nt(): lax.dot_general(a, b, (((1,), (1,)), ((), ())), preferred_element_type=F32)]
    ppermute x0 -> x141, starting transfers between devices: none -> 103 us  [the longest x40 51.6 us: send_down(): return lax.ppermute(x, 'cp', self.down)]
    all_gather x2 -> x0, waiting for transfers between devices: 87.9 us -> none  [the longest x1 47.4 us: body(): lax.all_gather(values_low, 'cp', axis=0, tiled=True)]
    pallas_call x0 -> x19, Pallas kernels: none -> 85.2 us  [the longest x5 30.3 us: attention_backward(): pl.pallas_call(functools.partial(backward_kernel, count, own, first, last...]
    psum x2 -> x0, blocking collectives: 69.2 us -> none  [the longest x1 64.2 us: body(): lax.psum((attn_gain_term, query_weight_grad, key_weight_grad, value_weigh...]
  transfers between devices with their start and end apart: 8 -> 141, of which waited for: 8 -> 51; matrix products, arithmetic and copies ran while one was open for 5% -> 14% of each run, Pallas kernels for 0% -> 13%
where the time goes in v1:
time: 584 us; the launch traced here: 577 us
  waiting for transfers between devices  269 us (46%)
  starting transfers between devices  103 us (18%)
  Pallas kernels  85.2 us (15%)
  local copies, waits for them, and re-layouts  46.7 us (8%)
  other arithmetic  43.9 us (8%)
  matrix products  16.3 us (3%)
  between operations  12.8 us (2%)
    ppermute x40, waiting for transfers between devices, send_up(): return lax.ppermute(x, 'cp', self.up)  141 us
    ppermute x40, waiting for transfers between devices, send_down(): return lax.ppermute(x, 'cp', self.down)  96.4 us
    ppermute x40, starting transfers between devices, send_down(): return lax.ppermute(x, 'cp', self.down)  51.6 us
    pallas_call x5, Pallas kernels, attention_backward(): pl.pallas_call(functools.partial(backward_kernel, count, own, first, last...  30.3 us
    ppermute x40, starting transfers between devices, send_up(): return lax.ppermute(x, 'cp', self.up)  29.9 us
    pallas_call x4, Pallas kernels, all_reduce(): pl.pallas_call(functools.partial(assemble_kernel, count), out_shape=jax.S...  27.7 us
    ppermute x4, waiting for transfers between devices, pair_sum(): return x.astype(F32) + lax.ppermute(x, 'tp', [(0, 1), (1, 0)]).astype(F32)  26.8 us
    pallas_call x5, Pallas kernels, attention_forward(): pl.pallas_call(kernel, out_shape=outs, grid=(groups,), in_specs=specs, ou...  21.8 us
  transfers between devices with their start and end apart: 141, of which 51 were waited for; matrix products, arithmetic and copies ran while one was open for 14% of the time, Pallas kernels for 13%

profile of v1, /device:TPU:0, one launch (start us, length us, event | category | flops | bytes accessed | tf_op | source)
XLA Modules:
  0.0 576.5 jit_solution(12130429122291221236)
XLA Ops:
  15.2 12.2 %collective-permute-done.refs_2_.refs_0_ = bf16[256,1024]{1,0:T(8,128)(2,1)} collective-permute-done((bf16[256,1024]{1,0:T(8,128)(2,1)}, bf16[256,1024]{1,0:T(8,128)(2,1)}, u32[]{:S(2)}, u32[]{:S(2)}) %collective-permute-start) | collective-permute-done | bytes 524320 | tf_op jit(solution)/shard_map/ppermute | solution.py:81
  33.0 7.8 %collective-permute-done.1.refs_2_.refs_0_ = bf16[256,1024]{1,0:T(8,128)(2,1)} collective-permute-done((bf16[256,1024]{1,0:T(8,128)(2,1)}, bf16[256,1024]{1,0:T(8,128)(2,1)}, u32[]{:S(2)}, u32[]{:S(2)}) %collective-permute-start.1) | collective-permute-done | bytes 524320 | tf_op jit(solution)/shard_map/ppermute | solution.py:81
  90.2 4.9 shard_map.267.refs_6_
  95.2 4.9 shard_map.268.refs_6_
  111.7 11.5 %collective-permute-done.16 = bf16[256,1024]{1,0:T(8,128)(2,1)S(1)} collective-permute-done((bf16[256,1024]{1,0:T(8,128)(2,1)S(1)}, bf16[256,1024]{1,0:T(8,128)(2,1)S(1)}, u32[]{:S(2)}, u32[]{:S(2)}) %collective-permute-start.16) | collective-permute-done | bytes 524320 | tf_op jit(solution)/shard_map/ppermute | solution.py:190
  138.8 15.3 %collective-permute-done.18 = bf16[256,1024]{1,0:T(8,128)(2,1)S(1)} collective-permute-done((bf16[256,1024]{1,0:T(8,128)(2,1)S(1)}, bf16[256,1024]{1,0:T(8,128)(2,1)S(1)}, u32[]{:S(2)}, u32[]{:S(2)}) %collective-permute-start.18) | collective-permute-done | bytes 524320 | tf_op jit(solution)/shard_map/ppermute | solution.py:190
  160.9 6.4 %shard_map.273 = (bf16[256,1024]{1,0:T(8,128)(2,1)S(1)}, bf16[256,1024]{1,0:T(8,128)(2,1)S(1)}, bf16[256,1024]{1,0:T(8,128)(2,1)S(1)}, bf16[256,1024]{1,0:T(8,128)(2,1)S(1)}, f32[4,2,128,256]{3,2,1,0:T(8,128)S(1)}) custom-call(s32[4]{0:T(128)S(1)} %pad_add_fusion.2.refs_0_.pick_ref, bf16[256,1024]{1,0:T(8,128)(2,1)S(1)} %copy-done.3, ...), custom_call_target="tpu_custom_call" | custom-call | flops 1342177280 | bytes 6291456 | tf_op jit(solution)/shard_map/pallas_call | solution.py:501
  167.8 6.5 %shard_map.274 = (bf16[256,1024]{1,0:T(8,128)(2,1)S(1)}, bf16[256,1024]{1,0:T(8,128)(2,1)S(1)}, bf16[256,1024]{1,0:T(8,128)(2,1)S(1)}, bf16[256,1024]{1,0:T(8,128)(2,1)S(1)}, f32[4,2,128,256]{3,2,1,0:T(8,128)S(1)}) custom-call(s32[4]{0:T(128)S(1)} %pad_add_fusion.3.refs_0_.pick_ref, bf16[256,1024]{1,0:T(8,128)(2,1)S(1)} %copy-done.3, ...), custom_call_target="tpu_custom_call" | custom-call | flops 1342177280 | bytes 6291456 | tf_op jit(solution)/shard_map/pallas_call | solution.py:501
  177.2 6.6 %shard_map.275 = (bf16[256,1024]{1,0:T(8,128)(2,1)S(1)}, bf16[256,1024]{1,0:T(8,128)(2,1)S(1)}, bf16[256,1024]{1,0:T(8,128)(2,1)S(1)}, bf16[256,1024]{1,0:T(8,128)(2,1)S(1)}, f32[4,2,128,256]{3,2,1,0:T(8,128)S(1)}) custom-call(s32[4]{0:T(128)S(1)} %pad_add_fusion.4.refs_0_.pick_ref, bf16[256,1024]{1,0:T(8,128)(2,1)S(1)} %copy-done.3, ...), custom_call_target="tpu_custom_call" | custom-call | flops 1342177280 | bytes 6291456 | tf_op jit(solution)/shard_map/pallas_call | solution.py:501
  183.9 6.5 %shard_map.276 = (bf16[256,1024]{1,0:T(8,128)(2,1)S(1)}, bf16[256,1024]{1,0:T(8,128)(2,1)}, f32[256,1024]{1,0:T(8,128)S(1)}) custom-call(s32[2]{0:T(128)S(1)} %pad_add_fusion.5.refs_0_.pick_ref, bf16[256,1024]{1,0:T(8,128)(2,1)S(1)} %copy-done.3, bf16[256,1024]{1,0:T(8,128)(2,1)S(1)} %convolution_convert_fusion.4.grad, ...), custom_call_target="tpu_custom_call" | custom-call | flops 838860800 | bytes 4194304 | tf_op jit(solution)/shard_map/pallas_call | solution.py:501
  194.6 5.3 collective-permute-done.31
  201.7 5.7 collective-permute-done.24
  211.7 11.1 %collective-permute-done.67 = bf16[32,1024]{1,0:T(8,128)(2,1)S(1)} collective-permute-done((bf16[32,1024]{1,0:T(8,128)(2,1)S(1)}, bf16[32,1024]{1,0:T(8,128)(2,1)S(1)}, u32[]{:S(2)}, u32[]{:S(2)}) %collective-permute-start.67) | collective-permute-done | bytes 65568 | tf_op jit(solution)/shard_map/ppermute | solution.py:81
  223.1 5.3 collective-permute-done.117
  249.9 8.1 %collective-permute-done.72 = bf16[64,1024]{1,0:T(8,128)(2,1)S(1)} collective-permute-done((bf16[64,1024]{1,0:T(8,128)(2,1)S(1)}, bf16[64,1024]{1,0:T(8,128)(2,1)S(1)}, u32[]{:S(2)}, u32[]{:S(2)}) %collective-permute-start.72) | collective-permute-done | bytes 131104 | tf_op jit(solution)/shard_map/ppermute | solution.py:84
  258.8 4.9 collective-permute-done.119
  284.2 8.9 %collective-permute-done.75.refs_1_ = bf16[64,1024]{1,0:T(8,128)(2,1)} collective-permute-done((bf16[64,1024]{1,0:T(8,128)(2,1)S(1)}, bf16[64,1024]{1,0:T(8,128)(2,1)}, u32[]{:S(2)}, u32[]{:S(2)}) %collective-permute-start.75) | collective-permute-done | bytes 131104 | tf_op jit(solution)/shard_map/ppermute | solution.py:81
  315.1 12.1 %collective-permute-done.81 = bf16[32,1024]{1,0:T(8,128)(2,1)S(1)} collective-permute-done((bf16[32,1024]{1,0:T(8,128)(2,1)S(1)}, bf16[32,1024]{1,0:T(8,128)(2,1)S(1)}, u32[]{:S(2)}, u32[]{:S(2)}) %collective-permute-start.81) | collective-permute-done | bytes 65568 | tf_op jit(solution)/shard_map/ppermute | solution.py:81
  332.0 5.2 collective-permute-done.125.refs_1_
  373.2 8.1 %shard_map.280 = f32[1024,1024]{1,0:T(8,128)} custom-call(s32[16]{0:T(128)S(1)} %stack.50.table_ref, bf16[64,1024]{1,0:T(8,128)(2,1)S(1)} %add_convert_fusion.46.refs_0_, bf16[64,1024]{1,0:T(8,128)(2,1)} %collective-permute-done.75.refs_1_, bf16[64,1024]{1,0:T(8,128)(2,1)} %collective-permute-done.76.refs_2_, bf16[64,1024]{1,0:T(8,128)(2,1)S(1)} %copy-done.44, ...), custom_call_target="tpu_custom_call" | custom-call | tf_op jit(solution)/shard_map/pallas_call | solution.py:166
  393.7 5.3 collective-permute-done.94
  403.2 9.3 %collective-permute-done.97 = bf16[64,3072]{1,0:T(8,128)(2,1)S(1)} collective-permute-done((bf16[64,3072]{1,0:T(8,128)(2,1)S(1)}, bf16[64,3072]{1,0:T(8,128)(2,1)S(1)}, u32[]{:S(2)}, u32[]{:S(2)}) %collective-permute-start.97) | collective-permute-done | bytes 393248 | tf_op jit(solution)/shard_map/ppermute | solution.py:84
  419.2 8.2 %collective-permute-done.98 = bf16[64,3072]{1,0:T(8,128)(2,1)S(1)} collective-permute-done((bf16[64,3072]{1,0:T(8,128)(2,1)S(1)}, bf16[64,3072]{1,0:T(8,128)(2,1)S(1)}, u32[]{:S(2)}, u32[]{:S(2)}) %collective-permute-start.98) | collective-permute-done | bytes 393248 | tf_op jit(solution)/shard_map/ppermute | solution.py:84
  436.2 6.8 %collective-permute-done.99 = bf16[64,3072]{1,0:T(8,128)(2,1)S(1)} collective-permute-done((bf16[64,3072]{1,0:T(8,128)(2,1)S(1)}, bf16[64,3072]{1,0:T(8,128)(2,1)S(1)}, u32[]{:S(2)}, u32[]{:S(2)}) %collective-permute-start.99) | collective-permute-done | bytes 393248 | tf_op jit(solution)/shard_map/ppermute | solution.py:84
  445.1 7.1 %collective-permute-done.44 = bf16[64,2048]{1,0:T(8,128)(2,1)S(1)} collective-permute-done((bf16[64,2048]{1,0:T(8,128)(2,1)S(1)}, bf16[64,2048]{1,0:T(8,128)(2,1)S(1)}, u32[]{:S(2)}, u32[]{:S(2)}) %collective-permute-start.44) | collective-permute-done | bytes 262176 | tf_op jit(solution)/shard_map/ppermute | solution.py:81
  455.5 8.4 %collective-permute-done.100.refs_1_ = bf16[64,3072]{1,0:T(8,128)(2,1)S(1)} collective-permute-done((bf16[64,3072]{1,0:T(8,128)(2,1)S(1)}, bf16[64,3072]{1,0:T(8,128)(2,1)S(1)}, u32[]{:S(2)}, u32[]{:S(2)}) %collective-permute-start.100) | collective-permute-done | bytes 393248 | tf_op jit(solution)/shard_map/ppermute | solution.py:81
  483.0 9.9 %collective-permute-done.45 = bf16[64,2048]{1,0:T(8,128)(2,1)S(1)} collective-permute-done((bf16[64,2048]{1,0:T(8,128)(2,1)S(1)}, bf16[64,2048]{1,0:T(8,128)(2,1)S(1)}, u32[]{:S(2)}, u32[]{:S(2)}) %collective-permute-start.45) | collective-permute-done | bytes 262176 | tf_op jit(solution)/shard_map/ppermute | solution.py:81
  498.6 7.4 %collective-permute-done.105.refs_6_ = bf16[64,3072]{1,0:T(8,128)(2,1)S(1)} collective-permute-done((bf16[64,3072]{1,0:T(8,128)(2,1)S(1)}, bf16[64,3072]{1,0:T(8,128)(2,1)S(1)}, u32[]{:S(2)}, u32[]{:S(2)}) %collective-permute-start.105) | collective-permute-done | bytes 393248 | tf_op jit(solution)/shard_map/ppermute | solution.py:84
  532.7 8.3 %shard_map.282 = f32[1536,1024]{1,0:T(8,128)} custom-call(s32[16]{0:T(128)S(1)} %stack.50.table_ref, bf16[96,1024]{1,0:T(8,128)(2,1)S(1)} %copy-done.21, bf16[96,1024]{1,0:T(8,128)(2,1)} %collective-permute-done.125.refs_1_, bf16[96,1024]{1,0:T(8,128)(2,1)S(1)} %copy-done.42, bf16[96,1024]{1,0:T(8,128)(2,1)} %collective-permute-done.127.refs_3_, ...), custom_call_target="tpu_custom_call" | custom-call | tf_op jit(solution)/shard_map/pallas_call | solution.py:166
  541.6 8.9 %shard_map.281 = f32[1024,3072]{1,0:T(8,128)} custom-call(s32[16]{0:T(128)S(1)} %stack.50.table_ref, bf16[64,3072]{1,0:T(8,128)(2,1)S(1)} %add_convert_fusion.5.refs_0_, bf16[64,3072]{1,0:T(8,128)(2,1)S(1)} %collective-permute-done.100.refs_1_, bf16[64,3072]{1,0:T(8,128)(2,1)S(1)} %collective-permute-done.101.refs_2_, ...), custom_call_target="tpu_custom_call" | custom-call | tf_op jit(solution)/shard_map/pallas_call | solution.py:166
  551.5 5.1 collective-permute-done.57
  557.7 10.6 %fusion.34 = (f32[1024,1536]{1,0:T(8,128)}, f32[1024,1536]{1,0:T(8,128)}) fusion(f32[1024,3072]{1,0:T(8,128)} %shard_map.281), kind=kLoop, calls=%fused_computation.188 | loop fusion | bytes 25165824 | tf_op jit(solution)/shard_map/slice | solution.py:707
  (572 shorter events, 311.3 us)
Async XLA Ops:
  29.1 50.9 %collective-permute-start.15 = (bf16[256,1024]{1,0:T(8,128)(2,1)}, bf16[256,1024]{1,0:T(8,128)(2,1)}, u32[]{:S(2)}, u32[]{:S(2)}) collective-permute-start(bf16[256,1024]{1,0:T(8,128)(2,1)} %get-tuple-element.48.refs_2_.refs_0_), channel_id=1, source_target_pairs={{0,1},{1,0},{2,3},{3,2},{4,5},{5,4},{6,7},{7,6},{8,9},{9,8},{10,11... | collective-permute-start | bytes 1572872 | tf_op jit(solution)/shard_map/ppermute | solution.py:87
  48.8 31.8 %collective-permute-start.13 = (bf16[256,1024]{1,0:T(8,128)(2,1)}, bf16[256,1024]{1,0:T(8,128)(2,1)}, u32[]{:S(2)}, u32[]{:S(2)}) collective-permute-start(bf16[256,1024]{1,0:T(8,128)(2,1)} %collective-permute-done.refs_2_.refs_0_), channel_id=1, source_target_pairs={{0,1},{1,0},{2,3},{3,2},{4,5},{5,4},{6,7},{7,6},{8,9},{9,8},{10,11... | collective-permute-start | bytes 1572872 | tf_op jit(solution)/shard_map/ppermute | solution.py:87
  50.2 31.9 %collective-permute-start.14 = (bf16[256,1024]{1,0:T(8,128)(2,1)}, bf16[256,1024]{1,0:T(8,128)(2,1)}, u32[]{:S(2)}, u32[]{:S(2)}) collective-permute-start(bf16[256,1024]{1,0:T(8,128)(2,1)} %collective-permute-done.4.refs_3_.refs_1_), channel_id=1, source_target_pairs={{0,1},{1,0},{2,3},{3,2},{4,5},{5,4},{6,7},{7,6},{8,9},{9,8},{10,11... | collective-permute-start | bytes 1572872 | tf_op jit(solution)/shard_map/ppermute | solution.py:87
  54.7 24.2 %collective-permute-start.3 = (bf16[128,1024]{1,0:T(8,128)(2,1)}, bf16[128,1024]{1,0:T(8,128)(2,1)}, u32[]{:S(2)}, u32[]{:S(2)}) collective-permute-start(bf16[128,1024]{1,0:T(8,128)(2,1)} %slice.457), channel_id=1, source_target_pairs={{0,2},{1,3},{2,6},{3,7},{6,10},{7,11},{10,14},{11,15},{14,12},{15,... | collective-permute-start | bytes 786440 | tf_op jit(solution)/shard_map/ppermute | solution.py:81
  82.0 22.5 %collective-permute-start.8 = (bf16[256,1024]{1,0:T(8,128)(2,1)S(1)}, bf16[256,1024]{1,0:T(8,128)(2,1)S(1)}, u32[]{:S(2)}, u32[]{:S(2)}) collective-permute-start(bf16[256,1024]{1,0:T(8,128)(2,1)S(1)} %constant_dynamic-update-slice_fusion.refs_2_.refs_0_), channel_id=1, source_target_pairs={{0,1},{1,0},{2,3},{3,2},{4,5},{5,4},{6,7},{7,6},{8,9},{9,8},{10,11... | collective-permute-start | bytes 1572872 | tf_op jit(solution)/shard_map/ppermute | solution.py:87
  129.1 46.1 %collective-permute-start.17 = (bf16[256,1024]{1,0:T(8,128)(2,1)}, bf16[256,1024]{1,0:T(8,128)(2,1)}, u32[]{:S(2)}, u32[]{:S(2)}) collective-permute-start(bf16[256,1024]{1,0:T(8,128)(2,1)} %convolution_convert_fusion.6), channel_id=1, source_target_pairs={{0,16},{16,0},{1,17},{17,1},{2,18},{18,2},{3,19},{19,3},{4,20},{20... | collective-permute-start | bytes 1572872 | tf_op jit(solution)/shard_map/ppermute | solution.py:190
  137.0 72.8 %collective-permute-start.116 = (bf16[768,1024]{1,0:T(8,128)(2,1)}, bf16[768,1024]{1,0:T(8,128)(2,1)S(1)}, u32[]{:S(2)}, u32[]{:S(2)}) collective-permute-start(bf16[768,1024]{1,0:T(8,128)(2,1)} %constant_dynamic-slice_fusion), channel_id=1, source_target_pairs={{0,1},{1,0},{2,3},{3,2},{4,5},{5,4},{6,7},{7,6},{8,9},{9,8},{10,11... | collective-permute-start | bytes 4718600 | tf_op jit(solution)/shard_map/ppermute | solution.py:87
  167.3 23.5 %collective-permute-start.30 = (bf16[256,1024]{1,0:T(8,128)(2,1)S(1)}, bf16[256,1024]{1,0:T(8,128)(2,1)S(1)}, u32[]{:S(2)}, u32[]{:S(2)}) collective-permute-start(bf16[256,1024]{1,0:T(8,128)(2,1)S(1)} %get-tuple-element.74), channel_id=1, source_target_pairs={{0,1},{1,0},{2,3},{3,2},{4,5},{5,4},{6,7},{7,6},{8,9},{9,8},{10,11... | collective-permute-start | bytes 1572872 | tf_op jit(solution)/shard_map/ppermute | solution.py:87
  167.3 23.1 %collective-permute-start.23 = (bf16[256,1024]{1,0:T(8,128)(2,1)S(1)}, bf16[256,1024]{1,0:T(8,128)(2,1)S(1)}, u32[]{:S(2)}, u32[]{:S(2)}) collective-permute-start(bf16[256,1024]{1,0:T(8,128)(2,1)S(1)} %get-tuple-element.68), channel_id=1, source_target_pairs={{0,1},{1,0},{2,3},{3,2},{4,5},{5,4},{6,7},{7,6},{8,9},{9,8},{10,11... | collective-permute-start | bytes 1572872 | tf_op jit(solution)/shard_map/ppermute | solution.py:87
  174.3 59.2 %collective-permute-start.29 = (bf16[256,1024]{1,0:T(8,128)(2,1)S(1)}, bf16[256,1024]{1,0:T(8,128)(2,1)S(1)}, u32[]{:S(2)}, u32[]{:S(2)}) collective-permute-start(bf16[256,1024]{1,0:T(8,128)(2,1)S(1)} %get-tuple-element.72), channel_id=1, source_target_pairs={{0,1},{1,0},{2,3},{3,2},{4,5},{5,4},{6,7},{7,6},{8,9},{9,8},{10,11... | collective-permute-start | bytes 1572872 | tf_op jit(solution)/shard_map/ppermute | solution.py:87
  190.5 45.5 %collective-permute-start.21 = (bf16[256,1024]{1,0:T(8,128)(2,1)S(1)}, bf16[256,1024]{1,0:T(8,128)(2,1)S(1)}, u32[]{:S(2)}, u32[]{:S(2)}) collective-permute-start(bf16[256,1024]{1,0:T(8,128)(2,1)S(1)} %get-tuple-element.64), channel_id=1, source_target_pairs={{0,1},{1,0},{2,3},{3,2},{4,5},{5,4},{6,7},{7,6},{8,9},{9,8},{10,11... | collective-permute-start | bytes 1572872 | tf_op jit(solution)/shard_map/ppermute | solution.py:87
  207.4 26.7 %collective-permute-start.32 = (bf16[256,1024]{1,0:T(8,128)(2,1)S(1)}, bf16[256,1024]{1,0:T(8,128)(2,1)S(1)}, u32[]{:S(2)}, u32[]{:S(2)}) collective-permute-start(bf16[256,1024]{1,0:T(8,128)(2,1)S(1)} %pad_maximum_fusion.1), channel_id=1, source_target_pairs={{2,0},{3,1},{6,2},{7,3},{10,6},{11,7},{14,10},{15,11},{12,14},{13,... | collective-permute-start | bytes 1572872 | tf_op jit(solution)/shard_map/ppermute | solution.py:84
  209.2 28.3 %collective-permute-start.25 = (bf16[256,1024]{1,0:T(8,128)(2,1)S(1)}, bf16[256,1024]{1,0:T(8,128)(2,1)S(1)}, u32[]{:S(2)}, u32[]{:S(2)}) collective-permute-start(bf16[256,1024]{1,0:T(8,128)(2,1)S(1)} %pad_maximum_fusion), channel_id=1, source_target_pairs={{0,2},{1,3},{2,6},{3,7},{6,10},{7,11},{10,14},{11,15},{14,12},{15,... | collective-permute-start | bytes 1572872 | tf_op jit(solution)/shard_map/ppermute | solution.py:81
  233.4 113.5 %collective-permute-start.91 = (bf16[512,3072]{1,0:T(8,128)(2,1)}, bf16[512,3072]{1,0:T(8,128)(2,1)}, u32[]{:S(2)}, u32[]{:S(2)}) collective-permute-start(bf16[512,3072]{1,0:T(8,128)(2,1)} %constant_dynamic-slice_fusion.1), channel_id=1, source_target_pairs={{0,1},{1,0},{2,3},{3,2},{4,5},{5,4},{6,7},{7,6},{8,9},{9,8},{10,11... | collective-permute-start | bytes 9437192 | tf_op jit(solution)/shard_map/ppermute | solution.py:87
  233.5 43.4 %collective-permute-start.28 = (bf16[256,1024]{1,0:T(8,128)(2,1)S(1)}, bf16[256,1024]{1,0:T(8,128)(2,1)S(1)}, u32[]{:S(2)}, u32[]{:S(2)}) collective-permute-start(bf16[256,1024]{1,0:T(8,128)(2,1)S(1)} %get-tuple-element.70), channel_id=1, source_target_pairs={{0,1},{1,0},{2,3},{3,2},{4,5},{5,4},{6,7},{7,6},{8,9},{9,8},{10,11... | collective-permute-start | bytes 1572872 | tf_op jit(solution)/shard_map/ppermute | solution.py:87
  236.0 34.2 %collective-permute-start.121 = (bf16[48,1024]{1,0:T(8,128)(2,1)S(1)}, bf16[48,1024]{1,0:T(8,128)(2,1)S(1)}, u32[]{:S(2)}, u32[]{:S(2)}) collective-permute-start(bf16[48,1024]{1,0:T(8,128)(2,1)S(1)} %get-tuple-element.127), channel_id=1, source_target_pairs={{2,0},{3,1},{6,2},{7,3},{10,6},{11,7},{14,10},{15,11},{12,14},{13,... | collective-permute-start | bytes 294920 | tf_op jit(solution)/shard_map/ppermute | solution.py:84
  243.2 39.3 %collective-permute-start.33 = (bf16[256,1024]{1,0:T(8,128)(2,1)S(1)}, bf16[256,1024]{1,0:T(8,128)(2,1)S(1)}, u32[]{:S(2)}, u32[]{:S(2)}) collective-permute-start(bf16[256,1024]{1,0:T(8,128)(2,1)S(1)} %add_convert_fusion.1), channel_id=1, source_target_pairs={{2,0},{3,1},{6,2},{7,3},{10,6},{11,7},{14,10},{15,11},{12,14},{13,... | collective-permute-start | bytes 1572872 | tf_op jit(solution)/shard_map/ppermute | solution.py:84
  274.7 25.9 %collective-permute-start.20 = (bf16[256,1024]{1,0:T(8,128)(2,1)S(1)}, bf16[256,1024]{1,0:T(8,128)(2,1)S(1)}, u32[]{:S(2)}, u32[]{:S(2)}) collective-permute-start(bf16[256,1024]{1,0:T(8,128)(2,1)S(1)} %get-tuple-element.62), channel_id=1, source_target_pairs={{0,1},{1,0},{2,3},{3,2},{4,5},{5,4},{6,7},{7,6},{8,9},{9,8},{10,11... | collective-permute-start | bytes 1572872 | tf_op jit(solution)/shard_map/ppermute | solution.py:87
  277.0 24.4 %collective-permute-start.26 = (bf16[256,1024]{1,0:T(8,128)(2,1)S(1)}, bf16[256,1024]{1,0:T(8,128)(2,1)S(1)}, u32[]{:S(2)}, u32[]{:S(2)}) collective-permute-start(bf16[256,1024]{1,0:T(8,128)(2,1)S(1)} %add_convert_fusion.3), channel_id=1, source_target_pairs={{0,2},{1,3},{2,6},{3,7},{6,10},{7,11},{10,14},{11,15},{14,12},{15,... | collective-permute-start | bytes 1572872 | tf_op jit(solution)/shard_map/ppermute | solution.py:81
  309.8 22.1 %collective-permute-start.19 = (bf16[256,1024]{1,0:T(8,128)(2,1)}, bf16[256,1024]{1,0:T(8,128)(2,1)}, u32[]{:S(2)}, u32[]{:S(2)}) collective-permute-start(bf16[256,1024]{1,0:T(8,128)(2,1)} %get-tuple-element.60), channel_id=1, source_target_pairs={{0,1},{1,0},{2,3},{3,2},{4,5},{5,4},{6,7},{7,6},{8,9},{9,8},{10,11... | collective-permute-start | bytes 1572872 | tf_op jit(solution)/shard_map/ppermute | solution.py:87
  309.8 27.3 %collective-permute-start.34 = (bf16[256,1024]{1,0:T(8,128)(2,1)}, bf16[256,1024]{1,0:T(8,128)(2,1)}, u32[]{:S(2)}, u32[]{:S(2)}) collective-permute-start(bf16[256,1024]{1,0:T(8,128)(2,1)} %add_convert_fusion), channel_id=1, source_target_pairs={{2,0},{3,1},{6,2},{7,3},{10,6},{11,7},{14,10},{15,11},{12,14},{13,... | collective-permute-start | bytes 1572872 | tf_op jit(solution)/shard_map/ppermute | solution.py:84
  311.5 26.2 %collective-permute-start.27 = (bf16[256,1024]{1,0:T(8,128)(2,1)}, bf16[256,1024]{1,0:T(8,128)(2,1)}, u32[]{:S(2)}, u32[]{:S(2)}) collective-permute-start(bf16[256,1024]{1,0:T(8,128)(2,1)} %add_convert_fusion.2), channel_id=1, source_target_pairs={{0,2},{1,3},{2,6},{3,7},{6,10},{7,11},{10,14},{11,15},{14,12},{15,... | collective-permute-start | bytes 1572872 | tf_op jit(solution)/shard_map/ppermute | solution.py:81
  331.9 26.9 %collective-permute-start.83 = (bf16[64,1024]{1,0:T(8,128)(2,1)S(1)}, bf16[64,1024]{1,0:T(8,128)(2,1)}, u32[]{:S(2)}, u32[]{:S(2)}) collective-permute-start(bf16[64,1024]{1,0:T(8,128)(2,1)S(1)} %add_convert_fusion.46.refs_0_), channel_id=1, source_target_pairs={{0,1},{1,0},{2,3},{3,2},{4,5},{5,4},{6,7},{7,6},{8,9},{9,8},{10,11... | collective-permute-start | bytes 393224 | tf_op jit(solution)/shard_map/ppermute | solution.py:87
  337.2 21.7 %collective-permute-start.84 = (bf16[64,1024]{1,0:T(8,128)(2,1)}, bf16[64,1024]{1,0:T(8,128)(2,1)}, u32[]{:S(2)}, u32[]{:S(2)}) collective-permute-start(bf16[64,1024]{1,0:T(8,128)(2,1)} %collective-permute-done.75.refs_1_), channel_id=1, source_target_pairs={{0,1},{1,0},{2,3},{3,2},{4,5},{5,4},{6,7},{7,6},{8,9},{9,8},{10,11... | collective-permute-start | bytes 393224 | tf_op jit(solution)/shard_map/ppermute | solution.py:87
  337.2 22.2 %collective-permute-start.85 = (bf16[64,1024]{1,0:T(8,128)(2,1)}, bf16[64,1024]{1,0:T(8,128)(2,1)}, u32[]{:S(2)}, u32[]{:S(2)}) collective-permute-start(bf16[64,1024]{1,0:T(8,128)(2,1)} %collective-permute-done.76.refs_2_), channel_id=1, source_target_pairs={{0,1},{1,0},{2,3},{3,2},{4,5},{5,4},{6,7},{7,6},{8,9},{9,8},{10,11... | collective-permute-start | bytes 393224 | tf_op jit(solution)/shard_map/ppermute | solution.py:87
  373.1 92.9 %collective-permute-start.133 = (bf16[96,1024]{1,0:T(8,128)(2,1)S(1)}, bf16[96,1024]{1,0:T(8,128)(2,1)S(1)}, u32[]{:S(2)}, u32[]{:S(2)}) collective-permute-start(bf16[96,1024]{1,0:T(8,128)(2,1)S(1)} %copy-done.20), channel_id=1, source_target_pairs={{0,1},{1,0},{2,3},{3,2},{4,5},{5,4},{6,7},{7,6},{8,9},{9,8},{10,11... | collective-permute-start | bytes 589832 | tf_op jit(solution)/shard_map/ppermute | solution.py:87
  381.2 88.0 %collective-permute-start.134 = (bf16[96,1024]{1,0:T(8,128)(2,1)}, bf16[96,1024]{1,0:T(8,128)(2,1)S(1)}, u32[]{:S(2)}, u32[]{:S(2)}) collective-permute-start(bf16[96,1024]{1,0:T(8,128)(2,1)} %collective-permute-done.125.refs_1_), channel_id=1, source_target_pairs={{0,1},{1,0},{2,3},{3,2},{4,5},{5,4},{6,7},{7,6},{8,9},{9,8},{10,11... | collective-permute-start | bytes 589832 | tf_op jit(solution)/shard_map/ppermute | solution.py:87
  381.7 20.8 %collective-permute-start.41 = (bf16[512,2048]{1,0:T(8,128)(2,1)S(1)}, bf16[512,2048]{1,0:T(8,128)(2,1)S(1)}, u32[]{:S(2)}, u32[]{:S(2)}) collective-permute-start(bf16[512,2048]{1,0:T(8,128)(2,1)S(1)} %copy-done.59), channel_id=1, source_target_pairs={{0,1},{1,0},{2,3},{3,2},{4,5},{5,4},{6,7},{7,6},{8,9},{9,8},{10,11... | collective-permute-start | bytes 6291464 | tf_op jit(solution)/shard_map/ppermute | solution.py:87
  399.0 55.7 %collective-permute-start.37 = (f32[18,128]{1,0:T(8,128)S(1)}, f32[18,128]{1,0:T(8,128)S(1)}, u32[]{:S(2)}, u32[]{:S(2)}) collective-permute-start(f32[18,128]{1,0:T(8,128)S(1)} %fusion.32), channel_id=1, source_target_pairs={{0,1},{1,0},{2,3},{3,2},{4,5},{5,4},{6,7},{7,6},{8,9},{9,8},{10,11... | collective-permute-start | bytes 27656 | tf_op jit(solution)/shard_map/ppermute | solution.py:183
  402.5 33.0 %collective-permute-start.95 = (bf16[64,3072]{1,0:T(8,128)(2,1)S(1)}, bf16[64,3072]{1,0:T(8,128)(2,1)S(1)}, u32[]{:S(2)}, u32[]{:S(2)}) collective-permute-start(bf16[64,3072]{1,0:T(8,128)(2,1)S(1)} %get-tuple-element.91), channel_id=1, source_target_pairs={{0,2},{1,3},{2,6},{3,7},{6,10},{7,11},{10,14},{11,15},{14,12},{15,... | collective-permute-start | bytes 1179656 | tf_op jit(solution)/shard_map/ppermute | solution.py:81
  529.5 21.0 %collective-permute-start.55 = (bf16[64,2048]{1,0:T(8,128)(2,1)S(1)}, bf16[64,2048]{1,0:T(8,128)(2,1)S(1)}, u32[]{:S(2)}, u32[]{:S(2)}) collective-permute-start(bf16[64,2048]{1,0:T(8,128)(2,1)S(1)} %collective-permute-done.53.refs_4_), channel_id=1, source_target_pairs={{2,0},{3,1},{6,2},{7,3},{10,6},{11,7},{14,10},{15,11},{12,14},{13,... | collective-permute-start | bytes 786440 | tf_op jit(solution)/shard_map/ppermute | solution.py:84
  530.5 20.4 %collective-permute-start.56 = (bf16[32,2048]{1,0:T(8,128)(2,1)S(1)}, bf16[32,2048]{1,0:T(8,128)(2,1)S(1)}, u32[]{:S(2)}, u32[]{:S(2)}) collective-permute-start(bf16[32,2048]{1,0:T(8,128)(2,1)S(1)} %slice.478), channel_id=1, source_target_pairs={{0,2},{1,3},{2,6},{3,7},{6,10},{7,11},{10,14},{11,15},{14,12},{15,... | collective-permute-start | bytes 393224 | tf_op jit(solution)/shard_map/ppermute | solution.py:81
  (176 other events, 2426.5 us)

commit v2 on v1

v2 whole, which is shorter than its diff:
```python
import functools
import math

import jax
import jax.numpy as jnp
from jax import lax
from jax.experimental import pallas as pl
from jax.experimental.pallas import tpu as pltpu
from jax.sharding import PartitionSpec as P

EPS = 1e-06
ROPE_BASE = 1000000.0
HEAD = 128
LOG2E = 1.4426950408889634
VMEM_LIMIT = 40 * 1024 * 1024
LIGHT = pl.CostEstimate(flops=1024, bytes_accessed=1024, transcendentals=0)
BF = jnp.bfloat16
F32 = jnp.float32


def nn(a, b):
    return lax.dot_general(a, b, (((1,), (0,)), ((), ())), preferred_element_type=F32)


def nt(a, b):
    return lax.dot_general(a, b, (((1,), (1,)), ((), ())), preferred_element_type=F32)


def tn(a, b):
    return lax.dot_general(a, b, (((0,), (0,)), ((), ())), preferred_element_type=F32)


def norm_rows(values):
    scale_rows = lax.rsqrt(jnp.mean(values * values, axis=-1, keepdims=True) + EPS)
    return (values * scale_rows, scale_rows)


def norm_back(grad_normed, normed, scale_rows):
    return scale_rows * (
        grad_normed - normed * jnp.mean(grad_normed * normed, axis=-1, keepdims=True)
    )


def tie(*values):
    return lax.optimization_barrier(values)


def waits(after):
    return list(after), [pl.BlockSpec(memory_space=pl.ANY)] * len(after)


def in_hbm(x):
    return pltpu.with_memory_space_constraint(x, pltpu.HBM)


def ring_order(chips):
    if chips % 8:
        return list(range(chips))
    rows, cols = 4, chips // 4
    if cols % 2 or cols < 4:
        path = list(range(cols))
    else:
        path = list(range(cols // 2)) + list(range(cols - 1, cols // 2 - 1, -1))
    walk = []
    for row in range(rows):
        across = range(1, cols) if row % 2 == 0 else range(cols - 1, 0, -1)
        walk += [(row, col) for col in across]
    walk = [(0, 0)] + walk + [(row, 0) for row in range(rows - 1, 0, -1)]
    return [row * cols + path[col] for row, col in walk]


class Ring:
    def __init__(self, devices):
        self.devices = devices
        self.chips = devices // 2
        order = ring_order(self.chips)
        self.order = order
        size = self.chips
        self.up = [
            (2 * order[i] + core, 2 * order[(i + 1) % size] + core)
            for i in range(size)
            for core in range(2)
        ]
        self.down = [(b, a) for a, b in self.up]
        self.swap = [(i, i ^ 1) for i in range(devices)]
        place = [0] * size
        for i, chip in enumerate(order):
            place[chip] = i
        index = lax.axis_index("cp")
        self.core = index % 2
        self.here = jnp.asarray(place, jnp.int32)[index // 2]
        self.half = size // 2
        table = [
            [order[(place[chip] + i) % size] for i in range(size)] + [core]
            for chip in range(size)
            for core in range(2)
        ]
        self.table = lax.dynamic_index_in_dim(
            jnp.asarray(table, jnp.int32), index, 0, keepdims=False
        )

    def send_up(self, x):
        return lax.ppermute(x, "cp", self.up)

    def send_down(self, x):
        return lax.ppermute(x, "cp", self.down)

    def sibling(self, x):
        return lax.ppermute(x, "cp", self.swap)

    def shard_at(self, table, offset, other=False):
        core = table[self.chips]
        return 2 * table[offset % self.chips] + (1 - core if other else core)


class Gradients:
    def __init__(self, ring, pack_rows, pack_columns, pieces):
        self.ring = ring
        self.shape = (pack_rows, pack_columns)
        self.pieces = pieces
        self.mine = [None] * len(pieces)
        self.other = [None] * len(pieces)

    def put(self, index, array):
        ring = self.ring
        groups, rows, columns = self.pieces[index][0]
        self.mine[index] = array
        halves = array.reshape(groups, ring.chips, 2, rows, columns)
        other = lax.dynamic_index_in_dim(halves, 1 - ring.core, 2, keepdims=False)
        self.other[index] = ring.sibling(other.reshape(groups, ring.chips * rows, columns))

    def shards(self, offsets, received, halves, after=()):
        ring, pieces = self.ring, self.pieces
        rows, columns = self.shape
        cut = columns // 2
        count, sides = len(pieces), len(offsets)
        args, specs = [], []
        for offset in offsets:
            for index, ((groups, part_rows, part_columns), _) in enumerate(pieces):
                block = (groups, part_rows, part_columns)
                args += [in_hbm(self.mine[index]), in_hbm(self.other[index])]
                specs += [
                    pl.BlockSpec(block, lambda i, t, at=offset: (0, ring.shard_at(t, at), 0)),
                    pl.BlockSpec(block, lambda i, t, at=offset: (0, t[at % ring.chips], 0)),
                ]
        args += received
        specs += [pl.BlockSpec(x.shape, lambda i, t: (0, 0)) for x in received]
        more_args, more_specs = waits(after)
        total_args = len(args) + len(more_args)

        def kernel(table_ref, *refs):
            outs = refs[total_args:]
            outs[-1][...] = jnp.zeros_like(outs[-1])
            gained = refs[2 * count * sides : len(args)]
            for side in range(sides):
                for index, (_, places) in enumerate(pieces):
                    mine = refs[2 * (count * side + index)]
                    other = refs[2 * (count * side + index) + 1]
                    for group, (row, column) in enumerate(places):
                        total = mine[group].astype(F32) + other[group].astype(F32)
                        high, wide = total.shape
                        here, end = slice(row, row + high), column + wide
                        if halves == "send":
                            for out, start in zip(outs, (0, cut)):
                                left, right = max(column, start), min(end, start + cut)
                                if left < right:
                                    out[here, left - start : right - start] = total[
                                        :, left - column : right - column
                                    ].astype(BF)
                        elif halves == "sum":
                            for more in gained:
                                total = total + more[here, column:end].astype(F32)
                            outs[0][here, column:end] = total.astype(BF)
                        elif halves == "add":
                            start, stop = side * cut, side * cut + cut
                            for left, right, more in (
                                (column, min(end, start), False),
                                (max(column, start), min(end, stop), True),
                                (max(column, stop), end, False),
                            ):
                                if left < right:
                                    part = total[:, left - column : right - column]
                                    if more:
                                        part = part + gained[side][
                                            here, left - start : right - start
                                        ].astype(F32)
                                    outs[side][here, left:right] = part.astype(BF)
                        else:
                            total = total + gained[side][here, column:end].astype(F32)
                            outs[side][here, column:end] = total.astype(BF)

        outs = {"send": [cut, cut], "sum": [columns]}.get(halves, [columns, columns])
        return pl.pallas_call(
            kernel,
            out_shape=[jax.ShapeDtypeStruct((rows, wide), BF) for wide in outs]
            + [jax.ShapeDtypeStruct((8, 128), F32)],
            grid_spec=pltpu.PrefetchScalarGridSpec(
                num_scalar_prefetch=1,
                grid=(1,),
                in_specs=specs + more_specs,
                out_specs=[pl.BlockSpec((rows, wide), lambda i, t: (0, 0)) for wide in outs]
                + [pl.BlockSpec((8, 128), lambda i, t: (0, 0))],
            ),
            compiler_params=pltpu.CompilerParams(vmem_limit_bytes=VMEM_LIMIT),
        cost_estimate=LIGHT,
        )(ring.table, *args, *more_args)

    def scatter(self, after=()):
        ring = self.ring
        up, down, token = self.shards([ring.half], [], "send", after)
        for step in range(ring.half - 1, -1, -1):
            (up, down), after = yield (ring.send_up(up), ring.send_down(down)), token
            if step:
                kind = "add" if step == ring.half - 1 else ""
                up, down, token = self.shards([step, -step], [up, down], kind, after)
        yield self.shards([0], [up, down], "sum", after)

    def gather(self, own):
        ring = self.ring
        cut = own.shape[1] // 2
        up = down = own
        ready = [(0, own)]
        for step in range(1, ring.half):
            up, down = yield (ring.send_up(up), ring.send_down(down)), ready
            ready = [(-step, up), (step, down)]
        left, right = yield (ring.send_up(up[:, :cut]), ring.send_down(down[:, cut:])), ready
        yield None, [(ring.half, jnp.concatenate([left, right], axis=1))]

    def unpack(self, ready, outs, before, after=()):
        ring, pieces = self.ring, self.pieces
        rows, columns = self.shape
        args = [part for _, part, _ in ready]
        count = len(args)
        places_of = [(offset, other) for offset, _, other in ready]

        def kernel(table_ref, *refs):
            step = pl.program_id(0)
            results = refs[-len(outs) :]
            for i in range(count):

                @pl.when(step == i)
                def _(i=i):
                    for out, (index, first, wide) in zip(results, outs):
                        (_, high, _), places = pieces[index]
                        for group, (row, column) in enumerate(places):
                            start = column + first
                            out[group] = refs[i][row : row + high, start : start + wide].astype(F32)

        def place(i, table):
            where = ring.shard_at(table, *places_of[0])
            for j in range(1, count):
                where = jnp.where(i == j, ring.shard_at(table, *places_of[j]), where)
            return (0, where, 0)

        shapes, out_specs = [], []
        for index, _, wide in outs:
            groups, high, _ = pieces[index][0]
            shapes.append(jax.ShapeDtypeStruct((groups, ring.devices * high, wide), F32))
            out_specs.append(pl.BlockSpec((groups, high, wide), place))
        specs = [pl.BlockSpec((rows, columns), lambda i, t: (0, 0))] * count
        aliases = {}
        if before is not None:
            specs += [pl.BlockSpec(memory_space=pl.ANY)] * len(outs)
            aliases = {1 + count + i: i for i in range(len(outs))}
            args += before
        more_args, more_specs = waits(after)
        args += more_args
        specs += more_specs
        return list(
            pl.pallas_call(
                kernel,
                out_shape=shapes,
                grid_spec=pltpu.PrefetchScalarGridSpec(
                    num_scalar_prefetch=1, grid=(count,), in_specs=specs, out_specs=out_specs
                ),
                input_output_aliases=aliases,
                compiler_params=pltpu.CompilerParams(vmem_limit_bytes=VMEM_LIMIT),
        cost_estimate=LIGHT,
            )(ring.table, *args)
        )


def pair_add(own, received, half, after=()):
    more_args, more_specs = waits(after)

    def kernel(*refs):
        refs, outs = refs[:4], refs[4 + len(more_args) :]
        outs[-1][...] = jnp.zeros_like(outs[-1])
        for side in range(2):
            mine, got, out = refs[side], refs[2 + side], outs[side]
            if half:
                rows = got.shape[0]
                here = slice(side * rows, (side + 1) * rows)
                rest = slice((1 - side) * rows, (2 - side) * rows)
                out[here] = (mine[here].astype(F32) + got[...].astype(F32)).astype(BF)
                out[rest] = mine[rest]
            else:
                out[...] = (mine[...].astype(F32) + got[...].astype(F32)).astype(BF)

    shape = jax.ShapeDtypeStruct(own[0].shape, BF)
    return pl.pallas_call(
        kernel,
        out_shape=[shape, shape, jax.ShapeDtypeStruct((8, 128), F32)],
        in_specs=[pl.BlockSpec(memory_space=pltpu.VMEM)] * 4 + more_specs,
        compiler_params=pltpu.CompilerParams(vmem_limit_bytes=VMEM_LIMIT),
        cost_estimate=LIGHT,
    )(*own, *received, *more_args)


class SmallSum:
    def __init__(self, devices, x):
        self.devices, self.bit, self.total = devices, 1, x
        self.under_way = []
        self.send()

    def send(self):
        pairs = [(i, i ^ self.bit) for i in range(self.devices)]
        self.under_way = [lax.ppermute(self.total, "cp", pairs)] if self.bit < self.devices else []
        self.bit *= 2

    def came(self, arrived):
        if arrived:
            self.total = self.total + arrived[0]
            self.send()


def partner(x):
    return lax.ppermute(x, "tp", [(0, 1), (1, 0)])


def both(mine, other):
    return mine.astype(F32) + other.astype(F32)


def turn(values, cosine, sine):
    return values * cosine + pltpu.roll(values, values.shape[-1] // 2, 1) * sine


def turn_back(values, cosine, sine):
    return values * cosine - pltpu.roll(values, values.shape[-1] // 2, 1) * sine


def lower_first(order, table):
    device = 2 * table[0] + table[table.shape[0] - 1]
    return order[2 * device] < order[2 * device + 1]


def key_value_kernel(
    order, table, residual, gain, key_weight, value_weight, key_gain, cosine, sine,
    residual_out, normed_out, raw_out, cosine_out, sine_out, keep, give,
):
    span = residual.shape[0] // 2
    start = jnp.where(lower_first(order, table), 0, span)

    def canonical(ref):
        return jnp.concatenate(
            [
                ref[pl.ds(pl.multiple_of(start, span), span)],
                ref[pl.ds(pl.multiple_of(span - start, span), span)],
            ],
            axis=0,
        )

    rows = canonical(residual)
    residual_out[...] = rows
    unit, _ = norm_rows(rows.astype(F32))
    normed = (unit * gain[...]).astype(BF)
    normed_out[...] = normed
    cosine, sine = canonical(cosine), canonical(sine)
    cosine_out[...], sine_out[...] = cosine, sine
    width = key_gain.shape[1]
    raw = nn(normed, key_weight[...])
    raw_out[...] = raw
    values = nn(normed, value_weight[...]).astype(BF)
    parts = []
    for group in range(raw.shape[1] // width):
        here = slice(group * width, (group + 1) * width)
        key_unit, _ = norm_rows(raw[:, here])
        parts.append(turn(key_unit * key_gain[...], cosine, sine).astype(BF))
        parts.append(values[:, here])
    each = len(parts) // 2
    first = table[table.shape[0] - 1] == 0
    for i in range(each):
        here = slice(i * width, (i + 1) * width)
        keep[:, here] = jnp.where(first, parts[i], parts[each + i])
        give[:, here] = jnp.where(first, parts[each + i], parts[i])


def query_kernel(table, normed, weight, gain, cosine, sine, raw_out, keep, give):
    width = gain.shape[1]
    raw = nn(normed[...], weight[...])
    raw_out[...] = raw
    parts = []
    for head in range(raw.shape[1] // width):
        here = slice(head * width, (head + 1) * width)
        unit, _ = norm_rows(raw[:, here])
        parts.append(turn(unit * gain[...], cosine[...], sine[...]).astype(BF))
    each = len(parts) // 2
    first = table[table.shape[0] - 1] == 0
    for i in range(each):
        here = slice(i * width, (i + 1) * width)
        keep[:, here] = jnp.where(first, parts[i], parts[each + i])
        give[:, here] = jnp.where(first, parts[each + i], parts[i])


def query_back_kernel(table, kept, given, raw, gain, cosine, sine, low_out, gain_out):
    width = gain.shape[1]
    total = jnp.zeros((8, width), F32)
    first = table[table.shape[0] - 1] == 0
    heads = raw.shape[1] // width
    each = heads // 2
    for head in range(heads):
        here = slice(head * width, (head + 1) * width)
        at = slice(head % each * width, (head % each + 1) * width)
        grad = jnp.where(first == (head < each), kept[:, at], given[:, at])
        unit, scale_rows = norm_rows(raw[:, here])
        turned = turn_back(grad, cosine[...], sine[...])
        total = total + jnp.sum((turned * unit).reshape(-1, 8, width), axis=0)
        low_out[:, here] = norm_back(turned * gain[...], unit, scale_rows).astype(BF)
    gain_out[...] = total


def key_value_back_kernel(table, kept, given, raw, gain, cosine, sine, low_out, gain_out):
    width = gain.shape[1]
    groups = raw.shape[1] // width
    each = groups // 2
    total = jnp.zeros((8, width), F32)
    first = table[table.shape[0] - 1] == 0

    def part(group, which):
        place = 2 * (group % each) + which
        here = slice(place * width, (place + 1) * width)
        return jnp.where(
            first == (group < each), kept[:, here].astype(F32), given[:, here].astype(F32)
        )

    for group in range(groups):
        here = slice(group * width, (group + 1) * width)
        unit, scale_rows = norm_rows(raw[:, here])
        turned = turn_back(part(group, 0), cosine[...], sine[...])
        total = total + jnp.sum((turned * unit).reshape(-1, 8, width), axis=0)
        low_out[:, here] = norm_back(turned * gain[...], unit, scale_rows).astype(BF)
        low_out[:, (groups + group) * width : (groups + group + 1) * width] = part(
            group, 1
        ).astype(BF)
    gain_out[...] = total


def whole_call(kernel, scalars, outs, *args, after=()):
    more_args, more_specs = waits(after)
    taken = len(scalars) + len(args)

    def run(*refs):
        kernel(*refs[:taken], *refs[taken + len(more_args) :])

    return pl.pallas_call(
        run,
        out_shape=[jax.ShapeDtypeStruct(shape, dtype) for shape, dtype in outs],
        in_specs=[pl.BlockSpec(memory_space=pltpu.SMEM)] * len(scalars)
        + [pl.BlockSpec(memory_space=pltpu.VMEM)] * len(args)
        + more_specs,
        compiler_params=pltpu.CompilerParams(vmem_limit_bytes=VMEM_LIMIT),
        cost_estimate=LIGHT,
    )(*scalars, *args, *more_args)


def stacked(ref, start, span, width):
    rows = pl.ds(start, span)
    return jnp.concatenate([ref[rows, :width], ref[rows, width:]], axis=0)


def causal(span, transposed):
    shape = (span, 2 * span) if transposed else (2 * span, span)
    key = lax.broadcasted_iota(jnp.int32, shape, 0 if transposed else 1)
    row = lax.broadcasted_iota(jnp.int32, shape, 1 if transposed else 0)
    return key <= row % span


def side_met(order, table, pair, offset, other):
    last = table.shape[0] - 1
    core = table[last]

    def lower(device):
        return jnp.minimum(order[2 * device], order[2 * device + 1])

    mine = lower(2 * table[0] + (1 - core if pair else core))
    theirs = lower(2 * table[offset % last] + (1 - core if other else core))
    return jnp.where(theirs < mine, 0, 1)


def forward_kernel(places, own, last, span, width, order, table, *refs):
    count = len(places)
    queries, blocks, refs = refs[:2], refs[2 : 2 + count], refs[2 + count :]
    scale = LOG2E / math.sqrt(width)
    if own:
        before, outs = None, refs
    else:
        before, outs = refs[0], refs[1:]
    accum = outs[-1]
    ones = jnp.ones((span, width), BF)

    def weighted(rows, keys, values, allowed=None):
        scores = nt(rows, keys)
        probs = jnp.exp2(scores * scale)
        if allowed is not None:
            probs = jnp.where(allowed, probs, 0.0)
        return nn(probs.astype(BF), values)

    def extended(block, start):
        return jnp.concatenate([block[pl.ds(start, span), width:], ones], axis=1)

    keys = jnp.concatenate([block[:span, :width] for block in blocks], axis=0)
    values = jnp.concatenate([extended(block, 0) for block in blocks], axis=0)
    rows = jnp.concatenate([stacked(query, span, span, width) for query in queries], axis=0)
    high = weighted(rows, keys, values)
    for pair in range(2):
        part = high[pair * 2 * span : (pair + 1) * 2 * span]
        if own:
            allowed = causal(span, False)
            for side in range(2):
                block, start = blocks[pair], side * span
                met = weighted(
                    stacked(queries[pair], start, span, width),
                    block[start : start + span, :width],
                    extended(block, start),
                    allowed,
                )
                accum[0, pair, side] = met + part if side else met
        else:
            accum[0, pair, 0] = before[0, pair, 0]
            accum[0, pair, 1] = before[0, pair, 1] + part
    for i, (offset, other) in enumerate(places):
        for pair in range(2):
            if own and i == pair:
                continue
            side = side_met(order, table, pair, offset, other)
            start = pl.multiple_of(side * span, span)
            accum[0, pair, side] += weighted(
                stacked(queries[pair], start, span, width),
                blocks[i][pl.ds(start, span), :width],
                extended(blocks[i], start),
            )
    if last:
        wides, lows, logs = outs[0:2], outs[2:4], outs[4]
        for pair in range(2):
            for side in range(2):
                rows = slice(side * span, (side + 1) * span)
                whole = accum[0, pair, side]
                mass = whole[:, width:]
                out = whole[:, :width] / mass
                for head in range(2):
                    part = out[head * span : (head + 1) * span]
                    columns = slice(head * width, (head + 1) * width)
                    wides[pair][rows, columns] = part
                    lows[pair][rows, columns] = part.astype(BF)
                logs[0, pair, side] = jnp.log2(mass).T[:8]


def attention_forward(scalars, queries, blocks, places, before, own, last, after=()):
    rows, columns = queries[0].shape
    span, width = rows // 2, HEAD
    groups = columns // (2 * width)
    tile = pl.BlockSpec((rows, 2 * width), lambda g: (0, g))
    accum_block = (1, 2, 2, 2 * span, 2 * width)
    accum_spec = pl.BlockSpec(accum_block, lambda g: (g, 0, 0, 0, 0))
    args = [*scalars, *queries, *blocks]
    specs = [pl.BlockSpec(memory_space=pltpu.SMEM)] * 2 + [tile] * (2 + len(blocks))
    if not own:
        args.append(before)
        specs.append(accum_spec)
    taken = len(args)
    more_args, more_specs = waits(after)
    scratch = []
    if last:
        wide, low = jax.ShapeDtypeStruct((rows, columns), F32), jax.ShapeDtypeStruct((rows, columns), BF)
        outs = [wide, wide, low, low, jax.ShapeDtypeStruct((groups, 2, 2, 8, 2 * span), F32)]
        out_specs = [tile] * 4 + [pl.BlockSpec((1, 2, 2, 8, 2 * span), lambda g: (g, 0, 0, 0, 0))]
        scratch = [pltpu.VMEM(accum_block, F32)]
    else:
        outs = [jax.ShapeDtypeStruct((groups, *accum_block[1:]), F32)]
        out_specs = [accum_spec]

    def kernel(*refs):
        refs = refs[:taken] + refs[taken + len(more_args) :]
        forward_kernel(places, own, last, span, width, *refs)

    return pl.pallas_call(
        kernel,
        out_shape=outs,
        grid=(groups,),
        in_specs=specs + more_specs,
        out_specs=out_specs,
        scratch_shapes=scratch,
        compiler_params=pltpu.CompilerParams(vmem_limit_bytes=VMEM_LIMIT),
        cost_estimate=LIGHT,
    )(*args, *more_args)


def delta_kernel(grads, outs, delta):
    for pair in range(2):
        grad, out = grads[pair], outs[pair]
        width, span = grad.shape[1] // 2, grad.shape[0] // 2
        for side in range(2):
            rows = slice(side * span, (side + 1) * span)
            product = grad[rows, :].astype(F32) * out[rows, :]
            stack = jnp.concatenate([product[:, :width], product[:, width:]], axis=0)
            total = jnp.sum(stack.T, axis=0, keepdims=True)
            delta[0, pair, side] = jnp.broadcast_to(total, (8, 2 * span))


def attention_delta(grads, outs, after=()):
    rows, columns = grads[0].shape
    width, span = HEAD, rows // 2
    groups = columns // (2 * width)
    tile = pl.BlockSpec((rows, 2 * width), lambda g: (0, g))
    more_args, more_specs = waits(after)

    def kernel(*refs):
        delta_kernel(refs[:2], refs[2:4], refs[-1])

    return pl.pallas_call(
        kernel,
        out_shape=jax.ShapeDtypeStruct((groups, 2, 2, 8, 2 * span), F32),
        grid=(groups,),
        in_specs=[tile] * 4 + more_specs,
        out_specs=pl.BlockSpec((1, 2, 2, 8, 2 * span), lambda g: (g, 0, 0, 0, 0)),
        compiler_params=pltpu.CompilerParams(vmem_limit_bytes=VMEM_LIMIT),
        cost_estimate=LIGHT,
    )(*grads, *outs, *more_args)


def backward_kernel(places, own, first, last, split, span, width, order, table, *refs):
    count = len(places)
    queries, grads, (logs, delta), refs = refs[:2], refs[2:4], refs[4:6], refs[6:]
    blocks, refs = refs[:count], refs[count:]
    if not first:
        before, refs = refs[0], refs[1:]
    outs = refs[: count if split else count // 2]
    refs = refs[len(outs) :]
    if last:
        query_outs, accum = refs[:2], refs[2]
    else:
        accum = refs[0]
    scale = LOG2E / math.sqrt(width)
    factor = 1.0 / math.sqrt(width)

    def products(rows, row_grads, log, mean, keys, values, allowed=None):
        probs = jnp.exp2(nt(keys, rows) * scale - log)
        if allowed is not None:
            probs = jnp.where(allowed, probs, 0.0)
        prob_grad = nt(values, row_grads)
        score_grad = (probs * (prob_grad - mean)).astype(BF)
        return nn(score_grad, rows), nn(probs.astype(BF), row_grads), tn(keys, score_grad)

    def of_pair(pair, side, start, keys, values, allowed=None):
        return products(
            stacked(queries[pair], start, span, width),
            stacked(grads[pair], start, span, width),
            logs[0, pair, side, :1],
            delta[0, pair, side, :1],
            keys,
            values,
            allowed,
        )

    low_keys, low_values, high_query = products(
        jnp.concatenate([stacked(query, span, span, width) for query in queries], axis=0),
        jnp.concatenate([stacked(grad, span, span, width) for grad in grads], axis=0),
        jnp.concatenate([logs[0, pair, 1, :1] for pair in range(2)], axis=1),
        jnp.concatenate([delta[0, pair, 1, :1] for pair in range(2)], axis=1),
        jnp.concatenate([block[:span, :width] for block in blocks], axis=0),
        jnp.concatenate([block[:span, width:] for block in blocks], axis=0),
    )
    for pair in range(2):
        part = high_query[:, pair * 2 * span : (pair + 1) * 2 * span]
        if first:
            accum[0, pair, 0] = jnp.zeros_like(part)
            accum[0, pair, 1] = part
        else:
            accum[0, pair, 0] = before[0, pair, 0]
            accum[0, pair, 1] = before[0, pair, 1] + part
    for i, (offset, other) in enumerate(places):
        here = slice(i * span, (i + 1) * span)
        block = blocks[i]
        key_sums, value_sums = [low_keys[here], 0.0], [low_values[here], 0.0]
        for pair in range(2):
            if own and i == pair:
                allowed = causal(span, True)
                for side in range(2):
                    rows = slice(side * span, (side + 1) * span)
                    key_part, value_part, query_part = of_pair(
                        pair, side, side * span, block[rows, :width], block[rows, width:], allowed
                    )
                    accum[0, pair, side] += query_part
                    key_sums[side] = key_sums[side] + key_part
                    value_sums[side] = value_sums[side] + value_part
                continue
            side = side_met(order, table, pair, offset, other)
            start = pl.multiple_of(side * span, span)
            rows = pl.ds(start, span)
            key_part, value_part, query_part = of_pair(
                pair, side, start, block[rows, :width], block[rows, width:]
            )
            accum[0, pair, side] += query_part
            low = side == 0
            key_sums[0] = key_sums[0] + jnp.where(low, key_part, 0.0)
            value_sums[0] = value_sums[0] + jnp.where(low, value_part, 0.0)
            key_sums[1] = key_sums[1] + jnp.where(low, 0.0, key_part)
            value_sums[1] = value_sums[1] + jnp.where(low, 0.0, value_part)
        out = outs[i] if split else outs[i // 2]
        base = 0 if split else i % 2 * 2 * span
        for side in range(2):
            rows = slice(base + side * span, base + (side + 1) * span)
            out[rows, :width] = (key_sums[side] * factor).astype(BF)
            out[rows, width:] = value_sums[side].astype(BF)
    if last:
        for pair in range(2):
            for side in range(2):
                part = accum[0, pair, side].T * factor
                rows = slice(side * span, (side + 1) * span)
                query_outs[pair][rows, :width] = part[:span]
                query_outs[pair][rows, width:] = part[span:]


def attention_backward(
    scalars, queries, grads, logs, delta, blocks, places, before, own, last, split, after=()
):
    rows, columns = queries[0].shape
    span, width = rows // 2, HEAD
    groups = columns // (2 * width)
    count = len(blocks)
    first = before is None
    tile = pl.BlockSpec((rows, 2 * width), lambda g: (0, g))
    stat = pl.BlockSpec((1, 2, 2, 8, 2 * span), lambda g: (g, 0, 0, 0, 0))
    accum_block = (1, 2, 2, width, 2 * span)
    accum_spec = pl.BlockSpec(accum_block, lambda g: (g, 0, 0, 0, 0))
    args = [*scalars, *queries, *grads, logs, delta, *blocks]
    specs = [pl.BlockSpec(memory_space=pltpu.SMEM)] * 2 + [tile] * 4 + [stat] * 2 + [tile] * count
    if not first:
        args.append(before)
        specs.append(accum_spec)
    taken = len(args)
    more_args, more_specs = waits(after)
    if split:
        outs = [jax.ShapeDtypeStruct((rows, columns), BF)] * count
        out_specs = [tile] * count
    else:
        outs = [jax.ShapeDtypeStruct((2 * rows, columns), BF)] * (count // 2)
        out_specs = [pl.BlockSpec((2 * rows, 2 * width), lambda g: (0, g))] * (count // 2)
    scratch = []
    if last:
        outs += [jax.ShapeDtypeStruct((rows, columns), F32)] * 2
        out_specs += [tile] * 2
        scratch = [pltpu.VMEM(accum_block, F32)]
    else:
        outs.append(jax.ShapeDtypeStruct((groups, *accum_block[1:]), F32))
        out_specs.append(accum_spec)

    def kernel(*refs):
        refs = refs[:taken] + refs[taken + len(more_args) :]
        backward_kernel(places, own, first, last, split, span, width, *refs)

    return pl.pallas_call(
        kernel,
        out_shape=outs,
        grid=(groups,),
        in_specs=specs + more_specs,
        out_specs=out_specs,
        scratch_shapes=scratch,
        compiler_params=pltpu.CompilerParams(vmem_limit_bytes=VMEM_LIMIT),
        cost_estimate=LIGHT,
    )(*args, *more_args)


def body(
    devices,
    residual,
    cotangent,
    span_order,
    positions,
    attn_gain,
    query_weight,
    key_weight,
    value_weight,
    query_gain,
    key_gain,
    out_weight,
    mlp_gain,
    gate_weight,
    up_weight,
    down_weight,
):
    ring = Ring(devices)
    rows, model = residual.shape
    head_dim = query_gain.shape[0]
    span = rows // 2
    index = lax.axis_index("cp")
    scalars = [span_order, ring.table]
    table = [ring.table]
    ordered = lax.dynamic_slice_in_dim(span_order, 2 * index, 2)
    in_order = ordered[0] < ordered[1]

    def canonical(x):
        return jnp.where(in_order, x, jnp.roll(x, span, axis=0))

    half = head_dim // 2
    freq = ROPE_BASE ** (-(jnp.arange(half, dtype=F32) * 2.0) / head_dim)
    angle = positions.astype(F32)[:, None] * freq[None, :]
    cosine, sine = jnp.cos(angle), jnp.sin(angle)
    cosine = jnp.concatenate([cosine, cosine], axis=1)
    sine = jnp.concatenate([-sine, sine], axis=1)

    query_gain_row = query_gain.reshape(1, -1)
    key_gain_row = key_gain.reshape(1, -1)
    key_columns = key_weight.shape[1]
    query_columns = query_weight.shape[1]
    each = query_columns // 2

    residual, normed_low, keys_raw, cosine, sine, keep, give = whole_call(
        key_value_kernel,
        scalars,
        [((rows, model), BF), ((rows, model), BF), ((rows, key_columns), F32)]
        + [((rows, head_dim), F32)] * 2
        + [((rows, key_columns), BF)] * 2,
        residual, attn_gain.reshape(1, -1), key_weight, value_weight, key_gain_row, cosine, sine,
    )

    parts = [keep, ring.sibling(give)]
    ways = [(ring.send_up(part), ring.send_down(part)) for part in parts]
    queries_raw, query_keep, query_give = whole_call(
        query_kernel,
        table,
        [((rows, query_columns), F32)] + [((rows, each), BF)] * 2,
        normed_low, query_weight, query_gain_row, cosine, sine,
    )
    queries = [query_keep, ring.sibling(query_give)]

    def places_of(offsets):
        return [(offset, other) for offset in offsets for other in (False, True)]

    cotangent = canonical(cotangent)
    hidden_grad = nt(cotangent, down_weight)
    out_keep = lax.dynamic_slice_in_dim(out_weight, ring.core * each, each)
    out_give = lax.dynamic_slice_in_dim(out_weight, (1 - ring.core) * each, each)
    steps = ring.half
    calls = {0: ([0], parts)}
    state = None
    for step in range(1, steps):
        come = []
        for which in range(2):
            up, down = ways[which]
            if step > 1:
                up, down, state = tie(up, down, state)
            come.append((up, down))
            if step < steps - 1:
                ways[which] = ring.send_up(up), ring.send_down(down)
            else:
                ways[which] = ring.send_down(down) if which else ring.send_up(up)
        if step == 1:
            (state,) = attention_forward(
                scalars, queries, parts, places_of([0]), None, True, False, after=come[0]
            )
            state, hidden_grad, out_keep, out_give = tie(state, hidden_grad, out_keep, out_give)
        blocks = [come[0][0], come[1][0], come[0][1], come[1][1]]
        calls[step] = ([-step, step], blocks)
        (state,) = attention_forward(
            scalars, queries, blocks, places_of([-step, step]), state, False, False
        )
    *ways, state = tie(*ways, state)
    calls[steps] = ([steps], ways)
    *attended, low_keep, low_give, logs = attention_forward(
        scalars, queries, ways, places_of([steps]), state, False, True
    )
    low_other = ring.sibling(low_give)
    mixed_part = (nn(low_keep, out_keep) + nn(low_other, out_give)).astype(BF)

    residual_wide = residual.astype(F32)
    mixed = residual_wide + both(mixed_part, partner(mixed_part))
    normed_two, scale_two = norm_rows(mixed)
    normed_two_low = (normed_two * mlp_gain).astype(BF)
    gate = nn(normed_two_low, gate_weight)
    upward = nn(normed_two_low, up_weight)
    sigmoid_gate = jax.nn.sigmoid(gate)
    activated = gate * sigmoid_gate
    hidden_low = (activated * upward).astype(BF)
    gate_grad_low = (
        hidden_grad * upward * sigmoid_gate * (1.0 + gate * (1.0 - sigmoid_gate))
    ).astype(BF)
    up_grad_low = (hidden_grad * activated).astype(BF)
    normed_two_part = (nt(gate_grad_low, gate_weight) + nt(up_grad_low, up_weight)).astype(BF)
    normed_two_part, normed_two_low, hidden_low = tie(normed_two_part, normed_two_low, hidden_low)
    normed_two_other = partner(normed_two_part)

    units = gate_weight.shape[1]
    thirds = 2 * units // model
    gate_rows, down_rows = model // devices, units // thirds // devices
    wide = Gradients(
        ring,
        gate_rows + down_rows,
        2 * units,
        [
            ((1, gate_rows, 2 * units), [(0, 0)]),
            ((thirds, down_rows, model), [(gate_rows, i * model) for i in range(thirds)]),
        ],
    )
    both_grad_low = jnp.concatenate([gate_grad_low, up_grad_low], axis=1)
    wide.put(0, tn(normed_two_low, both_grad_low).astype(BF)[None])
    wide.put(1, tn(hidden_low, cotangent).astype(BF).reshape(thirds, -1, model))
    wide_steps = wide.scatter()
    wide_way, wide_token = next(wide_steps)
    normed_two_other, wide_token = tie(normed_two_other, wide_token)

    normed_two_grad = both(normed_two_part, normed_two_other)
    mlp_gain_term = jnp.sum(normed_two_grad * normed_two, axis=0)
    mixed_grad = cotangent.astype(F32) + norm_back(
        normed_two_grad * mlp_gain, normed_two, scale_two
    )
    mixed_grad_low = mixed_grad.astype(BF)
    grads = [
        nt(mixed_grad_low, out_keep).astype(BF),
        ring.sibling(nt(mixed_grad_low, out_give).astype(BF)),
    ]
    delta = attention_delta(grads, attended, after=[wide_token])

    def backward(step, state, after):
        offsets, blocks = calls[step]
        last = step == 0
        return attention_backward(
            scalars, queries, grads, logs, delta, blocks, places_of(offsets), state,
            last, last, last or step == steps, after,
        )

    up, down, state = backward(steps, None, [])
    token = up
    up, down = ring.send_up(up), ring.send_down(down)
    for step in range(steps - 1, 0, -1):
        back, front, state = backward(step, state, [token])
        wide_way, wide_token = wide_steps.send((wide_way, [state]))
        up, down, token = pair_add([front, back], [up, down], step == steps - 1, [wide_token])
        up, down = ring.send_up(up), ring.send_down(down)
    key_value_keep, key_value_give, grad_keep, grad_give = backward(0, state, [token])
    hidden_low, token = tie(hidden_low, token)
    layer_part = nn(hidden_low, down_weight).astype(BF)
    layer_other = partner(layer_part)
    query_grad_low, query_gain_term = whole_call(
        query_back_kernel,
        table,
        [((rows, query_columns), BF), ((8, head_dim), F32)],
        grad_keep, ring.sibling(grad_give), queries_raw, query_gain_row, cosine, sine,
    )
    wide_shard, wide_token = wide_steps.send((wide_way, [query_gain_term, token]))
    wide_outs = [(0, 0, units), (0, units, units), (1, 0, model)]
    wide_steps = wide.gather(wide_shard)
    wide_way, wide_ready = next(wide_steps)

    rows_each = model // devices
    narrow = Gradients(
        ring,
        rows_each,
        3 * model,
        [((1, rows_each, model), [(0, i * model)]) for i in range(3)],
    )
    narrow_outs = [(0, 0, model), (1, 0, model), (2, 0, key_columns), (2, key_columns, key_columns)]
    attended_low = jnp.where(
        ring.core == 0,
        jnp.concatenate([low_keep, low_other], axis=1),
        jnp.concatenate([low_other, low_keep], axis=1),
    )
    narrow.put(0, tn(attended_low, mixed_grad_low).astype(BF)[None])
    narrow.put(1, tn(normed_low, query_grad_low).astype(BF)[None])
    up, down, wide_token, layer_other, narrow.other[0], narrow.other[1] = tie(
        up, down, wide_token, layer_other, narrow.other[0], narrow.other[1]
    )
    up, down = up.astype(F32), down.astype(F32)
    key_value_give = (key_value_give.astype(F32) + up[rows:] + down[rows:]).astype(BF)
    key_value_keep = key_value_keep.astype(F32) + up[:rows] + down[:rows]
    key_value_other = ring.sibling(key_value_give)
    layer_out = canonical(mixed + both(layer_part, layer_other)).astype(BF)

    def own_ready(ready):
        return [(offset, part, False) for offset, part in ready]

    def other_ready(ready):
        return [(offset, ring.sibling(part), True) for offset, part in ready]

    wide_come = list(wide_ready)
    wide_results = wide.unpack(own_ready(wide_ready), wide_outs, None, [wide_token])
    key_value_grad, key_gain_term = whole_call(
        key_value_back_kernel,
        table,
        [((rows, 2 * key_columns), BF), ((8, head_dim), F32)],
        key_value_keep, key_value_other, keys_raw, key_gain_row, cosine, sine,
    )
    *wide_way, key_value_grad, wide_results[0] = tie(*wide_way, key_value_grad, wide_results[0])
    wide_way, wide_ready = wide_steps.send(wide_way)
    wide_come += wide_ready
    narrow.put(2, tn(normed_low, key_value_grad).astype(BF)[None])
    narrow_steps = narrow.scatter()
    narrow_way, token = next(narrow_steps)

    key_value_grad, token = tie(key_value_grad, token)
    normed_part = (
        nt(query_grad_low, query_weight)
        + nt(key_value_grad[:, :key_columns], key_weight)
        + nt(key_value_grad[:, key_columns:], value_weight)
    ).astype(BF)
    normed_other = partner(normed_part)
    gains = jnp.stack([jnp.sum(query_gain_term, axis=0), jnp.sum(key_gain_term, axis=0)])
    wide_results = wide.unpack(own_ready(wide_ready), wide_outs, wide_results, [token])

    narrow_way, token = narrow_steps.send((narrow_way, [wide_results[0]]))
    *wide_way, normed_other, token = tie(*wide_way, normed_other, token)
    wide_way, wide_ready = wide_steps.send(wide_way)
    wide_come += wide_ready
    gains = gains + partner(gains)
    normed_one, scale_one = norm_rows(residual_wide)
    normed_grad = both(normed_part, normed_other)
    attn_gain_term = jnp.sum(normed_grad * normed_one, axis=0)
    residual_grad = canonical(
        mixed_grad + norm_back(normed_grad * attn_gain, normed_one, scale_one)
    )
    wide_results = wide.unpack(own_ready(wide_ready), wide_outs, wide_results, [token])

    narrow_way, token = narrow_steps.send((narrow_way, [wide_results[0]]))
    small = SmallSum(
        devices,
        jnp.concatenate([attn_gain_term, mlp_gain_term, gains[0], gains[1]]).reshape(-1, 128),
    )
    for step in range(steps - 3):
        narrow_way, token = narrow_steps.send((narrow_way, [token]))
        *wide_way, token = tie(*wide_way, token)
        wide_way, wide_ready = wide_steps.send(wide_way)
        wide_come += wide_ready
        *came, token = tie(*small.under_way, token)
        small.came(came)
        wide_results = wide.unpack(own_ready(wide_ready), wide_outs, wide_results, [token])
    narrow_shard, token = narrow_steps.send((narrow_way, [wide_results[0]]))

    narrow_steps = narrow.gather(narrow_shard)
    narrow_way, narrow_ready = next(narrow_steps)
    wide_way, came, token = tie(wide_way, small.under_way, token)
    small.came(came)
    _, wide_ready = wide_steps.send(wide_way)
    wide_come += wide_ready
    wide_results = wide.unpack(own_ready(wide_ready), wide_outs, wide_results, [token])
    share = -(-len(wide_come) // steps)
    narrow_results = None
    for step in range(1, steps + 1):
        here = wide_come[(step - 1) * share : step * share]
        if here:
            wide_results = wide.unpack(other_ready(here), wide_outs, wide_results)
        ready = own_ready(narrow_ready) + other_ready(narrow_ready)
        narrow_results = narrow.unpack(ready, narrow_outs, narrow_results, [wide_results[0]])
        if step < steps:
            narrow_way, came, narrow_results[0] = tie(
                narrow_way, small.under_way, narrow_results[0]
            )
            small.came(came)
            narrow_way, narrow_ready = narrow_steps.send(narrow_way)
    while small.under_way:
        small.came(small.under_way)
    _, narrow_ready = narrow_steps.send(narrow_way)
    ready = own_ready(narrow_ready) + other_ready(narrow_ready)
    out_weight_sum, query_sum, key_sum, value_sum = narrow.unpack(
        ready, narrow_outs, narrow_results
    )
    gate_sum, up_sum, down_sum = wide_results
    small = small.total.reshape(-1)

    attn_gain_grad, mlp_gain_grad = small[:model], small[model : 2 * model]
    query_gain_grad = small[2 * model : 2 * model + head_dim]
    key_gain_grad = small[2 * model + head_dim :]
    return (
        layer_out,
        residual_grad,
        attn_gain_grad,
        query_sum[0],
        key_sum[0],
        value_sum[0],
        query_gain_grad,
        key_gain_grad,
        out_weight_sum[0],
        mlp_gain_grad,
        gate_sum[0],
        up_sum[0],
        down_sum.reshape(units, model),
    )


def solution(mesh):
    return jax.shard_map(
        functools.partial(body, mesh.shape["cp"]),
        mesh=mesh,
        in_specs=(
            P("cp", None),
            P("cp", None),
            P(),
            P("cp"),
            P(),
            P(None, "tp"),
            P(None, "tp"),
            P(None, "tp"),
            P(),
            P(),
            P("tp", None),
            P(),
            P(None, "tp"),
            P(None, "tp"),
            P("tp", None),
        ),
        out_specs=(
            P("cp", None),
            P("cp", None),
            P(),
            P(None, "tp"),
            P(None, "tp"),
            P(None, "tp"),
            P(),
            P(),
            P("tp", None),
            P(),
            P(None, "tp"),
            P(None, "tp"),
            P("tp", None),
        ),
        check_vma=False,
    )
```

time: 584 us -> 395 us (0.68)
  waiting for transfers between devices: 269 us -> 124 us
  other arithmetic: 43.9 us -> 11.8 us
  starting transfers between devices: 103 us -> 73.1 us
  Pallas kernels: 85.2 us -> 108 us
  between operations: 12.8 us -> 3.93 us
    ppermute x40 -> x27, waiting for transfers between devices: 141 us -> 66.7 us  [send_up(): return lax.ppermute(x, 'cp', self.up)]
    ppermute x40 -> x27, waiting for transfers between devices: 96.4 us -> 31.8 us  [send_down(): return lax.ppermute(x, 'cp', self.down)]
    unnamed x142 -> x216, local copies, waits for them, and re-layouts: 11.2 us -> 38.3 us
    ppermute x40 -> x27, starting transfers between devices: 51.6 us -> 27.4 us  [send_down(): return lax.ppermute(x, 'cp', self.down)]
    pallas_call x19 -> x42, Pallas kernels: 85.2 us -> 108 us  [the longest x14 32.1 us: unpack(): pl.pallas_call(kernel, out_shape=shapes, grid_spec=pltpu.PrefetchScalarGr...]
    slice x31 -> x4, local copies, waits for them, and re-layouts: 19.8 us -> 0.07 us  [the longest x2 0.03 us: gather(): down[:, cut:]]
    convert_element_type x40 -> x4, other arithmetic: 17.8 us -> 1.56 us  [the longest x1 0.99 us: body(): layer_out = canonical(mixed + both(layer_part, layer_other)).astype(BF)]
    ppermute x9, waiting for transfers between devices: 31.1 us -> 18.4 us  [the longest x5 17.4 us: partner(): return lax.ppermute(x, 'tp', [(0, 1), (1, 0)])]
  transfers between devices with their start and end apart: 141 -> 90, of which waited for: 51 -> 40; matrix products, arithmetic and copies ran while one was open for 14% -> 7% of each run, Pallas kernels for 13% -> 24%
where the time goes in v2:
time: 395 us; the launch traced here: 388 us
  waiting for transfers between devices  124 us (31%)
  Pallas kernels  108 us (27%)
  starting transfers between devices  73.1 us (19%)
  local copies, waits for them, and re-layouts  46 us (12%)
  matrix products  21.4 us (5%)
  other arithmetic  11.8 us (3%)
    ppermute x27, waiting for transfers between devices, send_up(): return lax.ppermute(x, 'cp', self.up)  66.7 us
    unnamed x216, local copies, waits for them, and re-layouts  38.3 us
    pallas_call x14, Pallas kernels, unpack(): pl.pallas_call(kernel, out_shape=shapes, grid_spec=pltpu.PrefetchScalarGr...  32.1 us
    ppermute x27, waiting for transfers between devices, send_down(): return lax.ppermute(x, 'cp', self.down)  31.8 us
    ppermute x27, starting transfers between devices, send_up(): return lax.ppermute(x, 'cp', self.up)  31.3 us
    ppermute x27, starting transfers between devices, send_down(): return lax.ppermute(x, 'cp', self.down)  27.4 us
    pallas_call x5, Pallas kernels, attention_backward(): pl.pallas_call(kernel, out_shape=outs, grid=(groups,), in_specs=specs + m...  26.8 us
    pallas_call x10, Pallas kernels, shards(): pl.pallas_call(kernel, out_shape=[jax.ShapeDtypeStruct((rows, wide), BF)...  22.2 us
  transfers between devices with their start and end apart: 90, of which 40 were waited for; matrix products, arithmetic and copies ran while one was open for 7% of the time, Pallas kernels for 24%

profile of v2, /device:TPU:0, one launch (start us, length us, event | category | flops | bytes accessed | tf_op | source)
XLA Modules:
  0.0 387.7 jit_solution(6361085112711094771)
XLA Ops:
  10.8 3.1 collective-permute-start.3
  17.8 3.0 constant_dynamic-slice_fusion.5
  33.4 4.1 %fusion.44 = f32[256,1536]{1,0:T(8,128)} fusion(bf16[256,1024]{1,0:T(8,128)(2,1)S(1)} %maximum_select_fusion.2, bf16[1536,1024]{1,0:T(8,128)(2,1)} %param.30), kind=kOutput, calls=%fused_computation.107 | convolution fusion | flops 805306368 | bytes 5242880 | tf_op jit(solution)/shard_map/dot_general | solution.py:26
  37.6 3.0 shard_map.257.refs_8_
  40.6 3.8 shard_map.258.refs_8_
  48.7 3.7 shard_map.259.refs_8_
  56.5 2.8 collective-permute-done.13.refs_5_.refs_9_
  61.4 3.7 shard_map.260.refs_6_
  66.2 3.4 shard_map.261
  76.1 12.8 %collective-permute-done.17 = bf16[256,1024]{1,0:T(8,128)(2,1)} collective-permute-done((bf16[256,1024]{1,0:T(8,128)(2,1)}, bf16[256,1024]{1,0:T(8,128)(2,1)}, u32[]{:S(2)}, u32[]{:S(2)}) %collective-permute-start.17) | collective-permute-done | bytes 524320 | tf_op jit(solution)/shard_map/ppermute | solution.py:328
  103.7 4.6 %collective-permute-done.20.refs_3_.refs_7_ = bf16[3,256,1024]{2,1,0:T(8,128)(2,1)S(1)} collective-permute-done((bf16[3,256,1024]{2,1,0:T(8,128)(2,1)S(1)}, bf16[3,256,1024]{2,1,0:T(8,128)(2,1)S(1)}, u32[]{:S(2)}, u32[]{:S(2)}) %collective-permute-start.20) | collective-permute-done | bytes 1572896 | tf_op jit(solution)/shard_map/ppermute | solution.py:109
  112.5 3.7 collective-permute-done.18
  121.1 3.7 shard_map.264
  126.9 5.7 %shard_map.265 = (bf16[512,512]{1,0:T(8,128)(2,1)S(1)}, bf16[512,512]{1,0:T(8,128)(2,1)S(1)}, f32[2,2,2,128,256]{4,3,2,1,0:T(8,128)S(1)}) custom-call(s32[32]{0:T(128)S(1)} %copy-done.64, s32[9]{0:T(128)S(1)} %fusion.32.refs_1_.refs_0_.table_ref, bf16[256,512]{1,0:T(8,128)(2,1)S(1)} %get-tuple-element.198.refs_2_, ...), custom_call_target="tpu_custom_call" | custom-call | flops 1024 | bytes 1024 | tf_op jit(solution)/shard_map/pallas_call | solution.py:763
  139.6 5.7 %shard_map.268 = (bf16[512,512]{1,0:T(8,128)(2,1)S(1)}, bf16[512,512]{1,0:T(8,128)(2,1)S(1)}, f32[2,2,2,128,256]{4,3,2,1,0:T(8,128)S(1)}) custom-call(s32[32]{0:T(128)S(1)} %copy-done.64, s32[9]{0:T(128)S(1)} %fusion.32.refs_1_.refs_0_.table_ref, bf16[256,512]{1,0:T(8,128)(2,1)S(1)} %get-tuple-element.198.refs_2_, ...), custom_call_target="tpu_custom_call" | custom-call | flops 1024 | bytes 1024 | tf_op jit(solution)/shard_map/pallas_call | solution.py:763
  145.3 6.3 %collective-permute-done.28.refs_8_ = bf16[96,3072]{1,0:T(8,128)(2,1)S(1)} collective-permute-done((bf16[96,3072]{1,0:T(8,128)(2,1)S(1)}, bf16[96,3072]{1,0:T(8,128)(2,1)S(1)}, u32[]{:S(2)}, u32[]{:S(2)}) %collective-permute-start.28) | collective-permute-done | bytes 589856 | tf_op jit(solution)/shard_map/ppermute | solution.py:103
  157.7 5.1 %collective-permute-done.26.refs_2_ = bf16[512,512]{1,0:T(8,128)(2,1)S(1)} collective-permute-done((bf16[512,512]{1,0:T(8,128)(2,1)S(1)}, bf16[512,512]{1,0:T(8,128)(2,1)S(1)}, u32[]{:S(2)}, u32[]{:S(2)}) %collective-permute-start.26) | collective-permute-done | bytes 524320 | tf_op jit(solution)/shard_map/ppermute | solution.py:103
  166.8 5.9 %shard_map.271 = (bf16[512,512]{1,0:T(8,128)(2,1)S(1)}, bf16[512,512]{1,0:T(8,128)(2,1)S(1)}, f32[2,2,2,128,256]{4,3,2,1,0:T(8,128)S(1)}) custom-call(s32[32]{0:T(128)S(1)} %copy-done.64, s32[9]{0:T(128)S(1)} %fusion.32.refs_1_.refs_0_.table_ref, bf16[256,512]{1,0:T(8,128)(2,1)S(1)} %get-tuple-element.198.refs_2_, ...), custom_call_target="tpu_custom_call" | custom-call | flops 1024 | bytes 1024 | tf_op jit(solution)/shard_map/pallas_call | solution.py:763
  179.5 5.5 %collective-permute-done.30.refs_2_ = bf16[512,512]{1,0:T(8,128)(2,1)S(1)} collective-permute-done((bf16[512,512]{1,0:T(8,128)(2,1)S(1)}, bf16[512,512]{1,0:T(8,128)(2,1)S(1)}, u32[]{:S(2)}, u32[]{:S(2)}) %collective-permute-start.30) | collective-permute-done | bytes 524320 | tf_op jit(solution)/shard_map/ppermute | solution.py:103
  186.5 5.7 %shard_map.274 = (bf16[256,512]{1,0:T(8,128)(2,1)S(1)}, bf16[256,512]{1,0:T(8,128)(2,1)S(1)}, f32[256,512]{1,0:T(8,128)S(1)}, f32[256,512]{1,0:T(8,128)}) custom-call(s32[32]{0:T(128)S(1)} %copy-done.64, s32[9]{0:T(128)S(1)} %fusion.32.refs_1_.refs_0_.table_ref, bf16[256,512]{1,0:T(8,128)(2,1)S(1)} %get-tuple-element.198.refs_2_, ...), custom_call_target="tpu_custom_call" | custom-call | flops 1024 | bytes 1024 | tf_op jit(solution)/shard_map/pallas_call | solution.py:763
  205.9 6.2 %collective-permute-done.36.refs_4_ = bf16[96,3072]{1,0:T(8,128)(2,1)S(1)} collective-permute-done((bf16[96,3072]{1,0:T(8,128)(2,1)}, bf16[96,3072]{1,0:T(8,128)(2,1)S(1)}, u32[]{:S(2)}, u32[]{:S(2)}) %collective-permute-start.36) | collective-permute-done | bytes 589856 | tf_op jit(solution)/shard_map/ppermute | solution.py:103
  219.4 7.6 %collective-permute-done.34 = bf16[512,512]{1,0:T(8,128)(2,1)S(1)} collective-permute-done((bf16[512,512]{1,0:T(8,128)(2,1)S(1)}, bf16[512,512]{1,0:T(8,128)(2,1)S(1)}, u32[]{:S(2)}, u32[]{:S(2)}) %collective-permute-start.34) | collective-permute-done | bytes 524320 | tf_op jit(solution)/shard_map/ppermute | solution.py:103
  232.5 6.8 %collective-permute-done.43.refs_1_ = bf16[96,3072]{1,0:T(8,128)(2,1)} collective-permute-done((bf16[96,3072]{1,0:T(8,128)(2,1)S(1)}, bf16[96,3072]{1,0:T(8,128)(2,1)}, u32[]{:S(2)}, u32[]{:S(2)}) %collective-permute-start.43) | collective-permute-done | bytes 589856 | tf_op jit(solution)/shard_map/ppermute | solution.py:106
  251.9 3.3 shard_map.280
  255.2 5.2 %collective-permute-done.49.refs_12_ = bf16[64,1536]{1,0:T(8,128)(2,1)S(1)} collective-permute-done((bf16[64,1536]{1,0:T(8,128)(2,1)S(1)}, bf16[64,1536]{1,0:T(8,128)(2,1)S(1)}, u32[]{:S(2)}, u32[]{:S(2)}) %collective-permute-start.49) | collective-permute-done | bytes 196640 | tf_op jit(solution)/shard_map/ppermute | solution.py:103
  270.6 3.3 shard_map.282
  274.0 3.5 collective-permute-done.55.refs_12_
  287.9 8.0 %collective-permute-done.57.refs_12_ = bf16[64,3072]{1,0:T(8,128)(2,1)S(1)} collective-permute-done((bf16[64,3072]{1,0:T(8,128)(2,1)S(1)}, bf16[64,3072]{1,0:T(8,128)(2,1)S(1)}, u32[]{:S(2)}, u32[]{:S(2)}) %collective-permute-start.57) | collective-permute-done | bytes 393248 | tf_op jit(solution)/shard_map/ppermute | solution.py:103
  302.6 5.9 %collective-permute-done.53.refs_0_ = bf16[96,3072]{1,0:T(8,128)(2,1)S(1)} collective-permute-done((bf16[96,3072]{1,0:T(8,128)(2,1)}, bf16[96,3072]{1,0:T(8,128)(2,1)S(1)}, u32[]{:S(2)}, u32[]{:S(2)}) %collective-permute-start.53) | collective-permute-done | bytes 589856 | tf_op jit(solution)/shard_map/ppermute | solution.py:103
  310.7 3.5 collective-permute-done.62.refs_6_
  367.3 2.9 collective-permute-done.83
  370.6 5.3 %collective-permute-done.84 = bf16[64,1536]{1,0:T(8,128)(2,1)S(1)} collective-permute-done((bf16[64,1536]{1,0:T(8,128)(2,1)S(1)}, bf16[64,1536]{1,0:T(8,128)(2,1)S(1)}, u32[]{:S(2)}, u32[]{:S(2)}) %collective-permute-start.84) | collective-permute-done | bytes 196640 | tf_op jit(solution)/shard_map/ppermute | solution.py:106
  (475 shorter events, 226.7 us)
Async XLA Ops:
  10.8 16.4 %collective-permute-start.3 = (bf16[256,512]{1,0:T(8,128)(2,1)}, bf16[256,512]{1,0:T(8,128)(2,1)}, u32[]{:S(2)}, u32[]{:S(2)}) collective-permute-start(bf16[256,512]{1,0:T(8,128)(2,1)} %get-tuple-element.200.refs_4_.refs_8_), channel_id=1, source_target_pairs={{2,0},{3,1},{6,2},{7,3},{10,6},{11,7},{14,10},{15,11},{12,14},{13,... | collective-permute-start | bytes 786440 | tf_op jit(solution)/shard_map/ppermute | solution.py:106
  13.9 15.4 %collective-permute-start.1 = (bf16[256,512]{1,0:T(8,128)(2,1)}, bf16[256,512]{1,0:T(8,128)(2,1)}, u32[]{:S(2)}, u32[]{:S(2)}) collective-permute-start(bf16[256,512]{1,0:T(8,128)(2,1)} %get-tuple-element.200.refs_4_.refs_8_), channel_id=1, source_target_pairs={{0,2},{1,3},{2,6},{3,7},{6,10},{7,11},{10,14},{11,15},{14,12},{15,... | collective-permute-start | bytes 786440 | tf_op jit(solution)/shard_map/ppermute | solution.py:103
  17.2 20.4 %collective-permute-start = (bf16[256,512]{1,0:T(8,128)(2,1)}, bf16[256,512]{1,0:T(8,128)(2,1)}, u32[]{:S(2)}, u32[]{:S(2)}) collective-permute-start(bf16[256,512]{1,0:T(8,128)(2,1)} %get-tuple-element.199), channel_id=1, source_target_pairs={{0,1},{1,0},{2,3},{3,2},{4,5},{5,4},{6,7},{7,6},{8,9},{9,8},{10,11... | collective-permute-start | bytes 786440 | tf_op jit(solution)/shard_map/ppermute | solution.py:109
  27.2 17.3 %collective-permute-start.4 = (bf16[256,512]{1,0:T(8,128)(2,1)}, bf16[256,512]{1,0:T(8,128)(2,1)S(1)}, u32[]{:S(2)}, u32[]{:S(2)}) collective-permute-start(bf16[256,512]{1,0:T(8,128)(2,1)} %collective-permute-done.3.refs_7_.refs_6_.refs_10_), channel_id=1, source_target_pairs={{2,0},{3,1},{6,2},{7,3},{10,6},{11,7},{14,10},{15,11},{12,14},{13,... | collective-permute-start | bytes 786440 | tf_op jit(solution)/shard_map/ppermute | solution.py:106
  29.3 15.2 %collective-permute-start.2 = (bf16[256,512]{1,0:T(8,128)(2,1)}, bf16[256,512]{1,0:T(8,128)(2,1)S(1)}, u32[]{:S(2)}, u32[]{:S(2)}) collective-permute-start(bf16[256,512]{1,0:T(8,128)(2,1)} %collective-permute-done.1.refs_6_.refs_4_.refs_8_), channel_id=1, source_target_pairs={{0,2},{1,3},{2,6},{3,7},{6,10},{7,11},{10,14},{11,15},{14,12},{15,... | collective-permute-start | bytes 786440 | tf_op jit(solution)/shard_map/ppermute | solution.py:103
  31.4 15.2 %collective-permute-start.11 = (bf16[256,512]{1,0:T(8,128)(2,1)S(1)}, bf16[256,512]{1,0:T(8,128)(2,1)S(1)}, u32[]{:S(2)}, u32[]{:S(2)}) collective-permute-start(bf16[256,512]{1,0:T(8,128)(2,1)S(1)} %collective-permute-done.7.refs_7_.refs_11_), channel_id=1, source_target_pairs={{2,0},{3,1},{6,2},{7,3},{10,6},{11,7},{14,10},{15,11},{12,14},{13,... | collective-permute-start | bytes 786440 | tf_op jit(solution)/shard_map/ppermute | solution.py:106
  135.2 16.3 %collective-permute-start.28 = (bf16[96,3072]{1,0:T(8,128)(2,1)S(1)}, bf16[96,3072]{1,0:T(8,128)(2,1)S(1)}, u32[]{:S(2)}, u32[]{:S(2)}) collective-permute-start(bf16[96,3072]{1,0:T(8,128)(2,1)S(1)} %get-tuple-element.247), channel_id=1, source_target_pairs={{0,2},{1,3},{2,6},{3,7},{6,10},{7,11},{10,14},{11,15},{14,12},{15,... | collective-permute-start | bytes 1769480 | tf_op jit(solution)/shard_map/ppermute | solution.py:103
  136.8 16.3 %collective-permute-start.29 = (bf16[96,3072]{1,0:T(8,128)(2,1)S(1)}, bf16[96,3072]{1,0:T(8,128)(2,1)S(1)}, u32[]{:S(2)}, u32[]{:S(2)}) collective-permute-start(bf16[96,3072]{1,0:T(8,128)(2,1)S(1)} %get-tuple-element.248), channel_id=1, source_target_pairs={{2,0},{3,1},{6,2},{7,3},{10,6},{11,7},{14,10},{15,11},{12,14},{13,... | collective-permute-start | bytes 1769480 | tf_op jit(solution)/shard_map/ppermute | solution.py:106
  137.5 25.3 %collective-permute-start.26 = (bf16[512,512]{1,0:T(8,128)(2,1)S(1)}, bf16[512,512]{1,0:T(8,128)(2,1)S(1)}, u32[]{:S(2)}, u32[]{:S(2)}) collective-permute-start(bf16[512,512]{1,0:T(8,128)(2,1)S(1)} %get-tuple-element.245), channel_id=1, source_target_pairs={{0,2},{1,3},{2,6},{3,7},{6,10},{7,11},{10,14},{11,15},{14,12},{15,... | collective-permute-start | bytes 1572872 | tf_op jit(solution)/shard_map/ppermute | solution.py:103
  139.0 25.3 %collective-permute-start.27 = (bf16[512,512]{1,0:T(8,128)(2,1)S(1)}, bf16[512,512]{1,0:T(8,128)(2,1)S(1)}, u32[]{:S(2)}, u32[]{:S(2)}) collective-permute-start(bf16[512,512]{1,0:T(8,128)(2,1)S(1)} %get-tuple-element.246), channel_id=1, source_target_pairs={{2,0},{3,1},{6,2},{7,3},{10,6},{11,7},{14,10},{15,11},{12,14},{13,... | collective-permute-start | bytes 1572872 | tf_op jit(solution)/shard_map/ppermute | solution.py:106
  155.6 19.8 %collective-permute-start.32 = (bf16[96,3072]{1,0:T(8,128)(2,1)S(1)}, bf16[96,3072]{1,0:T(8,128)(2,1)S(1)}, u32[]{:S(2)}, u32[]{:S(2)}) collective-permute-start(bf16[96,3072]{1,0:T(8,128)(2,1)S(1)} %get-tuple-element.255), channel_id=1, source_target_pairs={{0,2},{1,3},{2,6},{3,7},{6,10},{7,11},{10,14},{11,15},{14,12},{15,... | collective-permute-start | bytes 1769480 | tf_op jit(solution)/shard_map/ppermute | solution.py:103
  157.3 19.7 %collective-permute-start.33 = (bf16[96,3072]{1,0:T(8,128)(2,1)S(1)}, bf16[96,3072]{1,0:T(8,128)(2,1)S(1)}, u32[]{:S(2)}, u32[]{:S(2)}) collective-permute-start(bf16[96,3072]{1,0:T(8,128)(2,1)S(1)} %get-tuple-element.256), channel_id=1, source_target_pairs={{2,0},{3,1},{6,2},{7,3},{10,6},{11,7},{14,10},{15,11},{12,14},{13,... | collective-permute-start | bytes 1769480 | tf_op jit(solution)/shard_map/ppermute | solution.py:106
  164.5 20.4 %collective-permute-start.30 = (bf16[512,512]{1,0:T(8,128)(2,1)S(1)}, bf16[512,512]{1,0:T(8,128)(2,1)S(1)}, u32[]{:S(2)}, u32[]{:S(2)}) collective-permute-start(bf16[512,512]{1,0:T(8,128)(2,1)S(1)} %get-tuple-element.253), channel_id=1, source_target_pairs={{0,2},{1,3},{2,6},{3,7},{6,10},{7,11},{10,14},{11,15},{14,12},{15,... | collective-permute-start | bytes 1572872 | tf_op jit(solution)/shard_map/ppermute | solution.py:103
  166.2 20.0 %collective-permute-start.31 = (bf16[512,512]{1,0:T(8,128)(2,1)S(1)}, bf16[512,512]{1,0:T(8,128)(2,1)S(1)}, u32[]{:S(2)}, u32[]{:S(2)}) collective-permute-start(bf16[512,512]{1,0:T(8,128)(2,1)S(1)} %get-tuple-element.254), channel_id=1, source_target_pairs={{2,0},{3,1},{6,2},{7,3},{10,6},{11,7},{14,10},{15,11},{12,14},{13,... | collective-permute-start | bytes 1572872 | tf_op jit(solution)/shard_map/ppermute | solution.py:106
  196.1 20.2 %collective-permute-start.40 = (bf16[1,512,1024]{2,1,0:T(8,128)(2,1)S(1)}, bf16[1,512,1024]{2,1,0:T(8,128)(2,1)S(1)}, u32[]{:S(2)}, u32[]{:S(2)}) collective-permute-start(bf16[1,512,1024]{2,1,0:T(8,128)(2,1)S(1)} %bitcast.146), channel_id=1, source_target_pairs={{0,1},{1,0},{2,3},{3,2},{4,5},{5,4},{6,7},{7,6},{8,9},{9,8},{10,11... | collective-permute-start | bytes 3145736 | tf_op jit(solution)/shard_map/ppermute | solution.py:109
  196.6 15.5 %collective-permute-start.36 = (bf16[96,3072]{1,0:T(8,128)(2,1)}, bf16[96,3072]{1,0:T(8,128)(2,1)S(1)}, u32[]{:S(2)}, u32[]{:S(2)}) collective-permute-start(bf16[96,3072]{1,0:T(8,128)(2,1)} %copy-done.71), channel_id=1, source_target_pairs={{0,2},{1,3},{2,6},{3,7},{6,10},{7,11},{10,14},{11,15},{14,12},{15,... | collective-permute-start | bytes 1769480 | tf_op jit(solution)/shard_map/ppermute | solution.py:103
  198.2 15.5 %collective-permute-start.37 = (bf16[96,3072]{1,0:T(8,128)(2,1)}, bf16[96,3072]{1,0:T(8,128)(2,1)S(1)}, u32[]{:S(2)}, u32[]{:S(2)}) collective-permute-start(bf16[96,3072]{1,0:T(8,128)(2,1)} %copy-done.70), channel_id=1, source_target_pairs={{2,0},{3,1},{6,2},{7,3},{10,6},{11,7},{14,10},{15,11},{12,14},{13,... | collective-permute-start | bytes 1769480 | tf_op jit(solution)/shard_map/ppermute | solution.py:106
  201.4 27.2 %collective-permute-start.41 = (bf16[1,512,1024]{2,1,0:T(8,128)(2,1)S(1)}, bf16[1,512,1024]{2,1,0:T(8,128)(2,1)S(1)}, u32[]{:S(2)}, u32[]{:S(2)}) collective-permute-start(bf16[1,512,1024]{2,1,0:T(8,128)(2,1)S(1)} %bitcast.147), channel_id=1, source_target_pairs={{0,1},{1,0},{2,3},{3,2},{4,5},{5,4},{6,7},{7,6},{8,9},{9,8},{10,11... | collective-permute-start | bytes 3145736 | tf_op jit(solution)/shard_map/ppermute | solution.py:109
  216.3 23.0 %collective-permute-start.43 = (bf16[96,3072]{1,0:T(8,128)(2,1)S(1)}, bf16[96,3072]{1,0:T(8,128)(2,1)}, u32[]{:S(2)}, u32[]{:S(2)}) collective-permute-start(bf16[96,3072]{1,0:T(8,128)(2,1)S(1)} %get-tuple-element.273.refs_0_), channel_id=1, source_target_pairs={{2,0},{3,1},{6,2},{7,3},{10,6},{11,7},{14,10},{15,11},{12,14},{13,... | collective-permute-start | bytes 1769480 | tf_op jit(solution)/shard_map/ppermute | solution.py:106
  217.8 21.5 %collective-permute-start.42 = (bf16[96,3072]{1,0:T(8,128)(2,1)S(1)}, bf16[96,3072]{1,0:T(8,128)(2,1)}, u32[]{:S(2)}, u32[]{:S(2)}) collective-permute-start(bf16[96,3072]{1,0:T(8,128)(2,1)S(1)} %get-tuple-element.273.refs_0_), channel_id=1, source_target_pairs={{0,2},{1,3},{2,6},{3,7},{6,10},{7,11},{10,14},{11,15},{14,12},{15,... | collective-permute-start | bytes 1769480 | tf_op jit(solution)/shard_map/ppermute | solution.py:103
  240.2 28.9 %collective-permute-start.46 = (bf16[96,3072]{1,0:T(8,128)(2,1)}, bf16[96,3072]{1,0:T(8,128)(2,1)}, u32[]{:S(2)}, u32[]{:S(2)}) collective-permute-start(bf16[96,3072]{1,0:T(8,128)(2,1)} %collective-permute-done.42.refs_0_), channel_id=1, source_target_pairs={{0,2},{1,3},{2,6},{3,7},{6,10},{7,11},{10,14},{11,15},{14,12},{15,... | collective-permute-start | bytes 1769480 | tf_op jit(solution)/shard_map/ppermute | solution.py:103
  241.9 28.7 %collective-permute-start.47 = (bf16[96,3072]{1,0:T(8,128)(2,1)}, bf16[96,3072]{1,0:T(8,128)(2,1)}, u32[]{:S(2)}, u32[]{:S(2)}) collective-permute-start(bf16[96,3072]{1,0:T(8,128)(2,1)} %collective-permute-done.43.refs_1_), channel_id=1, source_target_pairs={{2,0},{3,1},{6,2},{7,3},{10,6},{11,7},{14,10},{15,11},{12,14},{13,... | collective-permute-start | bytes 1769480 | tf_op jit(solution)/shard_map/ppermute | solution.py:106
  250.4 20.3 %collective-permute-start.48 = (bf16[256,1024]{1,0:T(8,128)(2,1)}, bf16[256,1024]{1,0:T(8,128)(2,1)}, u32[]{:S(2)}, u32[]{:S(2)}) collective-permute-start(bf16[256,1024]{1,0:T(8,128)(2,1)} %fusion.8), channel_id=1, source_target_pairs={{0,16},{16,0},{1,17},{17,1},{2,18},{18,2},{3,19},{19,3},{4,20},{20... | collective-permute-start | bytes 1572872 | tf_op jit(solution)/shard_map/ppermute | solution.py:328
  269.1 18.8 %collective-permute-start.51 = (f32[2,128]{1,0:T(2,128)S(1)}, f32[2,128]{1,0:T(2,128)S(1)}, u32[]{:S(2)}, u32[]{:S(2)}) collective-permute-start(f32[2,128]{1,0:T(2,128)S(1)} %pad_maximum_fusion.2), channel_id=1, source_target_pairs={{0,16},{16,0},{1,17},{17,1},{2,18},{18,2},{3,19},{19,3},{4,20},{20... | collective-permute-start | bytes 3080 | tf_op jit(solution)/shard_map/ppermute | solution.py:328
  285.9 22.7 %collective-permute-start.53 = (bf16[96,3072]{1,0:T(8,128)(2,1)}, bf16[96,3072]{1,0:T(8,128)(2,1)S(1)}, u32[]{:S(2)}, u32[]{:S(2)}) collective-permute-start(bf16[96,3072]{1,0:T(8,128)(2,1)} %collective-permute-done.46.refs_0_), channel_id=1, source_target_pairs={{0,2},{1,3},{2,6},{3,7},{6,10},{7,11},{10,14},{11,15},{14,12},{15,... | collective-permute-start | bytes 1769480 | tf_op jit(solution)/shard_map/ppermute | solution.py:103
  286.4 22.7 %collective-permute-start.54 = (bf16[96,3072]{1,0:T(8,128)(2,1)}, bf16[96,3072]{1,0:T(8,128)(2,1)S(1)}, u32[]{:S(2)}, u32[]{:S(2)}) collective-permute-start(bf16[96,3072]{1,0:T(8,128)(2,1)} %collective-permute-done.47.refs_1_), channel_id=1, source_target_pairs={{2,0},{3,1},{6,2},{7,3},{10,6},{11,7},{14,10},{15,11},{12,14},{13,... | collective-permute-start | bytes 1769480 | tf_op jit(solution)/shard_map/ppermute | solution.py:106
  298.7 15.5 %collective-permute-start.62 = (bf16[64,3072]{1,0:T(8,128)(2,1)S(1)}, bf16[64,3072]{1,0:T(8,128)(2,1)S(1)}, u32[]{:S(2)}, u32[]{:S(2)}) collective-permute-start(bf16[64,3072]{1,0:T(8,128)(2,1)S(1)} %get-tuple-element.315), channel_id=1, source_target_pairs={{0,2},{1,3},{2,6},{3,7},{6,10},{7,11},{10,14},{11,15},{14,12},{15,... | collective-permute-start | bytes 1179656 | tf_op jit(solution)/shard_map/ppermute | solution.py:103
  299.3 17.3 %collective-permute-start.63 = (bf16[64,3072]{1,0:T(8,128)(2,1)S(1)}, bf16[64,3072]{1,0:T(8,128)(2,1)S(1)}, u32[]{:S(2)}, u32[]{:S(2)}) collective-permute-start(bf16[64,3072]{1,0:T(8,128)(2,1)S(1)} %get-tuple-element.316), channel_id=1, source_target_pairs={{2,0},{3,1},{6,2},{7,3},{10,6},{11,7},{14,10},{15,11},{12,14},{13,... | collective-permute-start | bytes 1179656 | tf_op jit(solution)/shard_map/ppermute | solution.py:106
  308.5 16.3 %collective-permute-start.68 = (bf16[96,3072]{1,0:T(8,128)(2,1)S(1)}, bf16[96,3072]{1,0:T(8,128)(2,1)S(1)}, u32[]{:S(2)}, u32[]{:S(2)}) collective-permute-start(bf16[96,3072]{1,0:T(8,128)(2,1)S(1)} %copy-done.50), channel_id=1, source_target_pairs={{0,1},{1,0},{2,3},{3,2},{4,5},{5,4},{6,7},{7,6},{8,9},{9,8},{10,11... | collective-permute-start | bytes 1769480 | tf_op jit(solution)/shard_map/ppermute | solution.py:109
  309.0 16.8 %collective-permute-start.69 = (bf16[96,3072]{1,0:T(8,128)(2,1)}, bf16[96,3072]{1,0:T(8,128)(2,1)S(1)}, u32[]{:S(2)}, u32[]{:S(2)}) collective-permute-start(bf16[96,3072]{1,0:T(8,128)(2,1)} %collective-permute-done.42.refs_0_), channel_id=1, source_target_pairs={{0,1},{1,0},{2,3},{3,2},{4,5},{5,4},{6,7},{7,6},{8,9},{9,8},{10,11... | collective-permute-start | bytes 1769480 | tf_op jit(solution)/shard_map/ppermute | solution.py:109
  309.1 15.2 %collective-permute-start.60 = (bf16[96,1536]{1,0:T(8,128)(2,1)S(1)}, bf16[96,1536]{1,0:T(8,128)(2,1)S(1)}, u32[]{:S(2)}, u32[]{:S(2)}) collective-permute-start(bf16[96,1536]{1,0:T(8,128)(2,1)S(1)} %slice.105), channel_id=1, source_target_pairs={{2,0},{3,1},{6,2},{7,3},{10,6},{11,7},{14,10},{15,11},{12,14},{13,... | collective-permute-start | bytes 884744 | tf_op jit(solution)/shard_map/ppermute | solution.py:106
  337.3 15.2 %collective-permute-start.81 = (bf16[96,3072]{1,0:T(8,128)(2,1)}, bf16[96,3072]{1,0:T(8,128)(2,1)S(1)}, u32[]{:S(2)}, u32[]{:S(2)}) collective-permute-start(bf16[96,3072]{1,0:T(8,128)(2,1)} %collective-permute-done.47.refs_1_), channel_id=1, source_target_pairs={{0,1},{1,0},{2,3},{3,2},{4,5},{5,4},{6,7},{7,6},{8,9},{9,8},{10,11... | collective-permute-start | bytes 1769480 | tf_op jit(solution)/shard_map/ppermute | solution.py:109
  (165 other events, 1406.7 us)

commit v3 on v2

v3 whole, which is shorter than its diff:
```python
import functools
import math

import jax
import jax.numpy as jnp
from jax import lax
from jax.experimental import pallas as pl
from jax.experimental.pallas import tpu as pltpu
from jax.sharding import PartitionSpec as P

EPS = 1e-06
ROPE_BASE = 1000000.0
HEAD = 128
LOG2E = 1.4426950408889634
VMEM_LIMIT = 32 * 1024 * 1024


def cost(microseconds):
    return pl.CostEstimate(
        flops=1024 + int(microseconds * 1e9), bytes_accessed=1024, transcendentals=0
    )


LIGHT = cost(0)
FORWARD = cost(0)
HEAVY = 50
SOME = 4
BF = jnp.bfloat16
F32 = jnp.float32
TOKEN = jax.ShapeDtypeStruct((8, 128), jnp.float32)


def nn(a, b):
    return lax.dot_general(a, b, (((1,), (0,)), ((), ())), preferred_element_type=F32)


def nt(a, b):
    return lax.dot_general(a, b, (((1,), (1,)), ((), ())), preferred_element_type=F32)


def tn(a, b):
    return lax.dot_general(a, b, (((0,), (0,)), ((), ())), preferred_element_type=F32)


def norm_rows(values):
    scale_rows = lax.rsqrt(jnp.mean(values * values, axis=-1, keepdims=True) + EPS)
    return (values * scale_rows, scale_rows)


def norm_back(grad_normed, normed, scale_rows):
    return scale_rows * (
        grad_normed - normed * jnp.mean(grad_normed * normed, axis=-1, keepdims=True)
    )


def tie(*values):
    return lax.optimization_barrier(values)


def waits(after):
    return list(after), [pl.BlockSpec(memory_space=pl.ANY)] * len(after)


def in_hbm(x):
    return pltpu.with_memory_space_constraint(x, pltpu.HBM)


def ring_order(chips):
    if chips % 8:
        return list(range(chips))
    rows, cols = 4, chips // 4
    if cols % 2 or cols < 4:
        path = list(range(cols))
    else:
        path = list(range(cols // 2)) + list(range(cols - 1, cols // 2 - 1, -1))
    walk = []
    for row in range(rows):
        across = range(1, cols) if row % 2 == 0 else range(cols - 1, 0, -1)
        walk += [(row, col) for col in across]
    walk = [(0, 0)] + walk + [(row, 0) for row in range(rows - 1, 0, -1)]
    return [row * cols + path[col] for row, col in walk]


class Ring:
    def __init__(self, devices):
        self.devices = devices
        self.chips = devices // 2
        order = ring_order(self.chips)
        self.order = order
        size = self.chips
        self.up = [
            (2 * order[i] + core, 2 * order[(i + 1) % size] + core)
            for i in range(size)
            for core in range(2)
        ]
        self.down = [(b, a) for a, b in self.up]
        self.swap = [(i, i ^ 1) for i in range(devices)]
        place = [0] * size
        for i, chip in enumerate(order):
            place[chip] = i
        index = lax.axis_index("cp")
        self.core = index % 2
        self.here = jnp.asarray(place, jnp.int32)[index // 2]
        self.half = size // 2
        table = [
            [order[(place[chip] + i) % size] for i in range(size)] + [core]
            for chip in range(size)
            for core in range(2)
        ]
        self.table = lax.dynamic_index_in_dim(
            jnp.asarray(table, jnp.int32), index, 0, keepdims=False
        )

    def send_up(self, x):
        return lax.ppermute(x, "cp", self.up)

    def send_down(self, x):
        return lax.ppermute(x, "cp", self.down)

    def sibling(self, x):
        return lax.ppermute(x, "cp", self.swap)


def products(table, lefts, rights, chips, packed, row, column, before, after=(), price=0, thirds=1, halved=True):
    tokens = lefts[0].shape[0]
    high = lefts[0].shape[1] // thirds // (2 if halved else 1)
    rows = high // chips
    wide = rights[0].shape[1]
    tile = min(wide, 512)
    last = table.shape[0] - 1
    more_args, more_specs = waits(after)
    if before is not None:
        more_args, more_specs = [before] + more_args, [pl.BlockSpec(memory_space=pl.ANY)] + more_specs
    side = len(lefts)

    def kernel(table_ref, *refs):
        out, token, turned = refs[side + len(rights) + len(more_args) :]

        @pl.when(pl.program_id(1) == 0)
        def _():
            for i in range(side):
                turned[:, i * tokens : (i + 1) * tokens] = refs[i][...].T
            token[...] = jnp.zeros_like(token)

        total, start = 0.0, 0
        for right in refs[side : side + len(rights)]:
            stop = start + right.shape[0]
            total = total + nn(turned[:, start:stop], right[...])
            start = stop
        out[...] = total.reshape(chips, rows, tile).astype(BF)

    def left_place(j, i, t):
        return (0, 2 * j + t[last] if halved else j)

    across = packed[1] // tile

    def out_place(j, i, t):
        at = column // tile + i
        return (0, row // rows + j + at // across, at % across)

    shape = jax.ShapeDtypeStruct((chips, *packed), BF)
    return pl.pallas_call(
        kernel,
        out_shape=[shape, TOKEN],
        grid_spec=pltpu.PrefetchScalarGridSpec(
            num_scalar_prefetch=1,
            grid=(thirds, wide // tile),
            in_specs=[pl.BlockSpec((tokens, high), left_place)] * side
            + [pl.BlockSpec((right.shape[0], tile), lambda j, i, t: (0, i)) for right in rights]
            + more_specs,
            out_specs=[
                pl.BlockSpec((chips, rows, tile), out_place),
                pl.BlockSpec((8, 128), lambda j, i, t: (0, 0)),
            ],
            scratch_shapes=[pltpu.VMEM((high, side * tokens), BF)],
        ),
        input_output_aliases={} if before is None else {1 + side + len(rights): 0},
        compiler_params=pltpu.CompilerParams(vmem_limit_bytes=VMEM_LIMIT),
        cost_estimate=cost(price),
    )(table, *lefts, *rights, *more_args)


class Gradients:
    def __init__(self, ring, rows, columns, outs):
        self.ring, self.rows, self.columns, self.outs = ring, rows, columns, outs
        self.cut = -(-rows // 32) * 16
        self.packed = None

    def shards(self, offsets, received, halves, after=()):
        ring, columns, rows, cut = self.ring, self.columns, self.rows, self.cut
        spans = [(0, cut), (cut, rows)]
        sides = len(offsets)
        args = [self.packed] * sides
        specs = [
            pl.BlockSpec((1, rows, columns), lambda i, t, at=offset: (t[at % ring.chips], 0, 0))
            for offset in offsets
        ]
        args += received
        specs += [pl.BlockSpec(x.shape, lambda i, t: (0, 0)) for x in received]
        more_args, more_specs = waits(after)
        taken = len(args) + len(more_args)

        def kernel(table_ref, *refs):
            outs = refs[taken:]
            outs[-1][...] = jnp.zeros_like(outs[-1])
            gained = refs[sides : len(args)]
            for side in range(sides):
                mine = refs[side]
                if halves == "send":
                    for out, (start, stop) in zip(outs, spans):
                        out[...] = mine[0, start:stop]
                elif halves == "add":
                    for got, (start, stop) in zip([gained[side]], [spans[side]]):
                        outs[side][start:stop] = (
                            mine[0, start:stop].astype(F32) + got[...].astype(F32)
                        ).astype(BF)
                    start, stop = spans[1 - side]
                    outs[side][start:stop] = mine[0, start:stop]
                else:
                    total = mine[0].astype(F32)
                    for got in gained if halves == "sum" else [gained[side]]:
                        total = total + got[...].astype(F32)
                    outs[side][...] = total.astype(BF)

        highs = {"send": [cut, rows - cut], "sum": [rows]}.get(halves, [rows, rows])
        return pl.pallas_call(
            kernel,
            out_shape=[jax.ShapeDtypeStruct((high, columns), BF) for high in highs] + [TOKEN],
            grid_spec=pltpu.PrefetchScalarGridSpec(
                num_scalar_prefetch=1,
                grid=(1,),
                in_specs=specs + more_specs,
                out_specs=[pl.BlockSpec((high, columns), lambda i, t: (0, 0)) for high in highs]
                + [pl.BlockSpec((8, 128), lambda i, t: (0, 0))],
            ),
            compiler_params=pltpu.CompilerParams(vmem_limit_bytes=VMEM_LIMIT),
            cost_estimate=LIGHT,
        )(ring.table, *args, *more_args)

    def scatter(self, after=()):
        ring = self.ring
        up, down, token = self.shards([ring.half], [], "send", after)
        for step in range(ring.half - 1, -1, -1):
            (up, down), after = yield (ring.send_up(up), ring.send_down(down)), token
            if step:
                kind = "add" if step == ring.half - 1 else ""
                up, down, token = self.shards([step, -step], [up, down], kind, after)
        yield self.shards([0], [up, down], "sum", after)

    def gather(self, own):
        ring, cut = self.ring, self.cut
        up = down = own
        ready = [(0, own)]
        for step in range(1, ring.half):
            up, down = yield (ring.send_up(up), ring.send_down(down)), ready
            ready = [(-step, up), (step, down)]
        high, low = yield (ring.send_up(up[:cut]), ring.send_down(down[cut:])), ready
        yield None, [(ring.half, jnp.concatenate([high, low], axis=0))]

    def unpack_stack(self, stack, offsets, before, after=(), price=0):
        return self.unpack(
            [(offset, stack, True) for offset in offsets], before, after, price, True
        )

    def unpack(self, ready, before, after=(), price=0, stacked=False):
        ring, outs = self.ring, self.outs
        count = len(ready)
        args = [ready[0][1]] if stacked else [part for _, part, _ in ready]
        places_of = [(offset, other) for offset, _, other in ready]

        def write(part, results):
            for out, (_, _, _, moves) in zip(results, outs):
                for where, rows, columns in moves:
                    out[where] = part[rows, columns].astype(F32)

        def kernel(table_ref, *refs):
            step = pl.program_id(0)
            results = refs[-len(outs) - 1 : -1]
            refs[-1][...] = jnp.zeros_like(refs[-1])
            if stacked:
                write(refs[0].at[0], results)
                return
            for i in range(count):
                pl.when(step == i)(functools.partial(write, refs[i], results))

        def place(of_chip, i, table):
            chip, core = None, None
            for j, (offset, other) in enumerate(places_of):
                here = table[offset % ring.chips]
                mine = table[ring.chips]
                mine = 1 - mine if other else mine
                chip = here if chip is None else jnp.where(i == j, here, chip)
                core = mine if core is None else jnp.where(i == j, mine, core)
            return of_chip(chip, core)

        shapes, out_specs = [], []
        for shape, block, of_chip, _ in outs:
            shapes.append(pltpu.HBM(shape, F32))
            out_specs.append(pl.BlockSpec(block, functools.partial(place, of_chip)))
        shapes.append(TOKEN)
        out_specs.append(pl.BlockSpec((8, 128), lambda i, t: (0, 0)))
        if stacked:
            specs = [pl.BlockSpec((1, self.rows, self.columns), lambda i, t: (i, 0, 0))]
        else:
            specs = [pl.BlockSpec((self.rows, self.columns), lambda i, t: (0, 0))] * count
        aliases = {}
        if before is not None:
            aliases = {1 + len(args) + i: i for i in range(len(outs))}
            specs += [pl.BlockSpec(memory_space=pl.ANY)] * len(outs)
            args += [in_hbm(x) for x in before[: len(outs)]]
        more_args, more_specs = waits(after)
        args += more_args
        specs += more_specs
        return list(
            pl.pallas_call(
                kernel,
                out_shape=shapes,
                grid_spec=pltpu.PrefetchScalarGridSpec(
                    num_scalar_prefetch=1, grid=(count,), in_specs=specs, out_specs=out_specs
                ),
                input_output_aliases=aliases,
                compiler_params=pltpu.CompilerParams(vmem_limit_bytes=VMEM_LIMIT),
                cost_estimate=cost(price),
            )(ring.table, *args)
        )


def stack(parts, after=()):
    rows, columns = parts[0].shape
    count = len(parts)
    more_args, more_specs = waits(after)

    def kernel(*refs):
        token, semaphores = refs[-2], refs[-1]
        token[...] = jnp.zeros_like(token)
        out = refs[-3]
        copies = [
            pltpu.make_async_copy(refs[i], out.at[i], semaphores.at[i]) for i in range(count)
        ]
        for copy in copies:
            copy.start()
        for copy in copies:
            copy.wait()

    return pl.pallas_call(
        kernel,
        out_shape=[jax.ShapeDtypeStruct((count, rows, columns), parts[0].dtype), TOKEN],
        in_specs=[pl.BlockSpec(memory_space=pl.ANY)] * count + more_specs,
        out_specs=[pl.BlockSpec(memory_space=pl.ANY), pl.BlockSpec(memory_space=pltpu.VMEM)],
        scratch_shapes=[pltpu.SemaphoreType.DMA((count,))],
        compiler_params=pltpu.CompilerParams(vmem_limit_bytes=VMEM_LIMIT),
        cost_estimate=LIGHT,
    )(*parts, *more_args)


def pair_add(own, received, half, after=()):
    more_args, more_specs = waits(after)

    def kernel(*refs):
        refs, outs = refs[:4], refs[4 + len(more_args) :]
        outs[-1][...] = jnp.zeros_like(outs[-1])
        for side in range(2):
            mine, got, out = refs[side], refs[2 + side], outs[side]
            if half:
                rows = got.shape[0]
                here = slice(side * rows, (side + 1) * rows)
                rest = slice((1 - side) * rows, (2 - side) * rows)
                out[here] = (mine[here].astype(F32) + got[...].astype(F32)).astype(BF)
                out[rest] = mine[rest]
            else:
                out[...] = (mine[...].astype(F32) + got[...].astype(F32)).astype(BF)

    shape = jax.ShapeDtypeStruct(own[0].shape, BF)
    return pl.pallas_call(
        kernel,
        out_shape=[shape, shape, TOKEN],
        in_specs=[pl.BlockSpec(memory_space=pltpu.VMEM)] * 4 + more_specs,
        compiler_params=pltpu.CompilerParams(vmem_limit_bytes=VMEM_LIMIT),
        cost_estimate=LIGHT,
    )(*own, *received, *more_args)


class SmallSum:
    def __init__(self, devices, x):
        self.devices, self.bit, self.total = devices, 1, x
        self.under_way = []
        self.send()

    def send(self):
        pairs = [(i, i ^ self.bit) for i in range(self.devices)]
        self.under_way = [lax.ppermute(self.total, "cp", pairs)] if self.bit < self.devices else []
        self.bit *= 2

    def came(self, arrived):
        if arrived:
            self.total = self.total + arrived[0]
            self.send()


def partner(x):
    return lax.ppermute(x, "tp", [(0, 1), (1, 0)])


def both(mine, other):
    return mine.astype(F32) + other.astype(F32)


def turn(values, cosine, sine):
    return values * cosine + pltpu.roll(values, values.shape[-1] // 2, 1) * sine


def turn_back(values, cosine, sine):
    return values * cosine - pltpu.roll(values, values.shape[-1] // 2, 1) * sine


def lower_first(order, table, other):
    core = table[table.shape[0] - 1]
    device = 2 * table[0] + (1 - core if other else core)
    return order[2 * device] < order[2 * device + 1]


def key_value_kernel(order, table, residuals, gain, key_weight, value_weight, key_gain, angles, outs):
    residual_out, normed_outs, raw_outs, cosine_outs, sine_outs, packed_outs = outs
    width = key_gain.shape[1]
    span = residuals[0].shape[0] // 2
    for pair in range(2):
        start = jnp.where(lower_first(order, table, pair == 1), 0, span)

        def canonical(ref):
            return jnp.concatenate(
                [
                    ref[pl.ds(pl.multiple_of(start, span), span)],
                    ref[pl.ds(pl.multiple_of(span - start, span), span)],
                ],
                axis=0,
            )

        rows = canonical(residuals[pair])
        if pair == 0:
            residual_out[...] = rows
        unit, _ = norm_rows(rows.astype(F32))
        normed = (unit * gain[...]).astype(BF)
        normed_outs[pair][...] = normed
        cosine, sine = canonical(angles[2 * pair]), canonical(angles[2 * pair + 1])
        cosine_outs[pair][...], sine_outs[pair][...] = cosine, sine
        raw = nn(normed, key_weight[...])
        raw_outs[pair][...] = raw
        values = nn(normed, value_weight[...]).astype(BF)
        for group in range(raw.shape[1] // width):
            here = slice(group * width, (group + 1) * width)
            key_unit, _ = norm_rows(raw[:, here])
            packed = packed_outs[pair]
            packed[:, 2 * group * width : (2 * group + 1) * width] = turn(
                key_unit * key_gain[...], cosine, sine
            ).astype(BF)
            packed[:, (2 * group + 1) * width : (2 * group + 2) * width] = values[:, here]


def query_kernel(normeds, weight, gain, cosines, sines, raw_outs, low_outs):
    width = gain.shape[1]
    for pair in range(2):
        raw = nn(normeds[pair][...], weight[...])
        raw_outs[pair][...] = raw
        for head in range(raw.shape[1] // width):
            here = slice(head * width, (head + 1) * width)
            unit, _ = norm_rows(raw[:, here])
            low_outs[pair][:, here] = turn(
                unit * gain[...], cosines[pair][...], sines[pair][...]
            ).astype(BF)


def heads_back(grad_of, raws, gain, cosines, sines, out, total):
    width = gain.shape[1]
    rows = raws[0].shape[0]
    for pair in range(2):
        here_rows = slice(pair * rows, (pair + 1) * rows)
        for head in range(raws[pair].shape[1] // width):
            here = slice(head * width, (head + 1) * width)
            unit, scale_rows = norm_rows(raws[pair][:, here])
            turned = turn_back(grad_of(pair, head), cosines[pair][...], sines[pair][...])
            total = total + jnp.sum((turned * unit).reshape(-1, 8, width), axis=0)
            out[here_rows, here] = norm_back(turned * gain[...], unit, scale_rows).astype(BF)
    return total


def query_back_kernel(grads, raws, gain, cosines, sines, low_out, gain_out):
    width = gain.shape[1]
    gain_out[...] = heads_back(
        lambda pair, head: grads[pair][:, head * width : (head + 1) * width],
        raws, gain, cosines, sines, low_out, jnp.zeros((8, width), F32),
    )


def key_value_back_kernel(owns, upward, downward, raws, gain, cosines, sines, low_out, gain_out):
    width = gain.shape[1]
    rows, columns = raws[0].shape
    groups = columns // width

    def summed(pair, place):
        here = slice(place * width, (place + 1) * width)
        at = slice(pair * rows, (pair + 1) * rows)
        return (
            owns[pair][:, here].astype(F32)
            + upward[at, here].astype(F32)
            + downward[at, here].astype(F32)
        )

    gain_out[...] = heads_back(
        lambda pair, head: summed(pair, 2 * head),
        raws, gain, cosines, sines, low_out, jnp.zeros((8, width), F32),
    )
    for pair in range(2):
        for group in range(groups):
            low_out[
                pair * rows : (pair + 1) * rows,
                columns + group * width : columns + (group + 1) * width,
            ] = summed(pair, 2 * group + 1).astype(BF)


def whole_call(kernel, scalars, outs, args, after=()):
    more_args, more_specs = waits(after)
    count = len(scalars)
    arrays, specs = [], []
    for arg in args:
        array, block, place = arg if isinstance(arg, tuple) else (arg, arg.shape, None)
        arrays.append(array)
        if place is None:
            specs.append(pl.BlockSpec(block, lambda i, *t: (0, 0)))
        else:
            specs.append(
                pl.BlockSpec(
                    block, lambda i, *t, place=place: place(t[-1][t[-1].shape[0] - 1])
                )
            )
    taken = count + len(args)

    def run(*refs):
        kernel(*refs[:taken], *refs[taken + len(more_args) :])

    return list(
        pl.pallas_call(
            run,
            out_shape=[
                pltpu.HBM(shape, dtype) if far else jax.ShapeDtypeStruct(shape, dtype)
                for shape, dtype, *far in outs
            ],
            grid_spec=pltpu.PrefetchScalarGridSpec(
                num_scalar_prefetch=count,
                grid=(1,),
                in_specs=specs + more_specs,
                out_specs=[pl.BlockSpec(shape, lambda i, *t: (0, 0)) for shape, *_ in outs],
            ),
            compiler_params=pltpu.CompilerParams(vmem_limit_bytes=VMEM_LIMIT),
            cost_estimate=LIGHT,
        )(*scalars, *arrays, *more_args)
    )


def matmul(left, right, after=()):
    rows, inner = left.shape
    columns = right.shape[1]
    tile = min(columns, 512)
    more_args, more_specs = waits(after)

    def kernel(left_ref, right_ref, *refs):
        refs[-1][...] = nn(left_ref[...], right_ref[...]).astype(BF)

    return pl.pallas_call(
        kernel,
        out_shape=jax.ShapeDtypeStruct((rows, columns), BF),
        grid=(columns // tile,),
        in_specs=[
            pl.BlockSpec((rows, inner), lambda i: (0, 0)),
            pl.BlockSpec((inner, tile), lambda i: (0, i)),
        ]
        + more_specs,
        out_specs=pl.BlockSpec((rows, tile), lambda i: (0, i)),
        compiler_params=pltpu.CompilerParams(vmem_limit_bytes=VMEM_LIMIT),
        cost_estimate=LIGHT,
    )(left, in_hbm(right), *more_args)


def out_projection(table, keep, other, weight):
    rows, inner = keep.shape
    columns = weight.shape[1]
    tile = columns
    last = table.shape[0] - 1

    def kernel(table_ref, keep_ref, other_ref, mine, theirs, out):
        out[...] = (nn(keep_ref[...], mine[...]) + nn(other_ref[...], theirs[...])).astype(BF)

    return pl.pallas_call(
        kernel,
        out_shape=jax.ShapeDtypeStruct((rows, columns), BF),
        grid_spec=pltpu.PrefetchScalarGridSpec(
            num_scalar_prefetch=1,
            grid=(columns // tile,),
            in_specs=[
                pl.BlockSpec((rows, inner), lambda i, t: (0, 0)),
                pl.BlockSpec((rows, inner), lambda i, t: (0, 0)),
                pl.BlockSpec((inner, tile), lambda i, t: (t[last], i)),
                pl.BlockSpec((inner, tile), lambda i, t: (1 - t[last], i)),
            ],
            out_specs=pl.BlockSpec((rows, tile), lambda i, t: (0, i)),
        ),
        compiler_params=pltpu.CompilerParams(vmem_limit_bytes=VMEM_LIMIT),
        cost_estimate=LIGHT,
    )(table, keep, other, in_hbm(weight), in_hbm(weight))


def heads_products(table, rows, weight, after=()):
    high, columns = rows[0].shape
    inner = weight.shape[0] // 2
    tile = min(inner, 256)
    count = inner // tile
    last = table.shape[0] - 1
    more_args, more_specs = waits(after)

    def kernel(table_ref, first, second, mine, *refs):
        refs[-2][...] = nt(first[...], mine[...]).astype(BF)
        refs[-1][...] = nt(second[...], mine[...]).astype(BF)

    shape = jax.ShapeDtypeStruct((high, inner), BF)
    spec = pl.BlockSpec((high, tile), lambda i, t: (0, i))
    whole = pl.BlockSpec((high, columns), lambda i, t: (0, 0))
    return pl.pallas_call(
        kernel,
        out_shape=[shape, shape],
        grid_spec=pltpu.PrefetchScalarGridSpec(
            num_scalar_prefetch=1,
            grid=(count,),
            in_specs=[
                whole,
                whole,
                pl.BlockSpec((tile, columns), lambda i, t: (t[last] * count + i, 0)),
            ]
            + more_specs,
            out_specs=[spec, spec],
        ),
        compiler_params=pltpu.CompilerParams(vmem_limit_bytes=VMEM_LIMIT),
        cost_estimate=LIGHT,
    )(table, *rows, in_hbm(weight), *more_args)


def normed_products(table, query_grad, key_value_grad, query_weight, key_weight, value_weight, after=()):
    rows, wide = query_grad.shape
    narrow = key_value_grad.shape[1] // 2
    columns = query_weight.shape[0]
    tile = min(columns, 256)
    last = table.shape[0] - 1
    more_args, more_specs = waits(after)

    def kernel(table_ref, queries, others, query, key, value, *refs):
        total = (
            nt(queries[...], query[...])
            + nt(others[:, :narrow], key[...])
            + nt(others[:, narrow:], value[...])
        ).astype(BF)
        refs[-2][...] = total[: rows // 2]
        refs[-1][...] = total[rows // 2 :]

    shape = jax.ShapeDtypeStruct((rows // 2, columns), BF)
    spec = pl.BlockSpec((rows // 2, tile), lambda i, t: (0, i))
    return pl.pallas_call(
        kernel,
        out_shape=[shape, shape],
        grid_spec=pltpu.PrefetchScalarGridSpec(
            num_scalar_prefetch=1,
            grid=(columns // tile,),
            in_specs=[
                pl.BlockSpec((rows, wide), lambda i, t: (0, 0)),
                pl.BlockSpec((rows, 2 * narrow), lambda i, t: (0, 0)),
                pl.BlockSpec((tile, wide), lambda i, t: (i, t[last])),
                pl.BlockSpec((tile, narrow), lambda i, t: (i, t[last])),
                pl.BlockSpec((tile, narrow), lambda i, t: (i, t[last])),
            ]
            + more_specs,
            out_specs=[spec, spec],
        ),
        compiler_params=pltpu.CompilerParams(vmem_limit_bytes=VMEM_LIMIT),
        cost_estimate=cost(HEAVY),
    )(
        table, query_grad, key_value_grad, in_hbm(query_weight), in_hbm(key_weight),
        in_hbm(value_weight), *more_args,
    )


def stacked(ref, start, span, width):
    rows = pl.ds(start, span)
    return jnp.concatenate([ref[rows, :width], ref[rows, width:]], axis=0)


def causal(span, transposed):
    shape = (span, 2 * span) if transposed else (2 * span, span)
    key = lax.broadcasted_iota(jnp.int32, shape, 0 if transposed else 1)
    row = lax.broadcasted_iota(jnp.int32, shape, 1 if transposed else 0)
    return key <= row % span


def side_met(order, table, pair, offset, other):
    last = table.shape[0] - 1
    core = table[last]

    def lower(device):
        return jnp.minimum(order[2 * device], order[2 * device + 1])

    mine = lower(2 * table[0] + (1 - core if pair else core))
    theirs = lower(2 * table[offset % last] + (1 - core if other else core))
    return jnp.where(theirs < mine, 0, 1)


def forward_kernel(places, own, last, span, width, order, table, *refs):
    count = len(places)
    queries, blocks, refs = refs[:2], refs[2 : 2 + count], refs[2 + count :]
    scale = LOG2E / math.sqrt(width)
    if own:
        before, outs = None, refs
    else:
        before, outs = refs[0], refs[1:]
    accum = outs[-1]
    ones = jnp.ones((span, width), BF)

    def weighted(rows, keys, values, allowed=None):
        scores = nt(rows, keys)
        probs = jnp.exp2(scores * scale)
        if allowed is not None:
            probs = jnp.where(allowed, probs, 0.0)
        return nn(probs.astype(BF), values)

    def extended(block, start):
        return jnp.concatenate([block[pl.ds(start, span), width:], ones], axis=1)

    keys = jnp.concatenate([block[:span, :width] for block in blocks], axis=0)
    values = jnp.concatenate([extended(block, 0) for block in blocks], axis=0)
    rows = jnp.concatenate([stacked(query, span, span, width) for query in queries], axis=0)
    high = weighted(rows, keys, values)
    for pair in range(2):
        part = high[pair * 2 * span : (pair + 1) * 2 * span]
        if own:
            allowed = causal(span, False)
            for side in range(2):
                block, start = blocks[pair], side * span
                met = weighted(
                    stacked(queries[pair], start, span, width),
                    block[start : start + span, :width],
                    extended(block, start),
                    allowed,
                )
                accum[0, pair, side] = met + part if side else met
        else:
            accum[0, pair, 0] = before[0, pair, 0]
            accum[0, pair, 1] = before[0, pair, 1] + part
    for i, (offset, other) in enumerate(places):
        for pair in range(2):
            if own and i == pair:
                continue
            side = side_met(order, table, pair, offset, other)
            start = pl.multiple_of(side * span, span)
            accum[0, pair, side] += weighted(
                stacked(queries[pair], start, span, width),
                blocks[i][pl.ds(start, span), :width],
                extended(blocks[i], start),
            )
    if last:
        wides, lows, logs = outs[0:2], outs[2:4], outs[4]
        for pair in range(2):
            for side in range(2):
                rows = slice(side * span, (side + 1) * span)
                whole = accum[0, pair, side]
                mass = whole[:, width:]
                out = whole[:, :width] / mass
                for head in range(2):
                    part = out[head * span : (head + 1) * span]
                    columns = slice(head * width, (head + 1) * width)
                    wides[pair][rows, columns] = part
                    lows[pair][rows, columns] = part.astype(BF)
                logs[0, pair, side] = jnp.log2(mass).T[:8]


def attention_forward(scalars, queries, blocks, places, before, own, last, after=()):
    rows, columns = queries[0].shape
    span, width = rows // 2, HEAD
    groups = columns // (2 * width)
    tile = pl.BlockSpec((rows, 2 * width), lambda g: (0, g))
    accum_block = (1, 2, 2, 2 * span, 2 * width)
    accum_spec = pl.BlockSpec(accum_block, lambda g: (g, 0, 0, 0, 0))
    args = [*scalars, *queries, *(in_hbm(block) for block in blocks)]
    specs = [pl.BlockSpec(memory_space=pltpu.SMEM)] * 2 + [tile] * (2 + len(blocks))
    if not own:
        args.append(before)
        specs.append(accum_spec)
    taken = len(args)
    more_args, more_specs = waits(after)
    scratch = []
    if last:
        wide, low = pltpu.HBM((rows, columns), F32), jax.ShapeDtypeStruct((rows, columns), BF)
        outs = [wide, wide, low, low, jax.ShapeDtypeStruct((groups, 2, 2, 8, 2 * span), F32)]
        out_specs = [tile] * 4 + [pl.BlockSpec((1, 2, 2, 8, 2 * span), lambda g: (g, 0, 0, 0, 0))]
        scratch = [pltpu.VMEM(accum_block, F32)]
    else:
        outs = [jax.ShapeDtypeStruct((groups, *accum_block[1:]), F32)]
        out_specs = [accum_spec]

    def kernel(*refs):
        refs = refs[:taken] + refs[taken + len(more_args) :]
        forward_kernel(places, own, last, span, width, *refs)

    return pl.pallas_call(
        kernel,
        out_shape=outs,
        grid=(groups,),
        in_specs=specs + more_specs,
        out_specs=out_specs,
        scratch_shapes=scratch,
        input_output_aliases={} if own or last else {taken - 1: 0},
        compiler_params=pltpu.CompilerParams(vmem_limit_bytes=VMEM_LIMIT),
        cost_estimate=FORWARD,
    )(*args, *more_args)


def delta_kernel(grads, outs, delta):
    for pair in range(2):
        grad, out = grads[pair], outs[pair]
        width, span = grad.shape[1] // 2, grad.shape[0] // 2
        for side in range(2):
            rows = slice(side * span, (side + 1) * span)
            product = grad[rows, :].astype(F32) * out[rows, :]
            stack = jnp.concatenate([product[:, :width], product[:, width:]], axis=0)
            total = jnp.sum(stack.T, axis=0, keepdims=True)
            delta[0, pair, side] = jnp.broadcast_to(total, (8, 2 * span))


def attention_delta(grads, outs, after=()):
    rows, columns = grads[0].shape
    width, span = HEAD, rows // 2
    groups = columns // (2 * width)
    tile = pl.BlockSpec((rows, 2 * width), lambda g: (0, g))
    more_args, more_specs = waits(after)

    def kernel(*refs):
        delta_kernel(refs[:2], refs[2:4], refs[-1])

    return pl.pallas_call(
        kernel,
        out_shape=jax.ShapeDtypeStruct((groups, 2, 2, 8, 2 * span), F32),
        grid=(groups,),
        in_specs=[tile] * 4 + more_specs,
        out_specs=pl.BlockSpec((1, 2, 2, 8, 2 * span), lambda g: (g, 0, 0, 0, 0)),
        compiler_params=pltpu.CompilerParams(vmem_limit_bytes=VMEM_LIMIT),
        cost_estimate=LIGHT,
    )(*grads, *outs, *more_args)


def backward_kernel(places, own, first, last, split, span, width, order, table, *refs):
    count = len(places)
    queries, grads, (logs, delta), refs = refs[:2], refs[2:4], refs[4:6], refs[6:]
    blocks, refs = refs[:count], refs[count:]
    if not first:
        before, refs = refs[0], refs[1:]
    outs = refs[: count if split else count // 2]
    refs = refs[len(outs) :]
    refs[0][...] = jnp.zeros_like(refs[0])
    refs = refs[1:]
    if last:
        query_outs, accum = refs[:2], refs[2]
    else:
        accum = refs[0]
    scale = LOG2E / math.sqrt(width)
    factor = 1.0 / math.sqrt(width)

    def products(rows, row_grads, log, mean, keys, values, allowed=None):
        probs = jnp.exp2(nt(keys, rows) * scale - log)
        if allowed is not None:
            probs = jnp.where(allowed, probs, 0.0)
        prob_grad = nt(values, row_grads)
        score_grad = (probs * (prob_grad - mean)).astype(BF)
        return nn(score_grad, rows), nn(probs.astype(BF), row_grads), tn(keys, score_grad)

    def of_pair(pair, side, start, keys, values, allowed=None):
        return products(
            stacked(queries[pair], start, span, width),
            stacked(grads[pair], start, span, width),
            logs[0, pair, side, :1],
            delta[0, pair, side, :1],
            keys,
            values,
            allowed,
        )

    low_keys, low_values, high_query = products(
        jnp.concatenate([stacked(query, span, span, width) for query in queries], axis=0),
        jnp.concatenate([stacked(grad, span, span, width) for grad in grads], axis=0),
        jnp.concatenate([logs[0, pair, 1, :1] for pair in range(2)], axis=1),
        jnp.concatenate([delta[0, pair, 1, :1] for pair in range(2)], axis=1),
        jnp.concatenate([block[:span, :width] for block in blocks], axis=0),
        jnp.concatenate([block[:span, width:] for block in blocks], axis=0),
    )
    for pair in range(2):
        part = high_query[:, pair * 2 * span : (pair + 1) * 2 * span]
        if first:
            accum[0, pair, 0] = jnp.zeros_like(part)
            accum[0, pair, 1] = part
        else:
            accum[0, pair, 0] = before[0, pair, 0]
            accum[0, pair, 1] = before[0, pair, 1] + part
    for i, (offset, other) in enumerate(places):
        here = slice(i * span, (i + 1) * span)
        block = blocks[i]
        key_sums, value_sums = [low_keys[here], 0.0], [low_values[here], 0.0]
        for pair in range(2):
            if own and i == pair:
                allowed = causal(span, True)
                for side in range(2):
                    rows = slice(side * span, (side + 1) * span)
                    key_part, value_part, query_part = of_pair(
                        pair, side, side * span, block[rows, :width], block[rows, width:], allowed
                    )
                    accum[0, pair, side] += query_part
                    key_sums[side] = key_sums[side] + key_part
                    value_sums[side] = value_sums[side] + value_part
                continue
            side = side_met(order, table, pair, offset, other)
            start = pl.multiple_of(side * span, span)
            rows = pl.ds(start, span)
            key_part, value_part, query_part = of_pair(
                pair, side, start, block[rows, :width], block[rows, width:]
            )
            accum[0, pair, side] += query_part
            low = side == 0
            key_sums[0] = key_sums[0] + jnp.where(low, key_part, 0.0)
            value_sums[0] = value_sums[0] + jnp.where(low, value_part, 0.0)
            key_sums[1] = key_sums[1] + jnp.where(low, 0.0, key_part)
            value_sums[1] = value_sums[1] + jnp.where(low, 0.0, value_part)
        out = outs[i] if split else outs[i // 2]
        base = 0 if split else i % 2 * 2 * span
        for side in range(2):
            rows = slice(base + side * span, base + (side + 1) * span)
            out[rows, :width] = (key_sums[side] * factor).astype(BF)
            out[rows, width:] = value_sums[side].astype(BF)
    if last:
        for pair in range(2):
            for side in range(2):
                part = accum[0, pair, side].T * factor
                rows = slice(side * span, (side + 1) * span)
                query_outs[pair][rows, :width] = part[:span]
                query_outs[pair][rows, width:] = part[span:]


def attention_backward(
    scalars, queries, grads, logs, delta, blocks, places, before, own, last, split, after=()
):
    rows, columns = queries[0].shape
    span, width = rows // 2, HEAD
    groups = columns // (2 * width)
    count = len(blocks)
    first = before is None
    tile = pl.BlockSpec((rows, 2 * width), lambda g: (0, g))
    stat = pl.BlockSpec((1, 2, 2, 8, 2 * span), lambda g: (g, 0, 0, 0, 0))
    accum_block = (1, 2, 2, width, 2 * span)
    accum_spec = pl.BlockSpec(accum_block, lambda g: (g, 0, 0, 0, 0))
    args = [*scalars, *queries, *grads, logs, delta, *(in_hbm(block) for block in blocks)]
    specs = [pl.BlockSpec(memory_space=pltpu.SMEM)] * 2 + [tile] * 4 + [stat] * 2 + [tile] * count
    if not first:
        args.append(before)
        specs.append(accum_spec)
    taken = len(args)
    more_args, more_specs = waits(after)
    if split:
        outs = [jax.ShapeDtypeStruct((rows, columns), BF)] * count
        out_specs = [tile] * count
    else:
        outs = [jax.ShapeDtypeStruct((2 * rows, columns), BF)] * (count // 2)
        out_specs = [pl.BlockSpec((2 * rows, 2 * width), lambda g: (0, g))] * (count // 2)
    outs.append(TOKEN)
    out_specs.append(pl.BlockSpec((8, 128), lambda g: (0, 0)))
    scratch = []
    if last:
        outs += [jax.ShapeDtypeStruct((rows, columns), F32)] * 2
        out_specs += [tile] * 2
        scratch = [pltpu.VMEM(accum_block, F32)]
    else:
        outs.append(jax.ShapeDtypeStruct((groups, *accum_block[1:]), F32))
        out_specs.append(accum_spec)

    def kernel(*refs):
        refs = refs[:taken] + refs[taken + len(more_args) :]
        backward_kernel(places, own, first, last, split, span, width, *refs)

    return pl.pallas_call(
        kernel,
        out_shape=outs,
        grid=(groups,),
        in_specs=specs + more_specs,
        out_specs=out_specs,
        scratch_shapes=scratch,
        input_output_aliases={} if first or last else {taken - 1: len(outs) - 1},
        compiler_params=pltpu.CompilerParams(vmem_limit_bytes=VMEM_LIMIT),
        cost_estimate=cost(HEAVY),
    )(*args, *more_args)


def body(
    devices,
    residual,
    cotangent,
    span_order,
    positions,
    attn_gain,
    query_weight,
    key_weight,
    value_weight,
    query_gain,
    key_gain,
    out_weight,
    mlp_gain,
    gate_weight,
    up_weight,
    down_weight,
):
    ring = Ring(devices)
    rows, model = residual.shape
    head_dim = query_gain.shape[0]
    span = rows // 2
    index = lax.axis_index("cp")
    scalars = [span_order, ring.table]
    table = [ring.table]
    ordered = lax.dynamic_slice_in_dim(span_order, 2 * index, 2)
    in_order = ordered[0] < ordered[1]

    def canonical(x):
        return jnp.where(in_order, x, jnp.roll(x, span, axis=0))

    residual_other, positions_other = ring.sibling(residual), ring.sibling(positions)
    cotangent = canonical(cotangent)

    half = head_dim // 2
    freq = ROPE_BASE ** (-(jnp.arange(half, dtype=F32) * 2.0) / head_dim)
    angles = []
    for where in (positions, positions_other):
        angle = where.astype(F32)[:, None] * freq[None, :]
        cosine, sine = jnp.cos(angle), jnp.sin(angle)
        angles.append(jnp.concatenate([cosine, cosine], axis=1))
        angles.append(jnp.concatenate([-sine, sine], axis=1))

    query_gain_row = query_gain.reshape(1, -1)
    key_gain_row = key_gain.reshape(1, -1)
    key_columns = key_weight.shape[1]
    query_columns = query_weight.shape[1]
    few, each = key_columns // 2, query_columns // 2

    def project_keys(order, table_ref, first, second, gain, key, value, row, c0, s0, c1, s1, *outs):
        key_value_kernel(
            order, table_ref, (first, second), gain, key, value, row, (c0, s0, c1, s1),
            (outs[0], outs[1:3], outs[3:5], outs[5:7], outs[7:9], outs[9:11]),
        )

    residual, *results = whole_call(
        project_keys,
        scalars,
        [((rows, model), BF, 1)]
        + [((rows, model), BF)] * 2
        + [((rows, few), F32, 1)] * 2
        + [((rows, head_dim), F32)] * 4
        + [((rows, key_columns), BF)] * 2,
        [
            in_hbm(residual), residual_other, in_hbm(attn_gain.reshape(1, -1)),
            (in_hbm(key_weight), (model, few), lambda core: (0, core)),
            (in_hbm(value_weight), (model, few), lambda core: (0, core)),
            in_hbm(key_gain_row), *angles,
        ],
    )
    normeds, keys_raw, cosines, sines, parts = (results[i : i + 2] for i in range(0, 10, 2))

    ways = [(ring.send_up(part), ring.send_down(part)) for part in parts]

    def project_queries(table_ref, n0, n1, weight, gain, c0, c1, s0, s1, *outs):
        query_kernel((n0, n1), weight, gain, (c0, c1), (s0, s1), outs[:2], outs[2:])

    *queries_raw, first, second = whole_call(
        project_queries,
        table,
        [((rows, each), F32, 1)] * 2 + [((rows, each), BF)] * 2,
        [
            *normeds, (in_hbm(query_weight), (model, each), lambda core: (0, core)),
            in_hbm(query_gain_row), *cosines, *sines,
        ],
    )
    queries = [first, second]

    def places_of(offsets):
        return [(offset, other) for offset in offsets for other in (False, True)]

    steps = ring.half
    calls = {0: ([0], parts)}
    state = None
    for step in range(1, steps):
        come = []
        for which in range(2):
            up, down = ways[which]
            if step == 1 and which == 0:
                up, down, queries[0] = tie(up, down, queries[0])
            else:
                up, down, state = tie(up, down, state)
            come.append((up, down))
            if step < steps - 1:
                ways[which] = ring.send_up(up), ring.send_down(down)
            else:
                ways[which] = ring.send_down(down) if which else ring.send_up(up)
            if step == 1 and which == 0:
                (state,) = attention_forward(
                    scalars, queries, parts, places_of([0]), None, True, False, after=come[0]
                )
        blocks = [come[0][0], come[1][0], come[0][1], come[1][1]]
        calls[step] = ([-step, step], blocks)
        (state,) = attention_forward(
            scalars, queries, blocks, places_of([-step, step]), state, False, False
        )
    *ways, state = tie(*ways, state)
    calls[steps] = ([steps], ways)
    *attended, low_keep, low_give, logs = attention_forward(
        scalars, queries, ways, places_of([steps]), state, False, True
    )
    low_other = ring.sibling(low_give)
    mixed_part = out_projection(ring.table, low_keep, low_other, out_weight)
    mixed_part, cotangent = tie(mixed_part, cotangent)
    mixed_other = partner(mixed_part)
    cotangents = [cotangent, ring.sibling(cotangent)]
    hidden_grad = nt(cotangent, down_weight)
    mixed_other, hidden_grad, cotangents = tie(mixed_other, hidden_grad, cotangents)

    residual_wide = residual.astype(F32)
    mixed = residual_wide + both(mixed_part, mixed_other)
    normed_two, scale_two = norm_rows(mixed)
    normed_two_low = (normed_two * mlp_gain).astype(BF)
    gate = nn(normed_two_low, gate_weight)
    upward = nn(normed_two_low, up_weight)
    sigmoid_gate = jax.nn.sigmoid(gate)
    activated = gate * sigmoid_gate
    hidden_low = (activated * upward).astype(BF)
    gate_grad_low = (
        hidden_grad * upward * sigmoid_gate * (1.0 + gate * (1.0 - sigmoid_gate))
    ).astype(BF)
    up_grad_low = (hidden_grad * activated).astype(BF)
    normed_two_part = (nt(gate_grad_low, gate_weight) + nt(up_grad_low, up_weight)).astype(BF)
    normed_two_other = partner(normed_two_part)

    units = gate_weight.shape[1]
    thirds = 2 * units // model
    chips = ring.chips
    gate_rows = model // 2 // chips
    down_rows = units // thirds // 2 // chips
    out_row = thirds * gate_rows
    down_row = out_row + gate_rows
    packed_shape = (down_row + thirds * down_rows, model)

    def shard_of(chip, core):
        return core * chips + chip

    def columns_of(start):
        moves, done = [], 0
        while done < units:
            tile, column = divmod(start + done, model)
            wide = min(model - column, units - done)
            moves.append(
                (
                    (slice(None), slice(done, done + wide)),
                    slice(tile * gate_rows, (tile + 1) * gate_rows),
                    slice(column, column + wide),
                )
            )
            done += wide
        return moves

    everything = slice(None)
    wide = Gradients(
        ring,
        *packed_shape,
        [
            ((model, units), (gate_rows, units), lambda c, k: (shard_of(c, k), 0), columns_of(0)),
            ((model, units), (gate_rows, units), lambda c, k: (shard_of(c, k), 0), columns_of(units)),
            (
                (thirds, units // thirds, model),
                (thirds, down_rows, model),
                lambda c, k: (0, shard_of(c, k), 0),
                [
                    (i, slice(down_row + i * down_rows, down_row + (i + 1) * down_rows), everything)
                    for i in range(thirds)
                ],
            ),
            (
                (2 * each, model),
                (gate_rows, model),
                lambda c, k: (shard_of(c, k), 0),
                [((everything, everything), slice(out_row, out_row + gate_rows), everything)],
            ),
        ],
    )
    both_grad_low = jnp.concatenate([gate_grad_low, up_grad_low], axis=1)
    packed, token = products(
        ring.table, [normed_two_low, ring.sibling(normed_two_low)],
        [both_grad_low, ring.sibling(both_grad_low)], chips, packed_shape, 0, 0, None,
        [normed_two_part],
    )
    packed, token = products(
        ring.table, [hidden_low, ring.sibling(hidden_low)], cotangents, chips, packed_shape,
        down_row, 0, packed, [token], thirds=thirds,
    )
    normed_two_other, token = tie(normed_two_other, token)

    normed_two_grad = both(normed_two_part, normed_two_other)
    mlp_gain_term = jnp.sum(normed_two_grad * normed_two, axis=0)
    mixed_grad = cotangent.astype(F32) + norm_back(
        normed_two_grad * mlp_gain, normed_two, scale_two
    )
    mixed_grad_low = mixed_grad.astype(BF)
    mixed_grads = [mixed_grad_low, ring.sibling(mixed_grad_low)]
    wide.packed, token = products(
        ring.table, [low_keep, low_give], mixed_grads, chips, packed_shape, out_row, 0, packed,
        [token], halved=False,
    )
    wide_steps = wide.scatter()
    wide_way, wide_token = next(wide_steps)
    grads = heads_products(ring.table, mixed_grads, out_weight, [wide_token])
    delta = attention_delta(grads, attended)

    def backward(step, state, after):
        offsets, blocks = calls[step]
        last = step == 0
        return attention_backward(
            scalars, queries, grads, logs, delta, blocks, places_of(offsets), state,
            last, last, last or step == steps, after,
        )

    narrow_rows = model // chips
    narrow_shape = (narrow_rows, each + 2 * few)

    def narrow_out(start, wide):
        return (
            (model, 2 * wide),
            (narrow_rows, wide),
            lambda c, k: (c, k),
            [((everything, everything), everything, slice(start, start + wide))],
        )

    narrow = Gradients(
        ring,
        *narrow_shape,
        [narrow_out(0, each), narrow_out(each, few), narrow_out(each + few, few)],
    )
    up, down, token, state = backward(steps, None, [])
    up, down = ring.send_up(up), ring.send_down(down)
    for step in range(steps - 1, 0, -1):
        wide_way, wide_token = wide_steps.send((wide_way, [token]))
        if step == steps - 1:
            layer_part = matmul(hidden_low, down_weight, [wide_token])
            layer_other = partner(layer_part)
        if step == steps - 2:
            layer_other, wide_token = tie(layer_other, wide_token)
        back, front, token, state = backward(step, state, [wide_token])
        up, down, token = pair_add([front, back], [up, down], step == steps - 1, [token])
        up, down = ring.send_up(up), ring.send_down(down)
    wide_shard, wide_token = wide_steps.send((wide_way, [token]))
    wide_steps = wide.gather(wide_shard)
    wide_way, wide_ready = next(wide_steps)
    *key_value_own, token, first, second = backward(0, state, [wide_token])

    def back_queries(table_ref, g0, g1, r0, r1, gain, c0, c1, s0, s1, *outs):
        query_back_kernel((g0, g1), (r0, r1), gain, (c0, c1), (s0, s1), *outs)

    query_grad_low, query_gain_term = whole_call(
        back_queries,
        table,
        [((2 * rows, each), BF), ((8, head_dim), F32)],
        [first, second, *queries_raw, query_gain_row, *cosines, *sines],
    )
    packed, token = products(
        ring.table, normeds, [query_grad_low], chips, narrow_shape, 0, 0, None, halved=False
    )

    def own_ready(ready):
        return [(offset, part, False) for offset, part in ready]

    def other_ready(ready):
        return [(offset, ring.sibling(part), True) for offset, part in ready]

    wide_come = list(wide_ready)
    up, down, token = tie(up, down, token)

    def back_keys(table_ref, o0, o1, up_ref, down_ref, r0, r1, gain, c0, c1, s0, s1, *outs):
        key_value_back_kernel(
            (o0, o1), up_ref, down_ref, (r0, r1), gain, (c0, c1), (s0, s1), *outs
        )

    key_value_grad, key_gain_term = whole_call(
        back_keys,
        table,
        [((2 * rows, 2 * few), BF), ((8, head_dim), F32)],
        [*key_value_own, up, down, *keys_raw, key_gain_row, *cosines, *sines],
        after=[token],
    )
    narrow.packed, token = products(
        ring.table, normeds, [key_value_grad], chips, narrow_shape, 0, each, packed, halved=False
    )
    narrow_steps = narrow.scatter()
    narrow_way, token = next(narrow_steps)

    wide_way, token = tie(wide_way, token)
    wide_way, next_ready = wide_steps.send(wide_way)
    wide_ready = wide_ready + next_ready
    wide_come += next_ready
    narrow_way, token = narrow_steps.send((narrow_way, [token]))

    normed_own, normed_give = normed_products(
        ring.table, query_grad_low, key_value_grad, query_weight, key_weight, value_weight, [token]
    )
    normed_part = both(normed_own, ring.sibling(normed_give)).astype(BF)
    normed_other = partner(normed_part)
    gains = jnp.stack([jnp.sum(query_gain_term, axis=0), jnp.sum(key_gain_term, axis=0)])
    wide_results = wide.unpack(own_ready(wide_ready), None, [normed_give])

    narrow_way, token = narrow_steps.send((narrow_way, [wide_results[-1]]))
    wide_way, normed_other, token = tie(wide_way, normed_other, token)
    wide_way, wide_ready = wide_steps.send(wide_way)
    wide_come += wide_ready
    gains = gains + partner(gains)
    normed_one, scale_one = norm_rows(residual_wide)
    normed_grad = both(normed_part, normed_other)
    attn_gain_term = jnp.sum(normed_grad * normed_one, axis=0)
    residual_grad = canonical(
        mixed_grad + norm_back(normed_grad * attn_gain, normed_one, scale_one)
    )
    layer_out = canonical(mixed + both(layer_part, layer_other)).astype(BF)
    wide_results = wide.unpack(own_ready(wide_ready), wide_results, [token], HEAVY)

    small = SmallSum(
        devices,
        jnp.concatenate([attn_gain_term, mlp_gain_term, gains[0], gains[1]]).reshape(-1, 128),
    )
    for step in range(steps - 3):
        narrow_way, token = narrow_steps.send((narrow_way, [wide_results[-1]]))
        wide_way, came, token = tie(wide_way, small.under_way, token)
        wide_way, wide_ready = wide_steps.send(wide_way)
        wide_come += wide_ready
        small.came(came)
        wide_results = wide.unpack(own_ready(wide_ready), wide_results, [token], HEAVY)
    narrow_shard, token = narrow_steps.send((narrow_way, [wide_results[-1]]))

    narrow_steps = narrow.gather(narrow_shard)
    narrow_way, narrow_ready = next(narrow_steps)
    wide_way, came, token = tie(wide_way, small.under_way, token)
    small.came(came)
    _, wide_ready = wide_steps.send(wide_way)
    wide_come += wide_ready
    wide_results = wide.unpack(own_ready(wide_ready), wide_results, [token])
    lot, token = stack([part for _, part in wide_come], [wide_results[-1]])
    lot_offsets = [offset for offset, _ in wide_come]
    lot_other = ring.sibling(lot)
    narrow_results = None
    for step in range(1, steps + 1):
        ready = own_ready(narrow_ready) + other_ready(narrow_ready)
        narrow_results = narrow.unpack(ready, narrow_results, [token], HEAVY)
        narrow_way, came, residual_grad, layer_out, token = tie(
            narrow_way, small.under_way, residual_grad, layer_out, narrow_results[-1]
        )
        small.came(came)
        if step < steps:
            narrow_way, narrow_ready = narrow_steps.send(narrow_way)
        if step == steps - 2:
            wide_results = wide.unpack_stack(lot_other, lot_offsets, wide_results, [token])
            token = wide_results[-1]
    while small.under_way:
        small.came(small.under_way)
    _, narrow_ready = narrow_steps.send(narrow_way)
    ready = own_ready(narrow_ready) + other_ready(narrow_ready)
    query_sum, key_sum, value_sum, _ = narrow.unpack(
        ready, narrow_results, [token]
    )
    gate_sum, up_sum, down_sum, out_weight_sum, _ = wide_results
    small = small.total.reshape(-1)

    attn_gain_grad, mlp_gain_grad = small[:model], small[model : 2 * model]
    query_gain_grad = small[2 * model : 2 * model + head_dim]
    key_gain_grad = small[2 * model + head_dim :]
    return (
        layer_out,
        residual_grad,
        attn_gain_grad,
        query_sum,
        key_sum,
        value_sum,
        query_gain_grad,
        key_gain_grad,
        out_weight_sum,
        mlp_gain_grad,
        gate_sum,
        up_sum,
        down_sum.reshape(units, model),
    )


def solution(mesh):
    return jax.shard_map(
        functools.partial(body, mesh.shape["cp"]),
        mesh=mesh,
        in_specs=(
            P("cp", None),
            P("cp", None),
            P(),
            P("cp"),
            P(),
            P(None, "tp"),
            P(None, "tp"),
            P(None, "tp"),
            P(),
            P(),
            P("tp", None),
            P(),
            P(None, "tp"),
            P(None, "tp"),
            P("tp", None),
        ),
        out_specs=(
            P("cp", None),
            P("cp", None),
            P(),
            P(None, "tp"),
            P(None, "tp"),
            P(None, "tp"),
            P(),
            P(),
            P("tp", None),
            P(),
            P(None, "tp"),
            P(None, "tp"),
            P("tp", None),
        ),
        check_vma=False,
    )
```

time: 395 us -> 350 us (0.89)
  local copies, waits for them, and re-layouts: 46 us -> 12.3 us
  matrix products: 21.4 us -> 5.02 us
  Pallas kernels: 108 us -> 120 us
  waiting for transfers between devices: 124 us -> 115 us
    unnamed x216 -> x166, local copies, waits for them, and re-layouts: 38.3 us -> 7.41 us
    pallas_call x17 -> x27, Pallas kernels: 30.5 us -> 47.4 us  [the longest x5 13.3 us: products(): pl.pallas_call(kernel, out_shape=[shape, TOKEN], grid_spec=pltpu.Prefetch...]
    ppermute x27, waiting for transfers between devices: 31.8 us -> 18.8 us  [send_down(): return lax.ppermute(x, 'cp', self.down)]
    ppermute x27, starting transfers between devices: 31.3 us -> 19.6 us  [send_up(): return lax.ppermute(x, 'cp', self.up)]
    ppermute x27, starting transfers between devices: 27.4 us -> 37.5 us  [send_down(): return lax.ppermute(x, 'cp', self.down)]
    dot_general x5 -> x0, matrix products: 6.75 us -> none  [tn(): lax.dot_general(a, b, (((0,), (0,)), ((), ())), preferred_element_type=F32)]
    pallas_call x14 -> x10, Pallas kernels: 32.1 us -> 25.5 us  [unpack(): pl.pallas_call(kernel, out_shape=shapes, grid_spec=pltpu.PrefetchScalarGr...]
    dot_general x8 -> x3, matrix products: 9.6 us -> 3.06 us  [nt(): lax.dot_general(a, b, (((1,), (1,)), ((), ())), preferred_element_type=F32)]
  transfers between devices with their start and end apart: 90 -> 81, of which waited for: 40 -> 31; matrix products, arithmetic and copies ran while one was open for 7% -> 5% of each run, Pallas kernels for 24% -> 29%
where the time goes in v3:
time: 350 us; the launch traced here: 343 us
  Pallas kernels  120 us (34%)
  waiting for transfers between devices  115 us (33%)
  starting transfers between devices  72.7 us (21%)
  other arithmetic  14.1 us (4%)
  local copies, waits for them, and re-layouts  12.3 us (4%)
  matrix products  5.02 us (1%)
  between operations  3.53 us (1%)
    ppermute x27, waiting for transfers between devices, send_up(): return lax.ppermute(x, 'cp', self.up)  72.1 us
    ppermute x27, starting transfers between devices, send_down(): return lax.ppermute(x, 'cp', self.down)  37.5 us
    pallas_call x5, Pallas kernels, attention_backward(): pl.pallas_call(kernel, out_shape=outs, grid=(groups,), in_specs=specs + m...  27.2 us
    pallas_call x10, Pallas kernels, unpack(): pl.pallas_call(kernel, out_shape=shapes, grid_spec=pltpu.PrefetchScalarGr...  25.5 us
    ppermute x27, starting transfers between devices, send_up(): return lax.ppermute(x, 'cp', self.up)  19.6 us
    pallas_call x5, Pallas kernels, attention_forward(): pl.pallas_call(kernel, out_shape=outs, grid=(groups,), in_specs=specs + m...  19 us
    ppermute x27, waiting for transfers between devices, send_down(): return lax.ppermute(x, 'cp', self.down)  18.8 us
    ppermute x5, waiting for transfers between devices, partner(): return lax.ppermute(x, 'tp', [(0, 1), (1, 0)])  16.5 us
  transfers between devices with their start and end apart: 81, of which 31 were waited for; matrix products, arithmetic and copies ran while one was open for 5% of the time, Pallas kernels for 29%

profile of v3, /device:TPU:0, one launch (start us, length us, event | category | flops | bytes accessed | tf_op | source)
XLA Modules:
  0.0 342.6 jit_solution(6893964436500198768)
XLA Ops:
  4.9 3.9 %shard_map.255 = (bf16[256,1024]{1,0:T(8,128)(2,1)}, bf16[256,1024]{1,0:T(8,128)(2,1)S(1)}, bf16[256,1024]{1,0:T(8,128)(2,1)S(1)}, f32[256,256]{1,0:T(8,128)}, f...) custom-call(s32[32]{0:T(128)S(1)} %copy-done.42, ...), custom_call_target="tpu_custom_call" | custom-call | flops 1024 | bytes 1024 | tf_op jit(solution)/shard_map/pallas_call | solution.py:541
  8.9 3.1 collective-permute-start.3
  13.9 3.3 shard_map.256
  23.2 3.0 shard_map.257.refs_8_
  28.8 4.0 %shard_map.258.refs_8_ = f32[2,2,2,256,256]{4,3,2,1,0:T(8,128)S(1)} custom-call(s32[32]{0:T(128)S(1)} %copy-done.42, s32[9]{0:T(128)S(1)} %dynamic-slice_bitcast_fusion.refs_1_.refs_0_.table_ref, bf16[256,512]{1,0:T(8,128)(2,1)S(1)} %get-tuple-element.231.refs_2_, bf16[256,512]{1,0:T(8,128)(2,1)S(1)} %get-tuple-element.232.refs_3_, ...), custom_call_target="tpu_custom_call", output_to_operand_aliasing={{}: (8, {})} | custom-call | flops 1024 | bytes 1024 | tf_op jit(solution)/shard_map/pallas_call | solution.py:808
  34.9 3.1 collective-permute-done.10.refs_5_.refs_9_
  40.1 4.0 %shard_map.259.refs_8_ = f32[2,2,2,256,256]{4,3,2,1,0:T(8,128)S(1)} custom-call(s32[32]{0:T(128)S(1)} %copy-done.42, s32[9]{0:T(128)S(1)} %dynamic-slice_bitcast_fusion.refs_1_.refs_0_.table_ref, bf16[256,512]{1,0:T(8,128)(2,1)S(1)} %get-tuple-element.231.refs_2_, bf16[256,512]{1,0:T(8,128)(2,1)S(1)} %get-tuple-element.232.refs_3_, ...), custom_call_target="tpu_custom_call", output_to_operand_aliasing={{}: (8, {})} | custom-call | flops 1024 | bytes 1024 | tf_op jit(solution)/shard_map/pallas_call | solution.py:808
  45.5 3.7 %collective-permute-done.13.refs_5_.refs_9_ = bf16[256,512]{1,0:T(8,128)(2,1)S(1)} collective-permute-done((bf16[256,512]{1,0:T(8,128)(2,1)S(1)}, bf16[256,512]{1,0:T(8,128)(2,1)S(1)}, u32[]{:S(2)}, u32[]{:S(2)}) %collective-permute-start.13) | collective-permute-done | bytes 262176 | tf_op jit(solution)/shard_map/ppermute | solution.py:115
  55.4 4.0 %shard_map.260.refs_6_ = f32[2,2,2,256,256]{4,3,2,1,0:T(8,128)S(1)} custom-call(s32[32]{0:T(128)S(1)} %copy-done.43, s32[9]{0:T(128)S(1)} %dynamic-slice_bitcast_fusion.refs_1_.refs_0_.table_ref, bf16[256,512]{1,0:T(8,128)(2,1)S(1)} %get-tuple-element.231.refs_2_, bf16[256,512]{1,0:T(8,128)(2,1)S(1)} %copy-done.9, ...), custom_call_target="tpu_custom_call", output_to_operand_aliasing={{}: (8, {})} | custom-call | flops 1024 | bytes 1024 | tf_op jit(solution)/shard_map/pallas_call | solution.py:808
  59.4 4.0 %shard_map.261 = (f32[256,512]{1,0:T(8,128)}, f32[256,512]{1,0:T(8,128)}, bf16[256,512]{1,0:T(8,128)(2,1)S(1)}, bf16[256,512]{1,0:T(8,128)(2,1)S(1)}, f32[2,2,2,8,256]{4,3,2,1,0:T(8,128)S(1)}) custom-call(s32[32]{0:T(128)S(1)} %copy-done.43, s32[9]{0:T(128)S(1)} %dynamic-slice_bitcast_fusion.refs_1_.refs_0_.table_ref, ...), custom_call_target="tpu_custom_call" | custom-call | flops 1024 | bytes 1024 | tf_op jit(solution)/shard_map/pallas_call | solution.py:808
  65.6 3.1 shard_map.262
  71.6 11.6 %collective-permute-done.17 = bf16[256,1024]{1,0:T(8,128)(2,1)S(1)} collective-permute-done((bf16[256,1024]{1,0:T(8,128)(2,1)S(1)}, bf16[256,1024]{1,0:T(8,128)(2,1)S(1)}, u32[]{:S(2)}, u32[]{:S(2)}) %collective-permute-start.17) | collective-permute-done | bytes 524320 | tf_op jit(solution)/shard_map/ppermute | solution.py:401
  91.9 4.3 %shard_map.263 = (bf16[8,352,1024]{2,1,0:T(8,128)(2,1)S(1)}, f32[8,128]{1,0:T(8,128)S(1)}) custom-call(s32[9]{0:T(128)S(1)} %dynamic-slice_bitcast_fusion.refs_1_.refs_0_.table_ref, bf16[256,1024]{1,0:T(8,128)(2,1)S(1)} %multiply_convert_fusion.3.refs_0_, bf16[256,1024]{1,0:T(8,128)(2,1)S(1)} %collective-permute-done.21.refs_1_, ...), custom_call_target="tpu_custom_call" | custom-call | flops 1024 | bytes 1024 | tf_op jit(solution)/shard_map/pallas_call | solution.py:162
  96.2 3.6 %shard_map.264 = (bf16[8,352,1024]{2,1,0:T(8,128)(2,1)S(1)}, f32[8,128]{1,0:T(8,128)S(1)}) custom-call(s32[9]{0:T(128)S(1)} %dynamic-slice_bitcast_fusion.refs_1_.refs_0_.table_ref, bf16[256,1536]{1,0:T(8,128)(2,1)S(1)} %get-tuple-element.439.refs_0_.left_ref, ...), custom_call_target="tpu_custom_call", output_to_operand_aliasing={{0}: (5, {})} | custom-call | flops 1024 | bytes 1024 | tf_op jit(solution)/shard_map/pallas_call | solution.py:162
  99.7 4.9 %collective-permute-done.19 = bf16[256,1024]{1,0:T(8,128)(2,1)S(1)} collective-permute-done((bf16[256,1024]{1,0:T(8,128)(2,1)S(1)}, bf16[256,1024]{1,0:T(8,128)(2,1)S(1)}, u32[]{:S(2)}, u32[]{:S(2)}) %collective-permute-start.19) | collective-permute-done | bytes 524320 | tf_op jit(solution)/shard_map/ppermute | solution.py:401
  113.4 2.6 shard_map.267
  116.7 3.9 %shard_map.269 = (bf16[256,512]{1,0:T(8,128)(2,1)S(1)}, bf16[256,512]{1,0:T(8,128)(2,1)S(1)}, f32[8,128]{1,0:T(8,128)S(1)}, f32[2,2,2,128,256]{4,3,2,1,0:T(8,128)S(1)}) custom-call(s32[32]{0:T(128)S(1)} %copy-done.43, s32[9]{0:T(128)S(1)} %dynamic-slice_bitcast_fusion.refs_1_.refs_0_.table_ref, bf16[256,512]{1,0:T(8,128)(2,1)S(1)} %get-tuple-element.231.refs_2_, ...), custom_call_target="tpu_custom_call" | custom-call | flops 50000003072 | bytes 1024 | tf_op jit(solution)/shard_map/pallas_call | solution.py:989
  129.6 6.0 %shard_map.271 = (bf16[512,512]{1,0:T(8,128)(2,1)S(1)}, bf16[512,512]{1,0:T(8,128)(2,1)S(1)}, f32[8,128]{1,0:T(8,128)S(1)}, f32[2,2,2,128,256]{4,3,2,1,0:T(8,128)S(1)}) custom-call(s32[32]{0:T(128)S(1)} %copy-done.43, s32[9]{0:T(128)S(1)} %dynamic-slice_bitcast_fusion.refs_1_.refs_0_.table_ref, ...), custom_call_target="tpu_custom_call", output_to_operand_aliasing={{3}: (12, {})} | custom-call | flops 50000003072 | bytes 1024 | tf_op jit(solution)/shard_map/pallas_call | solution.py:989
  137.9 8.8 %collective-permute-done.27.refs_2_ = bf16[352,1024]{1,0:T(8,128)(2,1)S(1)} collective-permute-done((bf16[352,1024]{1,0:T(8,128)(2,1)S(1)}, bf16[352,1024]{1,0:T(8,128)(2,1)S(1)}, u32[]{:S(2)}, u32[]{:S(2)}) %collective-permute-start.27) | collective-permute-done | bytes 720928 | tf_op jit(solution)/shard_map/ppermute | solution.py:115
  150.1 6.0 %shard_map.275 = (bf16[512,512]{1,0:T(8,128)(2,1)S(1)}, bf16[512,512]{1,0:T(8,128)(2,1)S(1)}, f32[8,128]{1,0:T(8,128)S(1)}, f32[2,2,2,128,256]{4,3,2,1,0:T(8,128)S(1)}) custom-call(s32[32]{0:T(128)S(1)} %copy-done.43, s32[9]{0:T(128)S(1)} %dynamic-slice_bitcast_fusion.refs_1_.refs_0_.table_ref, ...), custom_call_target="tpu_custom_call", output_to_operand_aliasing={{3}: (12, {})} | custom-call | flops 50000003072 | bytes 1024 | tf_op jit(solution)/shard_map/pallas_call | solution.py:989
  160.7 12.7 %collective-permute-done.31.refs_2_ = bf16[352,1024]{1,0:T(8,128)(2,1)S(1)} collective-permute-done((bf16[352,1024]{1,0:T(8,128)(2,1)S(1)}, bf16[352,1024]{1,0:T(8,128)(2,1)S(1)}, u32[]{:S(2)}, u32[]{:S(2)}) %collective-permute-start.31) | collective-permute-done | bytes 720928 | tf_op jit(solution)/shard_map/ppermute | solution.py:115
  176.8 6.0 %shard_map.278 = (bf16[512,512]{1,0:T(8,128)(2,1)S(1)}, bf16[512,512]{1,0:T(8,128)(2,1)S(1)}, f32[8,128]{1,0:T(8,128)S(1)}, f32[2,2,2,128,256]{4,3,2,1,0:T(8,128)S(1)}) custom-call(s32[32]{0:T(128)S(1)} %copy-done.43, s32[9]{0:T(128)S(1)} %dynamic-slice_bitcast_fusion.refs_1_.refs_0_.table_ref, ...), custom_call_target="tpu_custom_call", output_to_operand_aliasing={{3}: (12, {})} | custom-call | flops 50000003072 | bytes 1024 | tf_op jit(solution)/shard_map/pallas_call | solution.py:989
  187.7 12.3 %collective-permute-done.35.refs_1_ = bf16[352,1024]{1,0:T(8,128)(2,1)S(1)} collective-permute-done((bf16[352,1024]{1,0:T(8,128)(2,1)S(1)}, bf16[352,1024]{1,0:T(8,128)(2,1)S(1)}, u32[]{:S(2)}, u32[]{:S(2)}) %collective-permute-start.35) | collective-permute-done | bytes 720928 | tf_op jit(solution)/shard_map/ppermute | solution.py:115
  203.4 5.4 %shard_map.281 = (bf16[256,512]{1,0:T(8,128)(2,1)S(1)}, bf16[256,512]{1,0:T(8,128)(2,1)S(1)}, f32[8,128]{1,0:T(8,128)}, f32[256,512]{1,0:T(8,128)S(1)}, f32[256,512]{1,0:T(8,128)S(1)}) custom-call(s32[32]{0:T(128)S(1)} %copy-done.43, s32[9]{0:T(128)S(1)} %dynamic-slice_bitcast_fusion.refs_1_.refs_0_.table_ref, ...), custom_call_target="tpu_custom_call" | custom-call | flops 50000003072 | bytes 1024 | tf_op jit(solution)/shard_map/pallas_call | solution.py:989
  217.9 8.1 %collective-permute-done.44.refs_2_ = bf16[352,1024]{1,0:T(8,128)(2,1)S(1)} collective-permute-done((bf16[352,1024]{1,0:T(8,128)(2,1)S(1)}, bf16[352,1024]{1,0:T(8,128)(2,1)S(1)}, u32[]{:S(2)}, u32[]{:S(2)}) %collective-permute-start.44) | collective-permute-done | bytes 720928 | tf_op jit(solution)/shard_map/ppermute | solution.py:118
  228.7 5.1 %shard_map.288 = (bf16[256,1024]{1,0:T(8,128)(2,1)S(1)}, bf16[256,1024]{1,0:T(8,128)(2,1)}) custom-call(s32[9]{0:T(128)S(1)} %dynamic-slice_bitcast_fusion.refs_1_.refs_0_.table_ref, bf16[512,512]{1,0:T(8,128)(2,1)S(1)} %get-tuple-element.320.refs_2_.queries, bf16[512,512]{1,0:T(8,128)(2,1)S(1)} %get-tuple-element.327.refs_2_.others, ...), custom_call_target="tpu_custom_call" | custom-call | flops 50000003072 | bytes 1024 | tf_op jit(solution)/shard_map/pallas_call | solution.py:664
  247.3 3.0 shard_map.289
  250.3 11.9 %collective-permute-done.45.refs_2_ = bf16[128,1024]{1,0:T(8,128)(2,1)S(1)} collective-permute-done((bf16[128,1024]{1,0:T(8,128)(2,1)S(1)}, bf16[128,1024]{1,0:T(8,128)(2,1)S(1)}, u32[]{:S(2)}, u32[]{:S(2)}) %collective-permute-start.45) | collective-permute-done | bytes 262176 | tf_op jit(solution)/shard_map/ppermute | solution.py:115
  276.8 10.1 %collective-permute-done.55.refs_0_.refs_5_ = bf16[352,1024]{1,0:T(8,128)(2,1)S(1)} collective-permute-done((bf16[352,1024]{1,0:T(8,128)(2,1)S(1)}, bf16[352,1024]{1,0:T(8,128)(2,1)S(1)}, u32[]{:S(2)}, u32[]{:S(2)}) %collective-permute-start.55) | collective-permute-done | bytes 720928 | tf_op jit(solution)/shard_map/ppermute | solution.py:115
  296.4 4.6 %collective-permute-done.62 = bf16[176,1024]{1,0:T(8,128)(2,1)S(1)} collective-permute-done((bf16[176,1024]{1,0:T(8,128)(2,1)S(1)}, bf16[176,1024]{1,0:T(8,128)(2,1)S(1)}, u32[]{:S(2)}, u32[]{:S(2)}) %collective-permute-start.62) | collective-permute-done | bytes 360480 | tf_op jit(solution)/shard_map/ppermute | solution.py:118
  310.6 5.5 %collective-permute-done.69.refs_2_ = bf16[128,1024]{1,0:T(8,128)(2,1)S(1)} collective-permute-done((bf16[128,1024]{1,0:T(8,128)(2,1)S(1)}, bf16[128,1024]{1,0:T(8,128)(2,1)S(1)}, u32[]{:S(2)}, u32[]{:S(2)}) %collective-permute-start.69) | collective-permute-done | bytes 262176 | tf_op jit(solution)/shard_map/ppermute | solution.py:121
  323.7 5.6 %shard_map.299 = (f32[1024,1536]{1,0:T(8,128)}, f32[1024,1536]{1,0:T(8,128)}, f32[3,512,1024]{2,1,0:T(8,128)}, f32[1024,1024]{1,0:T(8,128)}, f32[8,128]{1,0:T(8,128)S(1)}) custom-call(s32[9]{0:T(128)S(1)} %dynamic-slice_bitcast_fusion.refs_1_.refs_0_.table_ref, ...), custom_call_target="tpu_custom_call", output_to_operand_aliasing={{0}: (2, {}), {1}: (3, {}), {2}: (4, {}), {3}: (5, {})} | custom-call | flops 1024 | bytes 1024 | tf_op jit(solution)/shard_map/pallas_call | solution.py:315
  (396 shorter events, 158.1 us)
Async XLA Ops:
  11.9 14.3 %collective-permute-start.7 = (bf16[256,512]{1,0:T(8,128)(2,1)S(1)}, bf16[256,512]{1,0:T(8,128)(2,1)S(1)}, u32[]{:S(2)}, u32[]{:S(2)}) collective-permute-start(bf16[256,512]{1,0:T(8,128)(2,1)S(1)} %get-tuple-element.235.refs_5_.refs_9_), channel_id=1, source_target_pairs={{2,0},{3,1},{6,2},{7,3},{10,6},{11,7},{14,10},{15,11},{12,14},{13,... | collective-permute-start | bytes 786440 | tf_op jit(solution)/shard_map/ppermute | solution.py:118
  45.4 14.0 %collective-permute-start.12 = (bf16[256,512]{1,0:T(8,128)(2,1)}, bf16[256,512]{1,0:T(8,128)(2,1)}, u32[]{:S(2)}, u32[]{:S(2)}) collective-permute-start(bf16[256,512]{1,0:T(8,128)(2,1)} %collective-permute-done.8.refs_4_.refs_8_), channel_id=1, source_target_pairs={{0,2},{1,3},{2,6},{3,7},{6,10},{7,11},{10,14},{11,15},{14,12},{15,... | collective-permute-start | bytes 786440 | tf_op jit(solution)/shard_map/ppermute | solution.py:115
  68.7 14.4 %collective-permute-start.17 = (bf16[256,1024]{1,0:T(8,128)(2,1)S(1)}, bf16[256,1024]{1,0:T(8,128)(2,1)S(1)}, u32[]{:S(2)}, u32[]{:S(2)}) collective-permute-start(bf16[256,1024]{1,0:T(8,128)(2,1)S(1)} %shard_map.262), channel_id=1, source_target_pairs={{0,16},{16,0},{1,17},{17,1},{2,18},{18,2},{3,19},{19,3},{4,20},{20... | collective-permute-start | bytes 1572872 | tf_op jit(solution)/shard_map/ppermute | solution.py:401
  90.3 14.3 %collective-permute-start.19 = (bf16[256,1024]{1,0:T(8,128)(2,1)S(1)}, bf16[256,1024]{1,0:T(8,128)(2,1)S(1)}, u32[]{:S(2)}, u32[]{:S(2)}) collective-permute-start(bf16[256,1024]{1,0:T(8,128)(2,1)S(1)} %fusion.4.refs_4_), channel_id=1, source_target_pairs={{0,16},{16,0},{1,17},{17,1},{2,18},{18,2},{3,19},{19,3},{4,20},{20... | collective-permute-start | bytes 1572872 | tf_op jit(solution)/shard_map/ppermute | solution.py:401
  120.6 15.1 %collective-permute-start.29 = (bf16[256,512]{1,0:T(8,128)(2,1)S(1)}, bf16[256,512]{1,0:T(8,128)(2,1)S(1)}, u32[]{:S(2)}, u32[]{:S(2)}) collective-permute-start(bf16[256,512]{1,0:T(8,128)(2,1)S(1)} %get-tuple-element.286), channel_id=1, source_target_pairs={{0,2},{1,3},{2,6},{3,7},{6,10},{7,11},{10,14},{11,15},{14,12},{15,... | collective-permute-start | bytes 786440 | tf_op jit(solution)/shard_map/ppermute | solution.py:115
  121.1 14.6 %collective-permute-start.30 = (bf16[256,512]{1,0:T(8,128)(2,1)S(1)}, bf16[256,512]{1,0:T(8,128)(2,1)S(1)}, u32[]{:S(2)}, u32[]{:S(2)}) collective-permute-start(bf16[256,512]{1,0:T(8,128)(2,1)S(1)} %get-tuple-element.287), channel_id=1, source_target_pairs={{2,0},{3,1},{6,2},{7,3},{10,6},{11,7},{14,10},{15,11},{12,14},{13,... | collective-permute-start | bytes 786440 | tf_op jit(solution)/shard_map/ppermute | solution.py:118
  126.0 22.0 %collective-permute-start.26 = (bf16[256,1024]{1,0:T(8,128)(2,1)S(1)}, bf16[256,1024]{1,0:T(8,128)(2,1)S(1)}, u32[]{:S(2)}, u32[]{:S(2)}) collective-permute-start(bf16[256,1024]{1,0:T(8,128)(2,1)S(1)} %shard_map.272), channel_id=1, source_target_pairs={{0,16},{16,0},{1,17},{17,1},{2,18},{18,2},{3,19},{19,3},{4,20},{20... | collective-permute-start | bytes 1572872 | tf_op jit(solution)/shard_map/ppermute | solution.py:401
  127.6 19.1 %collective-permute-start.27 = (bf16[352,1024]{1,0:T(8,128)(2,1)S(1)}, bf16[352,1024]{1,0:T(8,128)(2,1)S(1)}, u32[]{:S(2)}, u32[]{:S(2)}) collective-permute-start(bf16[352,1024]{1,0:T(8,128)(2,1)S(1)} %get-tuple-element.282), channel_id=1, source_target_pairs={{0,2},{1,3},{2,6},{3,7},{6,10},{7,11},{10,14},{11,15},{14,12},{15,... | collective-permute-start | bytes 2162696 | tf_op jit(solution)/shard_map/ppermute | solution.py:115
  128.0 19.1 %collective-permute-start.28 = (bf16[352,1024]{1,0:T(8,128)(2,1)S(1)}, bf16[352,1024]{1,0:T(8,128)(2,1)S(1)}, u32[]{:S(2)}, u32[]{:S(2)}) collective-permute-start(bf16[352,1024]{1,0:T(8,128)(2,1)S(1)} %get-tuple-element.283), channel_id=1, source_target_pairs={{2,0},{3,1},{6,2},{7,3},{10,6},{11,7},{14,10},{15,11},{12,14},{13,... | collective-permute-start | bytes 2162696 | tf_op jit(solution)/shard_map/ppermute | solution.py:118
  135.8 22.1 %collective-permute-start.33 = (bf16[512,512]{1,0:T(8,128)(2,1)S(1)}, bf16[512,512]{1,0:T(8,128)(2,1)S(1)}, u32[]{:S(2)}, u32[]{:S(2)}) collective-permute-start(bf16[512,512]{1,0:T(8,128)(2,1)S(1)} %get-tuple-element.297), channel_id=1, source_target_pairs={{0,2},{1,3},{2,6},{3,7},{6,10},{7,11},{10,14},{11,15},{14,12},{15,... | collective-permute-start | bytes 1572872 | tf_op jit(solution)/shard_map/ppermute | solution.py:115
  136.3 22.0 %collective-permute-start.34 = (bf16[512,512]{1,0:T(8,128)(2,1)S(1)}, bf16[512,512]{1,0:T(8,128)(2,1)S(1)}, u32[]{:S(2)}, u32[]{:S(2)}) collective-permute-start(bf16[512,512]{1,0:T(8,128)(2,1)S(1)} %get-tuple-element.298), channel_id=1, source_target_pairs={{2,0},{3,1},{6,2},{7,3},{10,6},{11,7},{14,10},{15,11},{12,14},{13,... | collective-permute-start | bytes 1572872 | tf_op jit(solution)/shard_map/ppermute | solution.py:118
  148.0 25.4 %collective-permute-start.31 = (bf16[352,1024]{1,0:T(8,128)(2,1)S(1)}, bf16[352,1024]{1,0:T(8,128)(2,1)S(1)}, u32[]{:S(2)}, u32[]{:S(2)}) collective-permute-start(bf16[352,1024]{1,0:T(8,128)(2,1)S(1)} %get-tuple-element.293), channel_id=1, source_target_pairs={{0,2},{1,3},{2,6},{3,7},{6,10},{7,11},{10,14},{11,15},{14,12},{15,... | collective-permute-start | bytes 2162696 | tf_op jit(solution)/shard_map/ppermute | solution.py:115
  149.0 24.8 %collective-permute-start.32 = (bf16[352,1024]{1,0:T(8,128)(2,1)S(1)}, bf16[352,1024]{1,0:T(8,128)(2,1)S(1)}, u32[]{:S(2)}, u32[]{:S(2)}) collective-permute-start(bf16[352,1024]{1,0:T(8,128)(2,1)S(1)} %get-tuple-element.294), channel_id=1, source_target_pairs={{2,0},{3,1},{6,2},{7,3},{10,6},{11,7},{14,10},{15,11},{12,14},{13,... | collective-permute-start | bytes 2162696 | tf_op jit(solution)/shard_map/ppermute | solution.py:118
  158.6 26.0 %collective-permute-start.37 = (bf16[512,512]{1,0:T(8,128)(2,1)S(1)}, bf16[512,512]{1,0:T(8,128)(2,1)S(1)}, u32[]{:S(2)}, u32[]{:S(2)}) collective-permute-start(bf16[512,512]{1,0:T(8,128)(2,1)S(1)} %get-tuple-element.307), channel_id=1, source_target_pairs={{0,2},{1,3},{2,6},{3,7},{6,10},{7,11},{10,14},{11,15},{14,12},{15,... | collective-permute-start | bytes 1572872 | tf_op jit(solution)/shard_map/ppermute | solution.py:115
  159.5 25.5 %collective-permute-start.38 = (bf16[512,512]{1,0:T(8,128)(2,1)S(1)}, bf16[512,512]{1,0:T(8,128)(2,1)S(1)}, u32[]{:S(2)}, u32[]{:S(2)}) collective-permute-start(bf16[512,512]{1,0:T(8,128)(2,1)S(1)} %get-tuple-element.308), channel_id=1, source_target_pairs={{2,0},{3,1},{6,2},{7,3},{10,6},{11,7},{14,10},{15,11},{12,14},{13,... | collective-permute-start | bytes 1572872 | tf_op jit(solution)/shard_map/ppermute | solution.py:118
  174.7 25.4 %collective-permute-start.35 = (bf16[352,1024]{1,0:T(8,128)(2,1)S(1)}, bf16[352,1024]{1,0:T(8,128)(2,1)S(1)}, u32[]{:S(2)}, u32[]{:S(2)}) collective-permute-start(bf16[352,1024]{1,0:T(8,128)(2,1)S(1)} %get-tuple-element.303), channel_id=1, source_target_pairs={{0,2},{1,3},{2,6},{3,7},{6,10},{7,11},{10,14},{11,15},{14,12},{15,... | collective-permute-start | bytes 2162696 | tf_op jit(solution)/shard_map/ppermute | solution.py:115
  175.7 24.8 %collective-permute-start.36 = (bf16[352,1024]{1,0:T(8,128)(2,1)S(1)}, bf16[352,1024]{1,0:T(8,128)(2,1)S(1)}, u32[]{:S(2)}, u32[]{:S(2)}) collective-permute-start(bf16[352,1024]{1,0:T(8,128)(2,1)S(1)} %get-tuple-element.304), channel_id=1, source_target_pairs={{2,0},{3,1},{6,2},{7,3},{10,6},{11,7},{14,10},{15,11},{12,14},{13,... | collective-permute-start | bytes 2162696 | tf_op jit(solution)/shard_map/ppermute | solution.py:118
  185.3 26.8 %collective-permute-start.39 = (bf16[512,512]{1,0:T(8,128)(2,1)S(1)}, bf16[512,512]{1,0:T(8,128)(2,1)S(1)}, u32[]{:S(2)}, u32[]{:S(2)}) collective-permute-start(bf16[512,512]{1,0:T(8,128)(2,1)S(1)} %get-tuple-element.314), channel_id=1, source_target_pairs={{0,2},{1,3},{2,6},{3,7},{6,10},{7,11},{10,14},{11,15},{14,12},{15,... | collective-permute-start | bytes 1572872 | tf_op jit(solution)/shard_map/ppermute | solution.py:115
  186.2 25.9 %collective-permute-start.40 = (bf16[512,512]{1,0:T(8,128)(2,1)S(1)}, bf16[512,512]{1,0:T(8,128)(2,1)S(1)}, u32[]{:S(2)}, u32[]{:S(2)}) collective-permute-start(bf16[512,512]{1,0:T(8,128)(2,1)S(1)} %get-tuple-element.315), channel_id=1, source_target_pairs={{2,0},{3,1},{6,2},{7,3},{10,6},{11,7},{14,10},{15,11},{12,14},{13,... | collective-permute-start | bytes 1572872 | tf_op jit(solution)/shard_map/ppermute | solution.py:118
  201.3 24.7 %collective-permute-start.44 = (bf16[352,1024]{1,0:T(8,128)(2,1)S(1)}, bf16[352,1024]{1,0:T(8,128)(2,1)S(1)}, u32[]{:S(2)}, u32[]{:S(2)}) collective-permute-start(bf16[352,1024]{1,0:T(8,128)(2,1)S(1)} %get-tuple-element.332.refs_0_), channel_id=1, source_target_pairs={{2,0},{3,1},{6,2},{7,3},{10,6},{11,7},{14,10},{15,11},{12,14},{13,... | collective-permute-start | bytes 2162696 | tf_op jit(solution)/shard_map/ppermute | solution.py:118
  202.9 23.0 %collective-permute-start.43 = (bf16[352,1024]{1,0:T(8,128)(2,1)S(1)}, bf16[352,1024]{1,0:T(8,128)(2,1)S(1)}, u32[]{:S(2)}, u32[]{:S(2)}) collective-permute-start(bf16[352,1024]{1,0:T(8,128)(2,1)S(1)} %get-tuple-element.332.refs_0_), channel_id=1, source_target_pairs={{0,2},{1,3},{2,6},{3,7},{6,10},{7,11},{10,14},{11,15},{14,12},{15,... | collective-permute-start | bytes 2162696 | tf_op jit(solution)/shard_map/ppermute | solution.py:115
  238.5 26.5 %collective-permute-start.49 = (bf16[352,1024]{1,0:T(8,128)(2,1)}, bf16[352,1024]{1,0:T(8,128)(2,1)S(1)}, u32[]{:S(2)}, u32[]{:S(2)}) collective-permute-start(bf16[352,1024]{1,0:T(8,128)(2,1)} %copy-done.19), channel_id=1, source_target_pairs={{0,2},{1,3},{2,6},{3,7},{6,10},{7,11},{10,14},{11,15},{14,12},{15,... | collective-permute-start | bytes 2162696 | tf_op jit(solution)/shard_map/ppermute | solution.py:115
  238.9 26.0 %collective-permute-start.50 = (bf16[352,1024]{1,0:T(8,128)(2,1)S(1)}, bf16[352,1024]{1,0:T(8,128)(2,1)S(1)}, u32[]{:S(2)}, u32[]{:S(2)}) collective-permute-start(bf16[352,1024]{1,0:T(8,128)(2,1)S(1)} %copy-done.18), channel_id=1, source_target_pairs={{2,0},{3,1},{6,2},{7,3},{10,6},{11,7},{14,10},{15,11},{12,14},{13,... | collective-permute-start | bytes 2162696 | tf_op jit(solution)/shard_map/ppermute | solution.py:118
  241.9 23.0 %collective-permute-start.52 = (bf16[256,1024]{1,0:T(8,128)(2,1)S(1)}, bf16[256,1024]{1,0:T(8,128)(2,1)S(1)}, u32[]{:S(2)}, u32[]{:S(2)}) collective-permute-start(bf16[256,1024]{1,0:T(8,128)(2,1)S(1)} %add_convert_fusion), channel_id=1, source_target_pairs={{0,16},{16,0},{1,17},{17,1},{2,18},{18,2},{3,19},{19,3},{4,20},{20... | collective-permute-start | bytes 1572872 | tf_op jit(solution)/shard_map/ppermute | solution.py:401
  245.2 17.0 %collective-permute-start.45 = (bf16[128,1024]{1,0:T(8,128)(2,1)S(1)}, bf16[128,1024]{1,0:T(8,128)(2,1)S(1)}, u32[]{:S(2)}, u32[]{:S(2)}) collective-permute-start(bf16[128,1024]{1,0:T(8,128)(2,1)S(1)} %copy-done.49), channel_id=1, source_target_pairs={{0,2},{1,3},{2,6},{3,7},{6,10},{7,11},{10,14},{11,15},{14,12},{15,... | collective-permute-start | bytes 786440 | tf_op jit(solution)/shard_map/ppermute | solution.py:115
  246.0 16.1 %collective-permute-start.46 = (bf16[128,1024]{1,0:T(8,128)(2,1)S(1)}, bf16[128,1024]{1,0:T(8,128)(2,1)S(1)}, u32[]{:S(2)}, u32[]{:S(2)}) collective-permute-start(bf16[128,1024]{1,0:T(8,128)(2,1)S(1)} %copy-done.47), channel_id=1, source_target_pairs={{2,0},{3,1},{6,2},{7,3},{10,6},{11,7},{14,10},{15,11},{12,14},{13,... | collective-permute-start | bytes 786440 | tf_op jit(solution)/shard_map/ppermute | solution.py:118
  265.5 21.3 %collective-permute-start.55 = (bf16[352,1024]{1,0:T(8,128)(2,1)S(1)}, bf16[352,1024]{1,0:T(8,128)(2,1)S(1)}, u32[]{:S(2)}, u32[]{:S(2)}) collective-permute-start(bf16[352,1024]{1,0:T(8,128)(2,1)S(1)} %collective-permute-done.49.refs_0_.refs_3_), channel_id=1, source_target_pairs={{0,2},{1,3},{2,6},{3,7},{6,10},{7,11},{10,14},{11,15},{14,12},{15,... | collective-permute-start | bytes 2162696 | tf_op jit(solution)/shard_map/ppermute | solution.py:115
  267.1 20.3 %collective-permute-start.56 = (bf16[352,1024]{1,0:T(8,128)(2,1)S(1)}, bf16[352,1024]{1,0:T(8,128)(2,1)S(1)}, u32[]{:S(2)}, u32[]{:S(2)}) collective-permute-start(bf16[352,1024]{1,0:T(8,128)(2,1)S(1)} %collective-permute-done.50.refs_1_.refs_4_), channel_id=1, source_target_pairs={{2,0},{3,1},{6,2},{7,3},{10,6},{11,7},{14,10},{15,11},{12,14},{13,... | collective-permute-start | bytes 2162696 | tf_op jit(solution)/shard_map/ppermute | solution.py:118
  272.7 20.8 %collective-permute-start.53 = (bf16[128,1024]{1,0:T(8,128)(2,1)S(1)}, bf16[128,1024]{1,0:T(8,128)(2,1)S(1)}, u32[]{:S(2)}, u32[]{:S(2)}) collective-permute-start(bf16[128,1024]{1,0:T(8,128)(2,1)S(1)} %get-tuple-element.354), channel_id=1, source_target_pairs={{0,2},{1,3},{2,6},{3,7},{6,10},{7,11},{10,14},{11,15},{14,12},{15,... | collective-permute-start | bytes 786440 | tf_op jit(solution)/shard_map/ppermute | solution.py:115
  274.3 19.2 %collective-permute-start.54 = (bf16[128,1024]{1,0:T(8,128)(2,1)S(1)}, bf16[128,1024]{1,0:T(8,128)(2,1)S(1)}, u32[]{:S(2)}, u32[]{:S(2)}) collective-permute-start(bf16[128,1024]{1,0:T(8,128)(2,1)S(1)} %get-tuple-element.355), channel_id=1, source_target_pairs={{2,0},{3,1},{6,2},{7,3},{10,6},{11,7},{14,10},{15,11},{12,14},{13,... | collective-permute-start | bytes 786440 | tf_op jit(solution)/shard_map/ppermute | solution.py:118
  294.2 13.8 %collective-permute-start.60 = (bf16[128,1024]{1,0:T(8,128)(2,1)S(1)}, bf16[128,1024]{1,0:T(8,128)(2,1)S(1)}, u32[]{:S(2)}, u32[]{:S(2)}) collective-permute-start(bf16[128,1024]{1,0:T(8,128)(2,1)S(1)} %get-tuple-element.368.refs_0_), channel_id=1, source_target_pairs={{2,0},{3,1},{6,2},{7,3},{10,6},{11,7},{14,10},{15,11},{12,14},{13,... | collective-permute-start | bytes 786440 | tf_op jit(solution)/shard_map/ppermute | solution.py:118
  306.3 17.4 %collective-permute-start.75 = (bf16[8,352,1024]{2,1,0:T(8,128)(2,1)S(1)}, bf16[8,352,1024]{2,1,0:T(8,128)(2,1)S(1)}, u32[]{:S(2)}, u32[]{:S(2)}) collective-permute-start(bf16[8,352,1024]{2,1,0:T(8,128)(2,1)S(1)} %get-tuple-element.400), channel_id=1, source_target_pairs={{0,1},{1,0},{2,3},{3,2},{4,5},{5,4},{6,7},{7,6},{8,9},{9,8},{10,11... | collective-permute-start | bytes 17301512 | tf_op jit(solution)/shard_map/ppermute | solution.py:121
  (131 other events, 1183.4 us)
